TPU v7x, 32 devices: a whole 2x2x4 slice. The times are simulated.
32 devices in a mesh: dp: 8 (over z, x), mp: 4 (over y, core).
Axes of the slice: x: 2, y: 2, z: 4, core: 2. Of those that a mesh axis runs over, the one named last changes fastest.
Arguments:
- text_tokens: bfloat16 [32, 64, 768], P('dp'), may hold values from -6 to 6
- image_tokens: bfloat16 [32, 576, 768], P('dp'), may hold values from -6 to 6
- text_lengths: int32 [32], P('dp'), may hold values from 8 to 64, as said below
- patch_counts: int32 [32], P('dp'), may hold values from 196 to 576, as said below
- self_qkv: bfloat16 [3, 768, 768], P(None, 'dp', 'mp'), may hold values from -0.21875 to 0.21875
- self_out: bfloat16 [768, 768], P('mp', 'dp'), may hold values from -0.625 to 0.625
- cross_query: bfloat16 [768, 768], P('dp', 'mp'), may hold values from -0.21875 to 0.21875
- cross_keyval: bfloat16 [2, 768, 768], P(None, 'dp', 'mp'), may hold values from -0.21875 to 0.21875
- cross_out: bfloat16 [768, 768], P('mp', 'dp'), may hold values from -0.875 to 0.875
- mlp_up: bfloat16 [768, 3072], P('dp', 'mp'), may hold values from -0.21875 to 0.21875
- mlp_down: bfloat16 [3072, 768], P('mp', 'dp'), may hold values from -0.15625 to 0.15625
- norm_gain: float32 [3, 768], replicated, may hold values from 0.25 to 1.75
- norm_bias: float32 [3, 768], replicated, may hold values from -4 to 4
- out_bias: float32 [3, 768], replicated, may hold values from -4 to 4
- up_bias: float32 [3072], P('mp'), may hold values from -4 to 4
- out_grad: bfloat16 [32, 64, 768], P('dp'), may hold values from -6 to 6
Outputs:
- layer_out: bfloat16 [32, 64, 768], P('dp')
- text_grad: float32 [32, 64, 768], P('dp')
- image_grad: float32 [32, 576, 768], P('dp', None, 'mp')
- self_qkv_grad: float32 [3, 768, 768], P(None, 'dp', 'mp')
- self_out_grad: float32 [768, 768], P('mp', 'dp')
- cross_query_grad: float32 [768, 768], P('dp', 'mp')
- cross_keyval_grad: float32 [2, 768, 768], P(None, 'dp', 'mp')
- cross_out_grad: float32 [768, 768], P('mp', 'dp')
- mlp_up_grad: float32 [768, 3072], P('dp', 'mp')
- mlp_down_grad: float32 [3072, 768], P('mp', 'dp')
- norm_gain_grad: float32 [3, 768], replicated
- norm_bias_grad: float32 [3, 768], replicated
- out_bias_grad: float32 [3, 768], replicated
- up_bias_grad: float32 [3072], P('mp')
Inputs may be any that keep to these rules, and one draw needn't show every extreme that they name: Caption b holds text_lengths[b] real tokens at its first positions; keys past them are padding. Image b has patch_counts[b] valid tokens at its first positions, either 196 or 576.
All inputs are finite; a program needn't handle non-finite values.
Results may differ from a plain program's by a relative error of at most 0.018.
Values may be sent and summed in bfloat16 or wider, within the bound.
No kernel may reach another device: no remote copies, remote signals or barrier semaphores. Data moves between devices by JAX's collectives and lax.ppermute only.
A program may use at most 128 MiB of HBM per device.

v0:
```python
import math

import jax
import jax.numpy as jnp
from jax import lax
from jax.sharding import PartitionSpec as P

HEAD_DIM = 64


NORM_EPS = 1e-05
NEG_FILL = -1e30
INV_ROOT_TWO = 1.0 / math.sqrt(2.0)
INV_ROOT_TAU = 1.0 / math.sqrt(2.0 * math.pi)


def norm_forward(values, gain_row, shift_row):
    center = jnp.mean(values, axis=-1, keepdims=True)
    centered = values - center
    variance = jnp.mean(centered * centered, axis=-1, keepdims=True)
    inv_std = lax.rsqrt(variance + NORM_EPS)
    normed = centered * inv_std
    return ((normed * gain_row + shift_row).astype(jnp.bfloat16), normed, inv_std)


def norm_backward(grad_out, normed, inv_std, gain_row):
    scaled = grad_out * gain_row
    first_mean = jnp.mean(scaled, axis=-1, keepdims=True)
    second_mean = jnp.mean(scaled * normed, axis=-1, keepdims=True)
    grad_in = inv_std * (scaled - first_mean - normed * second_mean)
    return (grad_in, jnp.sum(grad_out * normed, axis=0), jnp.sum(grad_out, axis=0))


def split_heads(flat, seq_count, positions):
    return flat.reshape(seq_count, positions, -1, HEAD_DIM)


def masked_scores(queries, key_heads, allowed, score_scale):
    scores = (
        jnp.einsum("bqhe,bkhe->bhqk", queries, key_heads, preferred_element_type=jnp.float32)
        * score_scale
    )
    return jnp.where(allowed[:, None], scores, NEG_FILL)


def attend(queries, key_heads, value_heads, allowed, score_scale):
    scores = masked_scores(queries, key_heads, allowed, score_scale)
    row_peak = jnp.max(scores, axis=-1, keepdims=True)
    raised = jnp.exp(scores - row_peak)
    row_total = jnp.sum(raised, axis=-1, keepdims=True)
    probability = (raised / row_total).astype(jnp.bfloat16)
    context = jnp.einsum(
        "bhqk,bkhe->bqhe", probability, value_heads, preferred_element_type=jnp.float32
    )
    return (context.astype(jnp.bfloat16), row_peak + jnp.log(row_total))


def attend_back(queries, key_heads, value_heads, allowed, log_total, grad_ctx, score_scale):
    scores = masked_scores(queries, key_heads, allowed, score_scale)
    probability = jnp.exp(scores - log_total)
    grad_prob = jnp.einsum(
        "bqhe,bkhe->bhqk", grad_ctx, value_heads, preferred_element_type=jnp.float32
    )
    grad_values = jnp.einsum(
        "bhqk,bqhe->bkhe",
        probability.astype(jnp.bfloat16),
        grad_ctx,
        preferred_element_type=jnp.float32,
    )
    inner_sum = jnp.sum(probability * grad_prob, axis=-1, keepdims=True)
    grad_scores = (probability * (grad_prob - inner_sum)).astype(jnp.bfloat16)
    grad_queries = (
        jnp.einsum("bhqk,bkhe->bqhe", grad_scores, key_heads, preferred_element_type=jnp.float32)
        * score_scale
    )
    grad_keys = (
        jnp.einsum("bhqk,bqhe->bkhe", grad_scores, queries, preferred_element_type=jnp.float32)
        * score_scale
    )
    return (
        grad_queries.astype(jnp.bfloat16),
        grad_keys.astype(jnp.bfloat16),
        grad_values.astype(jnp.bfloat16),
    )


def gelu_parts(hidden):
    normal_cdf = 0.5 * (1.0 + lax.erf(hidden * INV_ROOT_TWO))
    density = jnp.exp(-0.5 * hidden * hidden) * INV_ROOT_TAU
    return (hidden * normal_cdf, normal_cdf + hidden * density)


def head_total(partial_sum):
    return lax.psum(partial_sum, "mp")


def input_total(partial_sum):
    return lax.psum(partial_sum, "mp")


def per_device(
    text_tokens,
    image_tokens,
    text_lengths,
    patch_counts,
    self_qkv,
    self_out,
    cross_query,
    cross_keyval,
    cross_out,
    mlp_up,
    mlp_down,
    norm_gain,
    norm_bias,
    out_bias,
    up_bias,
    out_grad,
):
    seq_count, positions, feature_width = text_tokens.shape
    patches = image_tokens.shape[1]
    row_count = seq_count * positions
    score_scale = HEAD_DIM ** (-0.5)
    gathered = (
        lax.all_gather(self_qkv, "dp", axis=1, tiled=True),
        lax.all_gather(self_out, "dp", axis=1, tiled=True),
        lax.all_gather(cross_query, "dp", axis=0, tiled=True),
        lax.all_gather(cross_keyval, "dp", axis=1, tiled=True),
        lax.all_gather(cross_out, "dp", axis=1, tiled=True),
        lax.all_gather(mlp_up, "dp", axis=0, tiled=True),
        lax.all_gather(mlp_down, "dp", axis=1, tiled=True),
    )
    w_qkv, w_self_out, w_cross_q, w_cross_kv, w_cross_out, w_up, w_down = gathered
    position = jnp.arange(positions)
    key_live = position[None, :] < text_lengths[:, None]
    self_allowed = (position[:, None] >= position[None, :])[None] & key_live[:, None, :]
    cross_allowed = (jnp.arange(patches)[None, :] < patch_counts[:, None])[:, None, :]
    stream_in = text_tokens.reshape(row_count, feature_width).astype(jnp.float32)
    normed_text, norm_zero, inv_zero = norm_forward(stream_in, norm_gain[0], norm_bias[0])
    projected = jnp.einsum(
        "td,jdc->jtc", normed_text, w_qkv, preferred_element_type=jnp.float32
    ).astype(jnp.bfloat16)
    self_query = split_heads(projected[0], seq_count, positions)
    self_keys = split_heads(projected[1], seq_count, positions)
    self_values = split_heads(projected[2], seq_count, positions)
    self_ctx, self_lse = attend(self_query, self_keys, self_values, self_allowed, score_scale)
    self_flat = self_ctx.reshape(row_count, -1)
    hidden_one = (
        stream_in
        + head_total(jnp.dot(self_flat, w_self_out, preferred_element_type=jnp.float32))
        + out_bias[0]
    )
    normed_mid, norm_one, inv_one = norm_forward(hidden_one, norm_gain[1], norm_bias[1])
    image_flat = image_tokens.reshape(seq_count * patches, feature_width)
    fwd_q, fwd_kv, fwd_out = (w_cross_q, w_cross_kv, w_cross_out)
    cross_flat_q = jnp.dot(normed_mid, fwd_q, preferred_element_type=jnp.float32).astype(
        jnp.bfloat16
    )
    cross_heads_q = split_heads(cross_flat_q, seq_count, positions)
    keyval = jnp.einsum(
        "td,jdc->jtc", image_flat, fwd_kv, preferred_element_type=jnp.float32
    ).astype(jnp.bfloat16)
    cross_keys = split_heads(keyval[0], seq_count, patches)
    cross_values = split_heads(keyval[1], seq_count, patches)
    cross_ctx, cross_lse = attend(
        cross_heads_q, cross_keys, cross_values, cross_allowed, score_scale
    )
    cross_flat = cross_ctx.reshape(seq_count * positions, -1)
    cross_term = jnp.dot(cross_flat, fwd_out, preferred_element_type=jnp.float32)
    cross_branch = head_total(cross_term)
    hidden_two = hidden_one + cross_branch + out_bias[1]
    normed_ffn, norm_two, inv_two = norm_forward(hidden_two, norm_gain[2], norm_bias[2])
    pre_act = jnp.dot(normed_ffn, w_up, preferred_element_type=jnp.float32) + up_bias
    activation, gelu_slope = gelu_parts(pre_act)
    activation_low = activation.astype(jnp.bfloat16)
    result = (
        hidden_two
        + head_total(jnp.dot(activation_low, w_down, preferred_element_type=jnp.float32))
        + out_bias[2]
    )
    layer_out = result.astype(jnp.bfloat16).reshape(seq_count, positions, feature_width)
    back_weights = (
        lax.all_gather(self_qkv, "dp", axis=1, tiled=True),
        lax.all_gather(self_out, "dp", axis=1, tiled=True),
        lax.all_gather(cross_query, "dp", axis=0, tiled=True),
        lax.all_gather(cross_keyval, "dp", axis=1, tiled=True),
        lax.all_gather(cross_out, "dp", axis=1, tiled=True),
        lax.all_gather(mlp_up, "dp", axis=0, tiled=True),
        lax.all_gather(mlp_down, "dp", axis=1, tiled=True),
    )
    back_qkv, back_self_out, back_cross_q, back_cross_kv, back_cross_out, back_up, back_down = (
        back_weights
    )
    cot_low = out_grad.reshape(row_count, feature_width)
    cotangent = cot_low.astype(jnp.float32)
    grad_down = jnp.einsum("tf,td->fd", activation_low, cot_low, preferred_element_type=jnp.float32)
    grad_activ = jnp.einsum("td,fd->tf", cot_low, back_down, preferred_element_type=jnp.float32)
    grad_pre = grad_activ * gelu_slope
    grad_pre_low = grad_pre.astype(jnp.bfloat16)
    grad_up = jnp.einsum("td,tf->df", normed_ffn, grad_pre_low, preferred_element_type=jnp.float32)
    grad_ffn_in = input_total(
        jnp.einsum("tf,df->td", grad_pre_low, back_up, preferred_element_type=jnp.float32)
    )
    ln_two, gain_two, shift_two = norm_backward(grad_ffn_in, norm_two, inv_two, norm_gain[2])
    grad_two = cotangent + ln_two
    grad_two_low = grad_two.astype(jnp.bfloat16)
    use_q, use_kv, use_out = (back_cross_q, back_cross_kv, back_cross_out)
    grad_cross_out = jnp.einsum(
        "tc,td->cd", cross_flat, grad_two_low, preferred_element_type=jnp.float32
    )
    cross_ctx_grad = jnp.einsum(
        "td,cd->tc", grad_two_low, use_out, preferred_element_type=jnp.float32
    ).astype(jnp.bfloat16)
    cross_dq, cross_dk, cross_dv = attend_back(
        cross_heads_q,
        cross_keys,
        cross_values,
        cross_allowed,
        cross_lse,
        split_heads(cross_ctx_grad, seq_count, positions),
        score_scale,
    )
    cross_dq_flat = cross_dq.reshape(seq_count * positions, -1)
    grad_keyval = jnp.stack(
        [cross_dk.reshape(seq_count * patches, -1), cross_dv.reshape(seq_count * patches, -1)]
    )
    grad_cross_q = jnp.einsum(
        "td,tc->dc", normed_mid, cross_dq_flat, preferred_element_type=jnp.float32
    )
    grad_cross_kv = jnp.einsum(
        "td,jtc->jdc", image_flat, grad_keyval, preferred_element_type=jnp.float32
    )
    image_part = jnp.einsum(
        "jtc,jdc->td", grad_keyval, use_kv, preferred_element_type=jnp.float32
    ).reshape(seq_count, patches, feature_width)
    mid_part = jnp.einsum("tc,dc->td", cross_dq_flat, use_q, preferred_element_type=jnp.float32)
    image_grad = lax.psum_scatter(
        image_part.astype(jnp.bfloat16), "mp", scatter_dimension=2, tiled=True
    ).astype(jnp.float32)
    grad_mid_in = input_total(mid_part)
    ln_one, gain_one, shift_one = norm_backward(grad_mid_in, norm_one, inv_one, norm_gain[1])
    grad_one = grad_two + ln_one
    grad_one_low = grad_one.astype(jnp.bfloat16)
    grad_self_out = jnp.einsum(
        "tc,td->cd", self_flat, grad_one_low, preferred_element_type=jnp.float32
    )
    self_ctx_grad = jnp.einsum(
        "td,cd->tc", grad_one_low, back_self_out, preferred_element_type=jnp.float32
    ).astype(jnp.bfloat16)
    self_dq, self_dk, self_dv = attend_back(
        self_query,
        self_keys,
        self_values,
        self_allowed,
        self_lse,
        split_heads(self_ctx_grad, seq_count, positions),
        score_scale,
    )
    grad_projected = jnp.stack(
        [
            self_dq.reshape(row_count, -1),
            self_dk.reshape(row_count, -1),
            self_dv.reshape(row_count, -1),
        ]
    )
    grad_self_qkv = jnp.einsum(
        "td,jtc->jdc", normed_text, grad_projected, preferred_element_type=jnp.float32
    )
    grad_text_in = input_total(
        jnp.einsum("jtc,jdc->td", grad_projected, back_qkv, preferred_element_type=jnp.float32)
    )
    ln_zero, gain_zero, shift_zero = norm_backward(grad_text_in, norm_zero, inv_zero, norm_gain[0])
    text_grad = (grad_one + ln_zero).reshape(seq_count, positions, feature_width)
    weight_grads = (
        lax.psum_scatter(grad_self_qkv, "dp", scatter_dimension=1, tiled=True),
        lax.psum_scatter(grad_self_out, "dp", scatter_dimension=1, tiled=True),
        lax.psum_scatter(grad_cross_q, "dp", scatter_dimension=0, tiled=True),
        lax.psum_scatter(grad_cross_kv, "dp", scatter_dimension=1, tiled=True),
        lax.psum_scatter(grad_cross_out, "dp", scatter_dimension=1, tiled=True),
        lax.psum_scatter(grad_up, "dp", scatter_dimension=0, tiled=True),
        lax.psum_scatter(grad_down, "dp", scatter_dimension=1, tiled=True),
    )
    vector_grads = lax.psum(
        (
            jnp.stack([gain_zero, gain_one, gain_two]),
            jnp.stack([shift_zero, shift_one, shift_two]),
            jnp.stack(
                [jnp.sum(grad_one, axis=0), jnp.sum(grad_two, axis=0), jnp.sum(cotangent, axis=0)]
            ),
            jnp.sum(grad_pre, axis=0),
        ),
        "dp",
    )
    return (
        layer_out,
        text_grad,
        image_grad,
        weight_grads[0],
        weight_grads[1],
        weight_grads[2],
        weight_grads[3],
        weight_grads[4],
        weight_grads[5],
        weight_grads[6],
        vector_grads[0],
        vector_grads[1],
        vector_grads[2],
        vector_grads[3],
    )


def solution(mesh):
    placed = (
        P("dp", None, None),
        P("dp", None, None),
        P("dp"),
        P("dp"),
        P(None, "dp", "mp"),
        P("mp", "dp"),
        P("dp", "mp"),
        P(None, "dp", "mp"),
        P("mp", "dp"),
        P("dp", "mp"),
        P("mp", "dp"),
        P(),
        P(),
        P(),
        P("mp"),
        P("dp", None, None),
    )
    return jax.shard_map(
        per_device,
        mesh=mesh,
        in_specs=placed,
        out_specs=(
            P("dp", None, None),
            P("dp", None, None),
            P("dp", None, "mp"),
            P(None, "dp", "mp"),
            P("mp", "dp"),
            P("dp", "mp"),
            P(None, "dp", "mp"),
            P("mp", "dp"),
            P("dp", "mp"),
            P("mp", "dp"),
            P(),
            P(),
            P(),
            P("mp"),
        ),
        check_vma=False,
    )
```

profile of v0, /device:TPU:0, one launch (start us, length us, event | category | flops | bytes accessed | tf_op | source)
XLA Modules:
  0.0 978.9 jit_solution(3556519981488609134)
XLA Ops:
  13.0 40.5 %all_gather.28 = bf16[3,768,192]{2,0,1:T(4,128)(2,1)} all-gather(bf16[3,96,192]{2,0,1:T(4,128)(2,1)S(1)} %copy.98), channel_id=1, replica_groups=mesh['dp'=8,'mp'=4] {'dp'}, dimensions={1}, use_global_device_ids=true | all-gather | bytes 995328 | tf_op jit(solution)/shard_map/all_gather | solution.py:124
  53.5 3.4 copy.99
  79.0 31.5 %all_gather.29 = bf16[192,768]{0,1:T(8,128)(2,1)S(1)} all-gather(bf16[192,96]{0,1:T(8,128)(2,1)} %copy.105), channel_id=1, replica_groups=mesh['dp'=8,'mp'=4] {'dp'}, dimensions={1}, use_global_device_ids=true | all-gather | bytes 331776 | tf_op jit(solution)/shard_map/all_gather | solution.py:125
  113.4 33.3 %all_gather.31 = bf16[768,192]{1,0:T(8,128)(2,1)} all-gather(bf16[96,192]{1,0:T(8,128)(2,1)} %param.22), channel_id=1, replica_groups=mesh['dp'=8,'mp'=4] {'dp'}, dimensions={0}, use_global_device_ids=true | all-gather | bytes 331776 | tf_op jit(solution)/shard_map/all_gather | solution.py:126
  147.7 31.7 %all_gather.30 = bf16[2,768,192]{2,0,1:T(2,128)(2,1)S(1)} all-gather(bf16[2,96,192]{2,0,1:T(2,128)(2,1)S(1)} %copy.106), channel_id=1, replica_groups=mesh['dp'=8,'mp'=4] {'dp'}, dimensions={1}, use_global_device_ids=true | all-gather | bytes 663552 | tf_op jit(solution)/shard_map/all_gather | solution.py:127
  191.7 33.3 %all_gather.32 = bf16[192,768]{0,1:T(8,128)(2,1)} all-gather(bf16[192,96]{0,1:T(8,128)(2,1)} %copy.112), channel_id=1, replica_groups=mesh['dp'=8,'mp'=4] {'dp'}, dimensions={1}, use_global_device_ids=true | all-gather | bytes 331776 | tf_op jit(solution)/shard_map/all_gather | solution.py:128
  241.7 32.8 %all-reduce.10.cloned.1.call-done = f32[256,768]{1,0:T(8,128)} async-done(((f32[256,768]{1,0:T(8,128)}), f32[256,768]{1,0:T(8,128)}) %all-reduce.10.cloned.1.call-update) | async-done | bytes 786448 | tf_op jit(solution)/shard_map/psum | solution.py:94
  277.7 6.1 all-gather.3.cloned.1.call-done
  286.9 39.0 %all-gather.5.cloned.1.call-done = bf16[768,768]{0,1:T(8,128)(2,1)} async-done(((bf16[768,96]{0,1:T(8,128)(2,1)}), bf16[768,768]{0,1:T(8,128)(2,1)}) %all-gather.5.cloned.1.call-update) | async-done | bytes 1179664 | tf_op jit(solution)/shard_map/all_gather | solution.py:130
  331.7 32.5 %all-reduce.12.cloned.1.call-done = f32[256,768]{1,0:T(8,128)} async-done(((f32[256,768]{1,0:T(8,128)}), f32[256,768]{1,0:T(8,128)}) %all-reduce.12.cloned.1.call-update) | async-done | bytes 786448 | tf_op jit(solution)/shard_map/psum | solution.py:98
  387.5 31.0 %all-reduce.14.cloned.1.call-done = f32[256,768]{1,0:T(8,128)} async-done(((f32[256,768]{1,0:T(8,128)}), f32[256,768]{1,0:T(8,128)}) %all-reduce.14.cloned.1.call-update) | async-done | bytes 786448 | tf_op jit(solution)/shard_map/psum | solution.py:98
  470.5 3.5 copy.151
  480.2 4.2 copy.147
  484.5 4.7 reshape.230
  489.2 5.6 bitcast_convert_fusion
  494.8 5.9 copy.137
  522.9 38.8 %all-reduce = (f32[3,768]{1,0:T(4,128)}, f32[3,768]{1,0:T(4,128)}, f32[3,768]{1,0:T(4,128)}, f32[768]{0:T(1024)}) all-reduce(f32[3,768]{1,0:T(4,128)} %pad_maximum_fusion, f32[3,768]{1,0:T(4,128)} %pad_maximum_fusion.1, f32[3,768]{1,0:T(4,128)S(1)} %pad_maximum_fusion.2, ...), channel_id=1, replica_groups=mesh['dp'=8,'mp'=4] {'dp'}, use_global_device_ids=true, to_apply=%region_35.36 | all-reduce | flops 7680 | bytes 61440 | tf_op jit(solution)/shard_map/psum | solution.py:282
  566.7 12.2 %reduce-scatter.27.cloned.1.call-done = f32[96,192]{1,0:T(8,128)} async-done(((f32[768,192]{1,0:T(8,128)}), f32[96,192]{1,0:T(8,128)}) %reduce-scatter.27.cloned.1.call-update) | async-done | bytes 73744
  580.5 65.0 %reduce-scatter.29.cloned.1.call-done = f32[96,384]{1,0:T(8,128)} async-done(((f32[768,384]{1,0:T(8,128)}), f32[96,384]{1,0:T(8,128)}) %reduce-scatter.29.cloned.1.call-update) | async-done | bytes 147472
  648.9 66.5 %reduce-scatter.25.cloned.1.call-done = f32[96,576]{1,0:T(8,128)} async-done(((f32[768,576]{1,0:T(8,128)}), f32[96,576]{1,0:T(8,128)}) %reduce-scatter.25.cloned.1.call-update) | async-done | bytes 221200
  719.0 40.7 %reduce-scatter.17.cloned.1.call-done = bf16[4,576,192]{1,2,0:T(8,128)(2,1)} async-done(((bf16[4,576,768]{1,2,0:T(8,128)(2,1)}), bf16[4,576,192]{1,2,0:T(8,128)(2,1)}) %reduce-scatter.17.cloned.1.call-update) | async-done | bytes 884752 | tf_op jit(solution)/shard_map/reduce_scatter | solution.py:236
  762.3 63.7 %reduce-scatter.19.cloned.1.call-done = f32[96,192]{1,0:T(8,128)} async-done(((f32[768,192]{1,0:T(8,128)}), f32[96,192]{1,0:T(8,128)}) %reduce-scatter.19.cloned.1.call-update) | async-done | bytes 73744 | tf_op jit(solution)/shard_map/reduce_scatter | solution.py:276
  826.0 72.7 %reduce-scatter.21.cloned.1.call-done = f32[96,768]{1,0:T(8,128)} async-done(((f32[768,768]{1,0:T(8,128)}), f32[96,768]{1,0:T(8,128)}) %reduce-scatter.21.cloned.1.call-update) | async-done | bytes 294928 | tf_op jit(solution)/shard_map/reduce_scatter | solution.py:279
  898.6 72.7 %reduce-scatter.23.cloned.1.call-done = f32[768,96]{0,1:T(8,128)} async-done(((f32[768,768]{0,1:T(8,128)}), f32[768,96]{0,1:T(8,128)}) %reduce-scatter.23.cloned.1.call-update) | async-done | bytes 294928 | tf_op jit(solution)/shard_map/reduce_scatter | solution.py:280
  (272 shorter events, 191.3 us)
Async XLA Ops:
  8.0 171.4 %copy-start = (bf16[4,576,768]{2,1,0:T(8,128)(2,1)S(1)}, bf16[4,576,768]{2,1,0:T(8,128)(2,1)}, u32[]{:S(2)}) copy-start(bf16[4,576,768]{2,1,0:T(8,128)(2,1)} %param.17) | copy-start | bytes 10616836
  8.0 218.4 %all-reduce.8.cloned.1.call-start = ((), (), s32[]{:S(2)}) async-start(), calls=%async_computation.8 | async-start | bytes 1572864 | tf_op jit(solution)/shard_map/psum | solution.py:94
  58.4 169.8 %copy-start.36 = (f32[768]{0:T(1024)}, f32[768]{0:T(1024)S(1)}, u32[]{:S(2)}) copy-start(f32[768]{0:T(1024)S(1)} %get-tuple-element.108) | copy-start | bytes 9220
  58.4 225.4 %copy-start.34 = (f32[768]{0:T(1024)}, f32[768]{0:T(1024)S(1)}, u32[]{:S(2)}) copy-start(f32[768]{0:T(1024)S(1)} %get-tuple-element.110) | copy-start | bytes 9220
  113.4 161.1 %all-reduce.10.cloned.1.call-start = ((), (), s32[]{:S(2)}) async-start(), calls=%async_computation.9 | async-start | bytes 1572864 | tf_op jit(solution)/shard_map/psum | solution.py:94
  190.2 38.5 %copy-start.52 = (f32[768]{0:T(1024)S(1)}, f32[768]{0:T(1024)}, u32[]{:S(2)}) copy-start(f32[768]{0:T(1024)} %get-tuple-element.76) | copy-start | bytes 9220
  235.6 38.9 %copy-start.50 = (f32[768]{0:T(1024)S(1)}, f32[768]{0:T(1024)}, u32[]{:S(2)}) copy-start(f32[768]{0:T(1024)} %get-tuple-element.70) | copy-start | bytes 9220
  240.4 43.3 %all-gather.3.cloned.1.call-start = ((), (), s32[]{:S(2)}) async-start(), calls=%async_computation.10 | async-start | bytes 1327104 | tf_op jit(solution)/shard_map/all_gather | solution.py:129
  241.0 84.8 %all-gather.5.cloned.1.call-start = ((), (), s32[]{:S(2)}) async-start(), calls=%async_computation.11 | async-start | bytes 1327104 | tf_op jit(solution)/shard_map/all_gather | solution.py:130
  241.6 122.6 %all-reduce.12.cloned.1.call-start = ((), (), s32[]{:S(2)}) async-start(), calls=%async_computation.12 | async-start | bytes 1572864 | tf_op jit(solution)/shard_map/psum | solution.py:98
  276.0 10.9 %copy-start.40 = (f32[256]{0:T(256)}, f32[256]{0:T(256)S(1)}, u32[]{:S(2)}) copy-start(f32[256]{0:T(256)S(1)} %broadcast_multiply_fusion.7) | copy-start | bytes 3076
  331.0 87.6 %all-reduce.14.cloned.1.call-start = ((), (), s32[]{:S(2)}) async-start(), calls=%async_computation.13 | async-start | bytes 1572864 | tf_op jit(solution)/shard_map/psum | solution.py:98
  364.3 5.5 copy-start.23
  383.7 131.5 %all-reduce.16.cloned.1.call-start = ((), (), s32[]{:S(2)}) async-start(), calls=%async_computation.22 | async-start | bytes 3145728 | tf_op jit(solution)/shard_map/psum | solution.py:94
  426.7 3.9 copy-start.30
  447.1 71.5 %reduce-scatter.31.cloned.1.call-start = ((), (), s32[]{:S(2)}) async-start(), calls=%async_computation.21 | async-start | bytes 884736
  449.6 129.3 %reduce-scatter.27.cloned.1.call-start = ((), (), s32[]{:S(2)}) async-start(), calls=%async_computation.19 | async-start | bytes 884736
  465.1 180.4 %reduce-scatter.29.cloned.1.call-start = ((), (), s32[]{:S(2)}) async-start(), calls=%async_computation.20 | async-start | bytes 1327104
  477.2 238.2 %reduce-scatter.25.cloned.1.call-start = ((), (), s32[]{:S(2)}) async-start(), calls=%async_computation.18 | async-start | bytes 2211840
  489.2 270.5 %reduce-scatter.17.cloned.1.call-start = ((), (), s32[]{:S(2)}) async-start(), calls=%async_computation.14 | async-start | bytes 4915200 | tf_op jit(solution)/shard_map/reduce_scatter | solution.py:236
  500.8 325.2 %reduce-scatter.19.cloned.1.call-start = ((), (), s32[]{:S(2)}) async-start(), calls=%async_computation.15 | async-start | bytes 884736 | tf_op jit(solution)/shard_map/reduce_scatter | solution.py:276
  503.1 395.6 %reduce-scatter.21.cloned.1.call-start = ((), (), s32[]{:S(2)}) async-start(), calls=%async_computation.16 | async-start | bytes 2654208 | tf_op jit(solution)/shard_map/reduce_scatter | solution.py:279
  506.5 464.8 %reduce-scatter.23.cloned.1.call-start = ((), (), s32[]{:S(2)}) async-start(), calls=%async_computation.17 | async-start | bytes 2654208 | tf_op jit(solution)/shard_map/reduce_scatter | solution.py:280
  509.6 5.6 copy-start.33
  (45 other events, 86.8 us)
Sparse Core Ops, SparseCore 0:
  113.5 33.5 all-reduce.7
  240.6 33.8 all-reduce.9
  331.1 33.1 all-reduce.11
  383.8 34.6 all-reduce.13
  447.3 43.0 all-reduce.15
Sparse Core Ops, SparseCore 1:
  243.1 40.6 all-gather.2
  285.9 40.0 all-gather.4
  450.9 62.6 reduce-scatter.30
  517.3 61.5 reduce-scatter.26
  582.3 63.2 reduce-scatter.28
  649.6 65.8 reduce-scatter.24
  718.0 41.7 reduce-scatter.16
  763.4 62.5 reduce-scatter.18
  830.3 68.3 reduce-scatter.20
  903.1 68.1 reduce-scatter.22
where the time goes:
time: 989 us; the launch traced here: 979 us
  waiting for transfers between devices  536 us (54%)
  blocking collectives  209 us (21%)
  local copies, waits for them, and re-layouts  112 us (11%)
  matrix products  67.6 us (7%)
  other arithmetic  36.8 us (4%)
  between operations  16.4 us (2%)
    unnamed x19, waiting for transfers between devices  145 us
    reduce_scatter x1, waiting for transfers between devices, per_device(): lax.psum_scatter(grad_down, 'dp', scatter_dimension=1, tiled=True)  72.7 us
    reduce_scatter x1, waiting for transfers between devices, per_device(): lax.psum_scatter(grad_up, 'dp', scatter_dimension=0, tiled=True)  72.7 us
    reduce_scatter x1, waiting for transfers between devices, per_device(): lax.psum_scatter(grad_cross_q, 'dp', scatter_dimension=0, tiled=True)  63.7 us
    psum x2, waiting for transfers between devices, input_total(): return lax.psum(partial_sum, 'mp')  63.5 us
    unnamed x125, local copies, waits for them, and re-layouts  44.3 us
    reduce_scatter x1, waiting for transfers between devices, per_device(): lax.psum_scatter(image_part.astype(jnp.bfloat16), 'mp', scatter_dimension...  40.7 us
    all_gather x1, blocking collectives, per_device(): lax.all_gather(self_qkv, 'dp', axis=1, tiled=True)  40.5 us
  transfers between devices with their start and end apart: 15, of which 12 were waited for; matrix products, arithmetic and copies ran while one was open for 12% of the time, Pallas kernels for 0%

commit v1 on v0

v1 whole, which is shorter than its diff:
```python
import functools
import math

import jax
import jax.numpy as jnp
from jax import lax
from jax.experimental import pallas as pl
from jax.experimental.pallas import tpu as pltpu
from jax.sharding import PartitionSpec as P

BF = jnp.bfloat16
F32 = jnp.float32
HEAD_DIM = 64
SCALE = HEAD_DIM ** (-0.5)
NORM_EPS = 1e-05
NEG_FILL = -1e30
INV_ROOT_TWO = 1.0 / math.sqrt(2.0)
INV_ROOT_TAU = 1.0 / math.sqrt(2.0 * math.pi)
VMEM_LIMIT = 40 * 1024 * 1024


def nn(a, b):
    return lax.dot_general(a, b, (((1,), (0,)), ((), ())), preferred_element_type=F32)


def nt(a, b):
    return lax.dot_general(a, b, (((1,), (1,)), ((), ())), preferred_element_type=F32)


def tn(a, b):
    return lax.dot_general(a, b, (((0,), (0,)), ((), ())), preferred_element_type=F32)


def norm_parts(values):
    centered = values - jnp.mean(values, axis=-1, keepdims=True)
    inv_std = lax.rsqrt(jnp.mean(centered * centered, axis=-1, keepdims=True) + NORM_EPS)
    return centered * inv_std, inv_std


def norm_back(grad, normed, inv_std, gain_row):
    scaled = grad * gain_row
    first = jnp.mean(scaled, axis=-1, keepdims=True)
    second = jnp.mean(scaled * normed, axis=-1, keepdims=True)
    return inv_std * (scaled - first - normed * second)


def head_masks(width, kind):
    column = lax.broadcasted_iota(jnp.int32, (1, width), 1) // HEAD_DIM
    return [(column == h).astype(F32).astype(kind) for h in range(width // HEAD_DIM)]


def stack_heads(rows, masks):
    return jnp.concatenate([rows * m for m in masks], axis=0)


def unstack_heads(stacked, masks):
    count = stacked.shape[0] // len(masks)
    total = stacked[:count] * masks[0]
    for h in range(1, len(masks)):
        total = total + stacked[h * count : (h + 1) * count] * masks[h]
    return total


def call(body, name, outs, scalars, arrays, scratch=(), flops=0):
    nbytes = sum(a.size * a.dtype.itemsize for a in arrays)
    nbytes += sum(math.prod(s) * jnp.dtype(d).itemsize for s, d in outs)
    return pl.pallas_call(
        body,
        out_shape=[jax.ShapeDtypeStruct(s, d) for s, d in outs],
        in_specs=[pl.BlockSpec(memory_space=pltpu.SMEM)] * len(scalars)
        + [pl.BlockSpec(memory_space=pltpu.VMEM)] * len(arrays),
        out_specs=[pl.BlockSpec(memory_space=pltpu.VMEM)] * len(outs),
        scratch_shapes=list(scratch),
        compiler_params=pltpu.CompilerParams(vmem_limit_bytes=VMEM_LIMIT),
        cost_estimate=pl.CostEstimate(flops=flops, bytes_accessed=nbytes, transcendentals=0),
        name=name,
    )(*scalars, *arrays)


def block_rows(tab, k, height):
    return pl.ds(pl.multiple_of(tab[k], 32), height)


def place_pieces(tab, pieces, targets):
    height = pieces[0].shape[0]
    for k, piece in enumerate(pieces):
        rows = block_rows(tab, k, height) if len(pieces) > 1 else slice(None)
        start = 0
        for target in targets:
            width = target.shape[1]
            target[rows, :] = piece[:, start : start + width]
            start += width


def join_halves(tab, own, other, target):
    half = own.shape[0]
    target[pl.ds(pl.multiple_of(tab[8], 32), half), :] = own[...]
    target[pl.ds(pl.multiple_of(tab[9], 32), half), :] = other[...]


def split_halves(tab, full, send, keep):
    half = send.shape[0]
    keep[...] = full[pl.ds(pl.multiple_of(tab[8], 32), half), :].astype(keep.dtype)
    send[...] = full[pl.ds(pl.multiple_of(tab[9], 32), half), :].astype(send.dtype)


def pack_self_kernel(qkv, out, packed):
    width = qkv.shape[2]
    for j in range(3):
        packed[:, j * width : (j + 1) * width] = qkv[j]
    packed[:, 3 * width :] = out[...].astype(F32).T.astype(BF)


def pack_rest_kernel(query, keyval, out, up, down, cross, ffn):
    width = query.shape[1]
    cross[:, :width] = query[...]
    cross[:, width : 2 * width] = keyval[0]
    cross[:, 2 * width : 3 * width] = keyval[1]
    cross[:, 3 * width :] = out[...].astype(F32).T.astype(BF)
    hidden = up.shape[1]
    ffn[:, :hidden] = up[...]
    ffn[:, hidden:] = down[...].astype(F32).T.astype(BF)


def self_forward_kernel(count, seqs, tab, lens, text, gain, bias, *refs):
    pieces, (wq, wk, wv, wo, normed, q, k, v, prob, ctx, send, keep, full) = (
        refs[:count],
        refs[count:],
    )
    place_pieces(tab, pieces, (wq, wk, wv, wo))
    n, _ = norm_parts(text[...].astype(F32))
    low = (n * gain[0:1] + bias[0:1]).astype(BF)
    normed[...] = low
    for w, target in ((wq, q), (wk, k), (wv, v)):
        target[...] = nn(low, w[...]).astype(BF)
    width = q.shape[1]
    low_masks, masks = head_masks(width, BF), head_masks(width, F32)
    rows = text.shape[0] // seqs
    stacked = rows * len(masks)
    query_at = lax.broadcasted_iota(jnp.int32, (stacked, rows), 0) % rows
    key_at = lax.broadcasted_iota(jnp.int32, (stacked, rows), 1)
    for b in range(seqs):
        at = slice(b * rows, (b + 1) * rows)
        scores = nt(stack_heads(q[at], low_masks), k[at]) * SCALE
        allowed = (key_at <= query_at) & (key_at < lens[b])
        scores = jnp.where(allowed, scores, NEG_FILL)
        raised = jnp.exp(scores - jnp.max(scores, axis=-1, keepdims=True))
        p = raised / jnp.sum(raised, axis=-1, keepdims=True)
        prob[b] = p
        ctx[at] = unstack_heads(nn(p.astype(BF), v[at]), masks).astype(BF)
    full[...] = nt(ctx[...], wo[...])
    split_halves(tab, full, send, keep)


def keyval_kernel(count, tab, image, *refs):
    pieces, (wq, wk, wv, wo, keys, values) = refs[:count], refs[count:]

    @pl.when(pl.program_id(0) == 0)
    def _():
        place_pieces(tab, pieces, (wq, wk, wv, wo))

    keys[...] = nn(image[...], wk[...]).astype(BF)
    values[...] = nn(image[...], wv[...]).astype(BF)


def norm_kernel(index, sliced, tab, chip, other, resid, out_bias, gain, bias, hidden, normed):
    half = chip.shape[0]
    if sliced:
        base = resid[pl.ds(pl.multiple_of(tab[8], 32), half), :].astype(F32)
    else:
        base = resid[...]
    value = (
        base
        + (chip[...].astype(F32) + other[...].astype(F32))
        + out_bias[index : index + 1]
    )
    hidden[...] = value
    n, _ = norm_parts(value)
    normed[...] = (n * gain[index + 1 : index + 2] + bias[index + 1 : index + 2]).astype(BF)


def cross_forward_kernel(
    seqs, tab, counts, own, other, wq, wo, keys, values, normed, q, prob, ctx, send, keep, full
):
    join_halves(tab, own, other, normed)
    q[...] = nn(normed[...], wq[...]).astype(BF)
    width = q.shape[1]
    low_masks, masks = head_masks(width, BF), head_masks(width, F32)
    rows = normed.shape[0] // seqs
    patches = keys.shape[0] // seqs
    patch_at = lax.broadcasted_iota(jnp.int32, (rows * len(masks), patches), 1)
    for b in range(seqs):
        at = slice(b * rows, (b + 1) * rows)
        ks = slice(b * patches, (b + 1) * patches)
        scores = nt(stack_heads(q[at], low_masks), keys[ks]) * SCALE
        scores = jnp.where(patch_at < counts[b], scores, NEG_FILL)
        raised = jnp.exp(scores - jnp.max(scores, axis=-1, keepdims=True))
        p = raised / jnp.sum(raised, axis=-1, keepdims=True)
        prob[b] = p
        ctx[at] = unstack_heads(nn(p.astype(BF), values[ks]), masks).astype(BF)
    full[...] = nt(ctx[...], wo[...])
    split_halves(tab, full, send, keep)


def ffn_ready_kernel(count, tab, grad, *refs):
    pieces, (up, down, grad_act) = refs[:count], refs[count:]
    place_pieces(tab, pieces, (up, down))
    grad_act[...] = nn(grad[...], down[...])


def ffn_kernel(
    tab, own, other, up, down, grad_act, up_bias,
    normed, act, grad_low, bias_sum, send, keep, out_send, out_keep, full,
):
    join_halves(tab, own, other, normed)
    pre = nn(normed[...], up[...]) + up_bias[...]
    cdf = 0.5 * (1.0 + lax.erf(pre * INV_ROOT_TWO))
    density = jnp.exp(-0.5 * pre * pre) * INV_ROOT_TAU
    grad_pre = grad_act[...] * (cdf + pre * density)
    grad_low[...] = grad_pre.astype(BF)
    act[...] = (pre * cdf).astype(BF)
    bias_sum[...] = jnp.sum(grad_pre, axis=0, keepdims=True)
    full[...] = nt(grad_low[...], up[...])
    split_halves(tab, full, send, keep)
    full[...] = nt(act[...], down[...])
    split_halves(tab, full, out_send, out_keep)


def scatter_blocks(tab, matrix, column, outs):
    blocks = sum(o.shape[0] for o in outs)
    height = outs[0].shape[1]
    width = matrix.shape[1]
    for k in range(blocks):
        rows = block_rows(tab, k, height) if blocks > 1 else slice(None)
        target = outs[k // outs[0].shape[0]]
        target[k % outs[0].shape[0], :, column : column + width] = matrix[rows, :].astype(BF)


def ffn_weight_kernel(parts, tab, normed, grad_low, grad, act, *refs):
    outs, full = refs[:parts], refs[parts]
    full[...] = tn(normed[...], grad_low[...])
    scatter_blocks(tab, full, 0, outs)
    full[...] = tn(grad[...], act[...])
    scatter_blocks(tab, full, full.shape[1], outs)


def norm_back_kernel(index, sliced, tab, chip, other, hidden, resid, gain, total, low, vec):
    half = chip.shape[0]
    if sliced:
        base = resid[pl.ds(pl.multiple_of(tab[8], 32), half), :].astype(F32)
    else:
        base = resid[...]
    grad = chip[...].astype(F32) + other[...].astype(F32)
    n, inv_std = norm_parts(hidden[...])
    value = base + norm_back(grad, n, inv_std, gain[index : index + 1])
    total[...] = value
    low[...] = value.astype(BF)
    vec[...] = jnp.zeros_like(vec)
    vec[0:1] = 0.5 * jnp.sum(grad * n, axis=0, keepdims=True)
    vec[1:2] = 0.5 * jnp.sum(grad, axis=0, keepdims=True)
    vec[2:3] = 0.5 * jnp.sum(value, axis=0, keepdims=True)
    if sliced:
        vec[3:4] = 0.5 * jnp.sum(base, axis=0, keepdims=True)


def attention_back(p, q_stack, keys, values, grad_stack):
    grad_p = nt(grad_stack, values)
    inner = jnp.sum(p * grad_p, axis=-1, keepdims=True)
    ds = (p * (grad_p - inner)).astype(BF)
    return (
        nn(ds, keys) * SCALE,
        (tn(ds, q_stack) * SCALE).astype(BF),
        tn(p.astype(BF), grad_stack).astype(BF),
    )


def cross_back_kernel(
    seqs, tab, own, other, wq, wo, keys, values, q, prob, grad_two, dq, dk, dv, send, keep, full
):
    join_halves(tab, own, other, grad_two)
    grad_ctx = nn(grad_two[...], wo[...]).astype(BF)
    width = q.shape[1]
    low_masks, masks = head_masks(width, BF), head_masks(width, F32)
    rows = q.shape[0] // seqs
    patches = keys.shape[0] // seqs
    for b in range(seqs):
        at = slice(b * rows, (b + 1) * rows)
        ks = slice(b * patches, (b + 1) * patches)
        gq, gk, gv = attention_back(
            prob[b],
            stack_heads(q[at], low_masks),
            keys[ks],
            values[ks],
            stack_heads(grad_ctx[at], low_masks),
        )
        dq[at] = unstack_heads(gq, masks).astype(BF)
        dk[ks] = gk
        dv[ks] = gv
    full[...] = nt(dq[...], wq[...])
    split_halves(tab, full, send, keep)


def cross_weight_kernel(parts, tab, image, dk, dv, normed, dq, grad_two, ctx, *refs):
    outs, (acc_k, acc_v) = refs[:parts], refs[parts:]
    step = pl.program_id(0)

    @pl.when(step == 0)
    def _():
        acc_k[...] = tn(normed[...], dq[...])
        acc_v[...] = tn(grad_two[...], ctx[...])
        width = acc_k.shape[1]
        scatter_blocks(tab, acc_k, 0, outs)
        scatter_blocks(tab, acc_v, 3 * width, outs)
        acc_k[...] = jnp.zeros_like(acc_k)
        acc_v[...] = jnp.zeros_like(acc_v)

    acc_k[...] += tn(image[...], dk[...])
    acc_v[...] += tn(image[...], dv[...])

    @pl.when(step == pl.num_programs(0) - 1)
    def _():
        width = acc_k.shape[1]
        scatter_blocks(tab, acc_k, width, outs)
        scatter_blocks(tab, acc_v, 2 * width, outs)


def image_part_kernel(tab, dk, dv, wk, wv, send, keep):
    width = wk.shape[1]
    for target, first in ((keep, 10), (send, 12)):
        for j in range(2):
            rows = pl.ds(pl.multiple_of(tab[first + j], 64), width)
            part = nt(dk[...], wk[rows, :]) + nt(dv[...], wv[rows, :])
            target[:, j * width : (j + 1) * width] = part.astype(BF)


def image_chip_kernel(keep, other, own, send):
    total = keep[...].astype(F32) + other[...].astype(F32)
    width = own.shape[1]
    half = send.shape[0]
    own[...] = total[:, :width].astype(BF)
    away = total[:, width:]
    send[:, :width] = away[:half].astype(BF)
    send[:, width:] = away[half:].astype(BF)


def image_sum_kernel(own, other, out):
    half = other.shape[0]
    width = own.shape[1]
    out[:half] = own[:half].astype(F32) + other[:, :width].astype(F32)
    out[half:] = own[half:].astype(F32) + other[:, width:].astype(F32)


def self_back_kernel(
    seqs, parts, tab, own, other, text, gain, normed, wq, wk, wv, wo, q, k, v, prob, ctx, *refs
):
    outs = refs[:parts]
    send, keep, vec, low, dq, dk, dv, full, narrow = refs[parts:]
    join_halves(tab, own, other, low)
    grad_ctx = nn(low[...], wo[...]).astype(BF)
    width = q.shape[1]
    low_masks, masks = head_masks(width, BF), head_masks(width, F32)
    rows = q.shape[0] // seqs
    for b in range(seqs):
        at = slice(b * rows, (b + 1) * rows)
        gq, gk, gv = attention_back(
            prob[b],
            stack_heads(q[at], low_masks),
            k[at],
            v[at],
            stack_heads(grad_ctx[at], low_masks),
        )
        dq[at] = unstack_heads(gq, masks).astype(BF)
        dk[at] = gk
        dv[at] = gv
    for j, (left, right) in enumerate(((normed, dq), (normed, dk), (normed, dv), (low, ctx))):
        narrow[...] = tn(left[...], right[...])
        scatter_blocks(tab, narrow, j * width, outs)
    full[...] = nt(dq[...], wq[...]) + nt(dk[...], wk[...]) + nt(dv[...], wv[...])
    split_halves(tab, full, send, keep)
    n, _ = norm_parts(text[...].astype(F32))
    part = full[...]
    vec[...] = jnp.zeros_like(vec)
    vec[0:1] = jnp.sum(part * n, axis=0, keepdims=True)
    vec[1:2] = jnp.sum(part, axis=0, keepdims=True)


def text_grad_kernel(tab, chip, other, text, resid, gain, out):
    half = chip.shape[0]
    grad = chip[...].astype(F32) + other[...].astype(F32)
    base = text[pl.ds(pl.multiple_of(tab[8], 32), half), :].astype(F32)
    n, inv_std = norm_parts(base)
    out[...] = resid[...] + norm_back(grad, n, inv_std, gain[0:1])


def layer_out_kernel(chip, other, hidden, out_bias, out):
    out[...] = (
        hidden[...] + (chip[...].astype(F32) + other[...].astype(F32)) + out_bias[2:3]
    ).astype(BF)


def join_kernel(tab, own, other, out):
    join_halves(tab, own, other, out)


def add_kernel(keep, other, *outs):
    for k, out in enumerate(outs):
        out[...] = (keep[k].astype(F32) + other[k].astype(F32)).astype(BF)


def sum_pieces(refs):
    total = refs[0][...].astype(F32)
    for ref in refs[1:]:
        total = total + ref[...].astype(F32)
    return total


def close_self_kernel(count, *refs):
    pieces, (qkv, out) = refs[:count], refs[count:]
    total = sum_pieces(pieces)
    width = qkv.shape[2]
    for j in range(3):
        qkv[j] = total[:, j * width : (j + 1) * width]
    out[...] = total[:, 3 * width :].T


def close_cross_kernel(count, *refs):
    pieces, (query, keyval, out) = refs[:count], refs[count:]
    total = sum_pieces(pieces)
    width = query.shape[1]
    query[...] = total[:, :width]
    keyval[0] = total[:, width : 2 * width]
    keyval[1] = total[:, 2 * width : 3 * width]
    out[...] = total[:, 3 * width :].T


def close_ffn_kernel(count, *refs):
    pieces, (up, down) = refs[:count], refs[count:]
    total = sum_pieces(pieces)
    hidden = up.shape[1]
    up[...] = total[:, :hidden]
    down[...] = total[:, hidden:].T


def swap(value, axis, size, bits):
    return lax.ppermute(value, axis, [(i, i ^ bits) for i in range(size)])


def per_device(
    dp_size,
    mp_size,
    text_tokens,
    image_tokens,
    text_lengths,
    patch_counts,
    self_qkv,
    self_out,
    cross_query,
    cross_keyval,
    cross_out,
    mlp_up,
    mlp_down,
    norm_gain,
    norm_bias,
    out_bias,
    up_bias,
    out_grad,
):
    seqs, positions, model = text_tokens.shape
    patches = image_tokens.shape[1]
    rows = seqs * positions
    half = rows // 2
    width = cross_query.shape[1]
    hidden = mlp_up.shape[1]
    image_rows = seqs * patches
    quick = dp_size == 8
    height = model // dp_size
    place = lax.axis_index("dp")
    lane = lax.axis_index("mp")
    core, level = lane % 2, lane // 2
    if quick:
        offsets = [(place ^ (((k & 3) << 1) | (k >> 2))) * height for k in range(8)]
        count, parts, out_blocks = 8, 2, [(4, height)] * 2
    else:
        offsets = [place * 0] * 8
        count, parts, out_blocks = 1, 1, [(1, model)]
    blocks = [(2 * (level ^ j) + (core ^ side)) * width for side in range(2) for j in range(2)]
    tab = jnp.stack(offsets + [core * half, (1 - core) * half] + blocks + [core, level]).astype(
        jnp.int32
    )

    def gather(shard):
        if not quick:
            return [lax.all_gather(shard, "dp", axis=0, tiled=True)]
        near = [shard] + [swap(shard, "dp", 8, k << 1) for k in (1, 2, 3)]
        return near + [swap(piece, "dp", 8, 1) for piece in near]

    def reduce_scatter(outs):
        if not quick:
            total = lax.psum_scatter(outs[0][0], "dp", scatter_dimension=0, tiled=True)
            return [total]
        keep, send = outs
        other = swap(send, "dp", 8, 1)
        near = call(
            add_kernel, "add_blocks", [(keep.shape[1:], BF)] * 4, (), (keep, other)
        )
        return [near[0]] + [swap(near[k], "dp", 8, k << 1) for k in (1, 2, 3)]

    def mp_sum(send, keep):
        other = swap(send, "mp", mp_size, 1)
        chip = (keep.astype(F32) + other.astype(F32)).astype(BF)
        return chip, swap(chip, "mp", mp_size, 2)

    def core_swap(value):
        return swap(value, "mp", mp_size, 1)

    text = text_tokens.reshape(rows, model)
    image = image_tokens.reshape(image_rows, model)
    grad = out_grad.reshape(rows, model)

    if quick:
        (self_shard,) = call(
            pack_self_kernel, "pack_self", [((height, 4 * width), BF)], (), (self_qkv, self_out)
        )
        cross_shard, ffn_shard = call(
            pack_rest_kernel,
            "pack_rest",
            [((height, 4 * width), BF), ((height, 2 * hidden), BF)],
            (),
            (cross_query, cross_keyval, cross_out, mlp_up, mlp_down),
        )
    else:
        self_shard = jnp.concatenate([self_qkv[0], self_qkv[1], self_qkv[2], self_out.T], 1)
        cross_shard = jnp.concatenate(
            [cross_query, cross_keyval[0], cross_keyval[1], cross_out.T], 1
        )
        ffn_shard = jnp.concatenate([mlp_up, mlp_down.T], 1)
    self_pieces = gather(self_shard)
    cross_pieces = gather(cross_shard)
    ffn_pieces = gather(ffn_shard)

    square = ((model, width), BF)
    narrow = ((rows, width), BF)
    wide = ((rows, model), BF)
    halves = [((half, model), BF)] * 2
    half_f32 = ((half, model), F32)
    half_low = ((half, model), BF)
    heads = width // HEAD_DIM
    full = pltpu.VMEM((rows, model), F32)

    (wq, wk, wv, wo, normed_text, q, k, v, self_prob, self_ctx, send, keep) = call(
        functools.partial(self_forward_kernel, count, seqs),
        "self_forward",
        [square] * 4
        + [wide]
        + [narrow] * 3
        + [((seqs, heads * positions, positions), F32), narrow]
        + halves,
        (tab, text_lengths),
        (text, norm_gain, norm_bias, *self_pieces),
        [full],
        flops=2 * rows * model * width * 4,
    )
    chip, other = mp_sum(send, keep)

    constant = lambda b: (0, 0)
    per_seq = lambda b: (b, 0)
    cq, ck, cv, co, keys, values = pl.pallas_call(
        functools.partial(keyval_kernel, count),
        grid=(seqs,),
        out_shape=[jax.ShapeDtypeStruct((model, width), BF)] * 4
        + [jax.ShapeDtypeStruct((image_rows, width), BF)] * 2,
        in_specs=[
            pl.BlockSpec(memory_space=pltpu.SMEM),
            pl.BlockSpec((patches, model), per_seq),
        ]
        + [pl.BlockSpec(cross_pieces[0].shape, constant)] * count,
        out_specs=[pl.BlockSpec((model, width), constant)] * 4
        + [pl.BlockSpec((patches, width), per_seq)] * 2,
        compiler_params=pltpu.CompilerParams(vmem_limit_bytes=VMEM_LIMIT),
        cost_estimate=pl.CostEstimate(
            flops=2 * image_rows * model * width * 2,
            bytes_accessed=image.size * 2,
            transcendentals=0,
        ),
        name="keyval",
    )(tab, image, *cross_pieces)

    hidden_one, normed_half = call(
        functools.partial(norm_kernel, 0, True),
        "norm_mid",
        [half_f32, half_low],
        (tab,),
        (chip, other, text, out_bias, norm_gain, norm_bias),
    )
    normed_mid, xq, cross_prob, cross_ctx, send, keep = call(
        functools.partial(cross_forward_kernel, seqs),
        "cross_forward",
        [wide, narrow, ((seqs, heads * positions, patches), F32), narrow] + halves,
        (tab, patch_counts),
        (normed_half, core_swap(normed_half), cq, co, keys, values),
        [full],
        flops=2 * rows * model * width * 2,
    )
    chip, other = mp_sum(send, keep)
    w_up, w_down, grad_act = call(
        functools.partial(ffn_ready_kernel, count),
        "ffn_ready",
        [((model, hidden), BF)] * 2 + [((rows, hidden), F32)],
        (tab,),
        (grad, *ffn_pieces),
        flops=2 * rows * model * hidden,
    )
    hidden_two, normed_half = call(
        functools.partial(norm_kernel, 1, False),
        "norm_ffn",
        [half_f32, half_low],
        (tab,),
        (chip, other, hidden_one, out_bias, norm_gain, norm_bias),
    )
    (normed_ffn, act, grad_low, up_sum, send, keep, out_send, out_keep) = call(
        ffn_kernel,
        "ffn",
        [wide, ((rows, hidden), BF), ((rows, hidden), BF), ((1, hidden), F32)] + halves + halves,
        (tab,),
        (
            normed_half,
            core_swap(normed_half),
            w_up,
            w_down,
            grad_act,
            up_bias.reshape(1, hidden),
        ),
        [full],
        flops=2 * rows * model * hidden * 3,
    )
    chip, other = mp_sum(send, keep)
    out_chip, out_other = mp_sum(out_send, out_keep)

    ffn_blocks = call(
        functools.partial(ffn_weight_kernel, parts),
        "ffn_weights",
        [(b + (2 * hidden,), BF) for b in out_blocks],
        (tab,),
        (normed_ffn, grad_low, grad, act),
        [pltpu.VMEM((model, hidden), F32)],
        flops=2 * rows * model * hidden * 2,
    )
    ffn_sums = reduce_scatter(ffn_blocks)
    vec_shape = ((8, model), F32)
    grad_two, low_half, vec_two = call(
        functools.partial(norm_back_kernel, 2, True),
        "norm_back_ffn",
        [half_f32, half_low, vec_shape],
        (tab,),
        (chip, other, hidden_two, grad, norm_gain),
    )
    grad_two_low, dq, dk, dv, send, keep = call(
        functools.partial(cross_back_kernel, seqs),
        "cross_back",
        [wide, narrow, ((image_rows, width), BF), ((image_rows, width), BF)] + halves,
        (tab,),
        (low_half, core_swap(low_half), cq, co, keys, values, xq, cross_prob),
        [full],
        flops=2 * rows * model * width * 2,
    )
    chip, other = mp_sum(send, keep)
    whole = lambda shape: pl.BlockSpec(shape, lambda b: (0,) * len(shape))
    cross_blocks = pl.pallas_call(
        functools.partial(cross_weight_kernel, parts),
        grid=(seqs,),
        out_shape=[jax.ShapeDtypeStruct(b + (4 * width,), BF) for b in out_blocks],
        in_specs=[
            pl.BlockSpec(memory_space=pltpu.SMEM),
            pl.BlockSpec((patches, model), per_seq),
            pl.BlockSpec((patches, width), per_seq),
            pl.BlockSpec((patches, width), per_seq),
            whole((rows, model)),
            whole((rows, width)),
            whole((rows, model)),
            whole((rows, width)),
        ],
        out_specs=[whole(b + (4 * width,)) for b in out_blocks],
        scratch_shapes=[pltpu.VMEM((model, width), F32)] * 2,
        compiler_params=pltpu.CompilerParams(vmem_limit_bytes=VMEM_LIMIT),
        cost_estimate=pl.CostEstimate(
            flops=2 * image_rows * model * width * 2,
            bytes_accessed=image.size * 2,
            transcendentals=0,
        ),
        name="cross_weights",
    )(tab, image, dk, dv, normed_mid, dq, grad_two_low, cross_ctx)
    cross_sums = reduce_scatter(cross_blocks)
    image_send, image_keep = pl.pallas_call(
        image_part_kernel,
        grid=(seqs,),
        out_shape=[jax.ShapeDtypeStruct((image_rows, 2 * width), BF)] * 2,
        in_specs=[
            pl.BlockSpec(memory_space=pltpu.SMEM),
            pl.BlockSpec((patches, width), per_seq),
            pl.BlockSpec((patches, width), per_seq),
            whole((model, width)),
            whole((model, width)),
        ],
        out_specs=[pl.BlockSpec((patches, 2 * width), per_seq)] * 2,
        compiler_params=pltpu.CompilerParams(vmem_limit_bytes=VMEM_LIMIT),
        cost_estimate=pl.CostEstimate(
            flops=2 * image_rows * model * width * 2,
            bytes_accessed=image.size * 2,
            transcendentals=0,
        ),
        name="image_part",
    )(tab, dk, dv, ck, cv)
    image_own, image_away = call(
        image_chip_kernel,
        "image_chip",
        [((image_rows, width), BF), ((image_rows // 2, 2 * width), BF)],
        (),
        (image_keep, core_swap(image_send)),
    )
    (image_grad,) = call(
        image_sum_kernel,
        "image_sum",
        [((image_rows, width), F32)],
        (),
        (image_own, swap(image_away, "mp", mp_size, 2)),
    )
    grad_one, low_half, vec_one = call(
        functools.partial(norm_back_kernel, 1, False),
        "norm_back_mid",
        [half_f32, half_low, vec_shape],
        (tab,),
        (chip, other, hidden_one, grad_two, norm_gain),
    )
    self_back = call(
        functools.partial(self_back_kernel, seqs, parts),
        "self_back",
        [(b + (4 * width,), BF) for b in out_blocks] + halves + [vec_shape],
        (tab,),
        (
            low_half,
            core_swap(low_half),
            text,
            norm_gain,
            normed_text,
            wq,
            wk,
            wv,
            wo,
            q,
            k,
            v,
            self_prob,
            self_ctx,
        ),
        [
            pltpu.VMEM((rows, model), BF),
            pltpu.VMEM((rows, width), BF),
            pltpu.VMEM((rows, width), BF),
            pltpu.VMEM((rows, width), BF),
            full,
            pltpu.VMEM((model, width), F32),
        ],
        flops=2 * rows * model * width * 8,
    )
    self_blocks, (send, keep, vec_zero) = self_back[:parts], self_back[parts:]
    self_sums = reduce_scatter(self_blocks)
    chip, other = mp_sum(send, keep)
    (text_half,) = call(
        text_grad_kernel,
        "text_grad",
        [half_f32],
        (tab,),
        (chip, other, text, grad_one, norm_gain),
    )
    (text_grad,) = call(
        join_kernel, "text_join", [((rows, model), F32)], (tab,), (text_half, core_swap(text_half))
    )
    (out_half,) = call(
        layer_out_kernel,
        "layer_out",
        [half_low],
        (),
        (out_chip, out_other, hidden_two, out_bias),
    )
    (layer_out,) = call(join_kernel, "out_join", [wide], (tab,), (out_half, core_swap(out_half)))

    vector = jnp.concatenate(
        [
            vec_zero[0:1],
            vec_one[0:1],
            vec_two[0:1],
            vec_zero[1:2],
            vec_one[1:2],
            vec_two[1:2],
            vec_one[2:3],
            vec_two[2:3],
            vec_two[3:4],
        ],
        axis=0,
    )
    if quick:
        for bits in (1, 2):
            vector = vector + swap(vector, "mp", mp_size, bits)
        vector = jnp.concatenate([vector, up_sum], axis=0)
        for bits in (1, 2, 4):
            vector = vector + swap(vector, "dp", dp_size, bits)
        gains, shifts, biases, ups = vector[0:3], vector[3:6], vector[6:9], vector[9]
    else:
        vector = lax.psum(vector, ("dp", "mp"))
        ups = lax.psum(up_sum, "dp")[0]
        gains, shifts, biases = vector[0:3], vector[3:6], vector[6:9]

    if quick:
        qkv_grad, self_out_grad = call(
            functools.partial(close_self_kernel, 4),
            "close_self",
            [((3, height, width), F32), ((width, height), F32)],
            (),
            self_sums,
        )
        query_grad, keyval_grad, cross_out_grad = call(
            functools.partial(close_cross_kernel, 4),
            "close_cross",
            [((height, width), F32), ((2, height, width), F32), ((width, height), F32)],
            (),
            cross_sums,
        )
        up_grad, down_grad = call(
            functools.partial(close_ffn_kernel, 4),
            "close_ffn",
            [((height, hidden), F32), ((hidden, height), F32)],
            (),
            ffn_sums,
        )
    else:
        total = self_sums[0].astype(F32)
        qkv_grad = jnp.stack([total[:, j * width : (j + 1) * width] for j in range(3)])
        self_out_grad = total[:, 3 * width :].T
        total = cross_sums[0].astype(F32)
        query_grad = total[:, :width]
        keyval_grad = jnp.stack([total[:, j * width : (j + 1) * width] for j in (1, 2)])
        cross_out_grad = total[:, 3 * width :].T
        total = ffn_sums[0].astype(F32)
        up_grad, down_grad = total[:, :hidden], total[:, hidden:].T
    return (
        layer_out.reshape(seqs, positions, model),
        text_grad.reshape(seqs, positions, model),
        image_grad.reshape(seqs, patches, width),
        qkv_grad,
        self_out_grad,
        query_grad,
        keyval_grad,
        cross_out_grad,
        up_grad,
        down_grad,
        gains,
        shifts,
        biases,
        ups,
    )


def solution(mesh):
    placed = (
        P("dp", None, None),
        P("dp", None, None),
        P("dp"),
        P("dp"),
        P(None, "dp", "mp"),
        P("mp", "dp"),
        P("dp", "mp"),
        P(None, "dp", "mp"),
        P("mp", "dp"),
        P("dp", "mp"),
        P("mp", "dp"),
        P(),
        P(),
        P(),
        P("mp"),
        P("dp", None, None),
    )
    return jax.shard_map(
        functools.partial(per_device, mesh.shape["dp"], mesh.shape["mp"]),
        mesh=mesh,
        in_specs=placed,
        out_specs=(
            P("dp", None, None),
            P("dp", None, None),
            P("dp", None, "mp"),
            P(None, "dp", "mp"),
            P("mp", "dp"),
            P("dp", "mp"),
            P(None, "dp", "mp"),
            P("mp", "dp"),
            P("dp", "mp"),
            P("mp", "dp"),
            P(),
            P(),
            P(),
            P("mp"),
        ),
        check_vma=False,
    )
```

time: 989 us -> 262 us (0.26)
  waiting for transfers between devices: 536 us -> 118 us
  blocking collectives: 209 us -> 0 us
  local copies, waits for them, and re-layouts: 112 us -> 26.8 us
  matrix products: 67.6 us -> 0 us
  starting transfers between devices: 1.11 us -> 62 us
  Pallas kernels: 0 us -> 51.1 us
  other arithmetic: 36.8 us -> 2.06 us
  between operations: 16.4 us -> 1.3 us
    reduce_scatter x4 -> x0, waiting for transfers between devices: 250 us -> none  [the longest x1 72.7 us: per_device(): lax.psum_scatter(grad_down, 'dp', scatter_dimension=1, tiled=True)]
    all_gather x5 -> x0, blocking collectives: 170 us -> none  [the longest x1 40.5 us: per_device(): lax.all_gather(self_qkv, 'dp', axis=1, tiled=True)]
    unnamed x19 -> x0, waiting for transfers between devices: 145 us -> none
    ppermute x0 -> x58, waiting for transfers between devices: none -> 118 us  [swap(): return lax.ppermute(value, axis, [(i, i ^ bits) for i in range(size)])]
    psum x5 -> x0, waiting for transfers between devices: 96.3 us -> none  [the longest x2 63.5 us: input_total(): return lax.psum(partial_sum, 'mp')]
    ppermute x0 -> x58, starting transfers between devices: none -> 62 us  [swap(): return lax.ppermute(value, axis, [(i, i ^ bits) for i in range(size)])]
    dot_general x30 -> x0, matrix products: 61.2 us -> none  [the longest x1 5.56 us: per_device(): jnp.einsum('jtc,jdc->td', grad_keyval, use_kv, preferred_element_type=jnp...]
    pallas_call x0 -> x28, Pallas kernels: none -> 51.1 us  [the longest x25 37 us: call(): pl.pallas_call(body, out_shape=[jax.ShapeDtypeStruct(s, d) for s, d in ou...]
  transfers between devices with their start and end apart: 15 -> 58, of which waited for: 12 -> 25; matrix products, arithmetic and copies ran while one was open for 12% -> 3% of each run, Pallas kernels for 0% -> 14%
where the time goes in v1:
time: 262 us; the launch traced here: 261 us
  waiting for transfers between devices  118 us (45%)
  starting transfers between devices  62 us (24%)
  Pallas kernels  51.1 us (20%)
  local copies, waits for them, and re-layouts  26.8 us (10%)
    ppermute x58, waiting for transfers between devices, swap(): return lax.ppermute(value, axis, [(i, i ^ bits) for i in range(size)])  118 us
    ppermute x58, starting transfers between devices, swap(): return lax.ppermute(value, axis, [(i, i ^ bits) for i in range(size)])  62 us
    pallas_call x25, Pallas kernels, call(): pl.pallas_call(body, out_shape=[jax.ShapeDtypeStruct(s, d) for s, d in ou...  37 us
    unnamed x115, local copies, waits for them, and re-layouts  22.1 us
    pallas_call x1, Pallas kernels, per_device(): pl.pallas_call(functools.partial(cross_weight_kernel, parts), grid=(seqs,...  5.83 us
  transfers between devices with their start and end apart: 58, of which 25 were waited for; matrix products, arithmetic and copies ran while one was open for 3% of the time, Pallas kernels for 14%

profile of v1, /device:TPU:0, one launch (start us, length us, event | category | flops | bytes accessed | tf_op | source)
XLA Modules:
  0.0 261.3 jit_solution(16248809662270683397)
XLA Ops:
  2.5 5.1 %collective-permute-start.2 = (bf16[96,768]{1,0:T(8,128)(2,1)S(1)}, bf16[96,768]{1,0:T(8,128)(2,1)S(1)}, u32[]{:S(2)}, u32[]{:S(2)}) collective-permute-start(bf16[96,768]{1,0:T(8,128)(2,1)S(1)} %pack_self.1.refs_0_), channel_id=1, source_target_pairs={{0,24},{4,28},{8,16},{12,20},{16,8},{20,12},{24,0},{28,4},{1,25},{... | collective-permute-start | bytes 442376 | tf_op jit(solution)/shard_map/ppermute | solution.py:445
  14.1 6.0 %collective-permute-done.1.refs_2_ = bf16[96,768]{1,0:T(8,128)(2,1)S(1)} collective-permute-done((bf16[96,768]{1,0:T(8,128)(2,1)S(1)}, bf16[96,768]{1,0:T(8,128)(2,1)S(1)}, u32[]{:S(2)}, u32[]{:S(2)}) %collective-permute-start.1) | collective-permute-done | bytes 147488 | tf_op jit(solution)/shard_map/ppermute | solution.py:445
  22.3 4.3 %collective-permute-done.5.refs_6_ = bf16[96,768]{1,0:T(8,128)(2,1)S(1)} collective-permute-done((bf16[96,768]{1,0:T(8,128)(2,1)S(1)}, bf16[96,768]{1,0:T(8,128)(2,1)S(1)}, u32[]{:S(2)}, u32[]{:S(2)}) %collective-permute-start.5) | collective-permute-done | bytes 147488 | tf_op jit(solution)/shard_map/ppermute | solution.py:445
  50.8 6.2 %collective-permute-done.11.refs_2_ = bf16[96,768]{1,0:T(8,128)(2,1)S(1)} collective-permute-done((bf16[96,768]{1,0:T(8,128)(2,1)S(1)}, bf16[96,768]{1,0:T(8,128)(2,1)S(1)}, u32[]{:S(2)}, u32[]{:S(2)}) %collective-permute-start.11) | collective-permute-done | bytes 147488 | tf_op jit(solution)/shard_map/ppermute | solution.py:445
  60.0 3.8 %collective-permute-done.15.refs_6_ = bf16[96,768]{1,0:T(8,128)(2,1)S(1)} collective-permute-done((bf16[96,768]{1,0:T(8,128)(2,1)S(1)}, bf16[96,768]{1,0:T(8,128)(2,1)S(1)}, u32[]{:S(2)}, u32[]{:S(2)}) %collective-permute-start.15) | collective-permute-done | bytes 147488 | tf_op jit(solution)/shard_map/ppermute | solution.py:445
  67.7 3.4 %keyval.3 = (bf16[768,192]{1,0:T(8,128)(2,1)S(1)}, bf16[768,192]{1,0:T(8,128)(2,1)S(1)}, bf16[768,192]{1,0:T(8,128)(2,1)S(1)}, bf16[768,192]{1,0:T(8,128)(2,1)S(...) custom-call(s32[16]{0:T(128)S(1)} %stack.67.tab, bf16[2304,768]{1,0:T(8,128)(2,1)S(1)} %bitcast.27, ...), custom_call_target="tpu_custom_call" | custom-call | flops 1358954496 | bytes 3538944 | tf_op jit(solution)/shard_map/keyval/pallas_call | solution.py:567
  71.1 3.0 %cross_forward.1 = (bf16[256,768]{1,0:T(8,128)(2,1)S(1)}, bf16[256,192]{1,0:T(8,128)(2,1)S(1)}, f32[4,192,576]{2,1,0:T(8,128)S(1)}, bf16[256,192]{1,0:T(8,128)(2...) custom-call(s32[16]{0:T(128)S(1)} %stack.67.tab, s32[4]{0:T(128)S(1)} %copy-done.49, ...), custom_call_target="tpu_custom_call" | custom-call | flops 150994944 | bytes 5505024 | tf_op jit(solution)/shard_map/cross_forward/pallas_call | solution.py:67
  81.8 4.2 %collective-permute-done.22.refs_3_ = bf16[96,1536]{1,0:T(8,128)(2,1)S(1)} collective-permute-done((bf16[96,1536]{1,0:T(8,128)(2,1)S(1)}, bf16[96,1536]{1,0:T(8,128)(2,1)S(1)}, u32[]{:S(2)}, u32[]{:S(2)}) %collective-permute-start.22) | collective-permute-done | bytes 294944 | tf_op jit(solution)/shard_map/ppermute | solution.py:445
  87.5 15.1 %collective-permute-done.21.refs_2_ = bf16[96,1536]{1,0:T(8,128)(2,1)S(1)} collective-permute-done((bf16[96,1536]{1,0:T(8,128)(2,1)S(1)}, bf16[96,1536]{1,0:T(8,128)(2,1)S(1)}, u32[]{:S(2)}, u32[]{:S(2)}) %collective-permute-start.21) | collective-permute-done | bytes 294944 | tf_op jit(solution)/shard_map/ppermute | solution.py:445
  105.6 7.0 %collective-permute-done.25.refs_6_ = bf16[96,1536]{1,0:T(8,128)(2,1)S(1)} collective-permute-done((bf16[96,1536]{1,0:T(8,128)(2,1)S(1)}, bf16[96,1536]{1,0:T(8,128)(2,1)S(1)}, u32[]{:S(2)}, u32[]{:S(2)}) %collective-permute-start.25) | collective-permute-done | bytes 294944 | tf_op jit(solution)/shard_map/ppermute | solution.py:445
  112.5 5.0 %collective-permute-done.24.refs_5_ = bf16[96,1536]{1,0:T(8,128)(2,1)S(1)} collective-permute-done((bf16[96,1536]{1,0:T(8,128)(2,1)S(1)}, bf16[96,1536]{1,0:T(8,128)(2,1)S(1)}, u32[]{:S(2)}, u32[]{:S(2)}) %collective-permute-start.24) | collective-permute-done | bytes 294944 | tf_op jit(solution)/shard_map/ppermute | solution.py:445
  124.4 5.4 %collective-permute-done.31.other = bf16[128,768]{1,0:T(8,128)(2,1)S(1)} collective-permute-done((bf16[128,768]{1,0:T(8,128)(2,1)S(1)}, bf16[128,768]{1,0:T(8,128)(2,1)S(1)}, u32[]{:S(2)}, u32[]{:S(2)}) %collective-permute-start.31) | collective-permute-done | bytes 196640 | tf_op jit(solution)/shard_map/ppermute | solution.py:445
  132.3 3.5 %cross_back.1 = (bf16[256,768]{1,0:T(8,128)(2,1)S(1)}, bf16[256,192]{1,0:T(8,128)(2,1)S(1)}, bf16[2304,192]{1,0:T(8,128)(2,1)S(1)}, bf16[2304,192]{1,0:T(8,128)(...) custom-call(s32[16]{0:T(128)S(1)} %stack.67.tab, bf16[128,768]{1,0:T(8,128)(2,1)S(1)} %get-tuple-element.120.own, ...), custom_call_target="tpu_custom_call" | custom-call | flops 150994944 | bytes 7274496 | tf_op jit(solution)/shard_map/cross_back/pallas_call | solution.py:67
  136.4 4.8 %image_part.1 = (bf16[2304,384]{1,0:T(8,128)(2,1)}, bf16[2304,384]{1,0:T(8,128)(2,1)S(1)}) custom-call(s32[16]{0:T(128)S(1)} %stack.67.tab, bf16[2304,192]{1,0:T(8,128)(2,1)S(1)} %get-tuple-element.140.dk, bf16[2304,192]{1,0:T(8,128)(2,1)S(1)} %get-tuple-element.141.dv, bf16[768,192]{1,0:T(8,128)(2,1)S(1)} %get-tuple-element.142.wk, ...), custom_call_target="tpu_custom_call" | custom-call | flops 1358954496 | bytes 3538944 | tf_op jit(solution)/shard_map/image_part/pallas_call | solution.py:693
  148.4 5.8 %cross_weights.1 = (bf16[4,96,768]{2,1,0:T(8,128)(2,1)S(1)}, bf16[4,96,768]{2,1,0:T(8,128)(2,1)}) custom-call(s32[16]{0:T(128)S(1)} %stack.67.tab, bf16[2304,768]{1,0:T(8,128)(2,1)S(1)} %bitcast.28, bf16[2304,192]{1,0:T(8,128)(2,1)S(1)} %get-tuple-element.140.dk, bf16[2304,192]{1,0:T(8,128)(2,1)S(1)} %get-tuple-element.141.dv, ...), custom_call_target="tpu_custom_call" | custom-call | flops 1358954496 | bytes 3538944 | tf_op jit(solution)/shard_map/cross_weights/pallas_call | solution.py:668
  157.3 3.3 %self_back.1 = (bf16[4,96,768]{2,1,0:T(8,128)(2,1)S(1)}, bf16[4,96,768]{2,1,0:T(8,128)(2,1)S(1)}, bf16[128,768]{1,0:T(8,128)(2,1)S(1)}, bf16[128,768]{1,0:T(8,128)(2,1)S(1)}, f32[8,768]{1,0:T(8,128)S(1)}) custom-call(s32[16]{0:T(128)S(1)} %stack.67.tab, bf16[128,768]{1,0:T(8,128)(2,1)S(1)} %get-tuple-element.126.own, ...), custom_call_target="tpu_custom_call" | custom-call | flops 603979776 | bytes 4555776 | tf_op jit(solution)/shard_map/self_back/pallas_call | solution.py:67
  168.8 6.1 %collective-permute-done.54 = f32[9,768]{1,0:T(8,128)S(1)} collective-permute-done((f32[9,768]{1,0:T(8,128)S(1)}, f32[9,768]{1,0:T(8,128)S(1)}, u32[]{:S(2)}, u32[]{:S(2)}) %collective-permute-start.54) | collective-permute-done | bytes 27680 | tf_op jit(solution)/shard_map/ppermute | solution.py:445
  178.1 7.6 %collective-permute-done.45.other = bf16[4,96,768]{2,1,0:T(8,128)(2,1)} collective-permute-done((bf16[4,96,768]{2,1,0:T(8,128)(2,1)}, bf16[4,96,768]{2,1,0:T(8,128)(2,1)}, u32[]{:S(2)}, u32[]{:S(2)}) %collective-permute-start.45) | collective-permute-done | bytes 589856 | tf_op jit(solution)/shard_map/ppermute | solution.py:445
  189.2 3.0 %image_chip.1 = (bf16[2304,192]{1,0:T(8,128)(2,1)S(1)}, bf16[1152,384]{1,0:T(8,128)(2,1)}) custom-call(bf16[2304,384]{1,0:T(8,128)(2,1)S(1)} %get-tuple-element.144.keep, bf16[2304,384]{1,0:T(8,128)(2,1)} %collective-permute-done.39.other), custom_call_target="tpu_custom_call" | custom-call | bytes 5308416 | tf_op jit(solution)/shard_map/image_chip/pallas_call | solution.py:67
  199.3 3.5 %collective-permute-done.57 = f32[10,768]{1,0:T(8,128)S(1)} collective-permute-done((f32[10,768]{1,0:T(8,128)S(1)}, f32[10,768]{1,0:T(8,128)S(1)}, u32[]{:S(2)}, u32[]{:S(2)}) %collective-permute-start.57) | collective-permute-done | bytes 30752 | tf_op jit(solution)/shard_map/ppermute | solution.py:445
  208.2 6.5 %collective-permute-done.47.refs_2_ = bf16[96,768]{1,0:T(8,128)(2,1)S(1)} collective-permute-done((bf16[96,768]{1,0:T(8,128)(2,1)S(1)}, bf16[96,768]{1,0:T(8,128)(2,1)S(1)}, u32[]{:S(2)}, u32[]{:S(2)}) %collective-permute-start.47) | collective-permute-done | bytes 147488 | tf_op jit(solution)/shard_map/ppermute | solution.py:445
  214.8 2.7 %collective-permute-start.51 = (bf16[96,1536]{1,0:T(8,128)(2,1)S(1)}, bf16[96,1536]{1,0:T(8,128)(2,1)S(1)}, u32[]{:S(2)}, u32[]{:S(2)}) collective-permute-start(bf16[96,1536]{1,0:T(8,128)(2,1)S(1)} %get-tuple-element.176), channel_id=1, source_target_pairs={{0,16},{4,20},{8,24},{12,28},{16,0},{20,4},{24,8},{28,12},{1,17},{... | collective-permute-start | bytes 884744 | tf_op jit(solution)/shard_map/ppermute | solution.py:445
  225.9 15.5 %collective-permute-done.51.refs_2_ = bf16[96,1536]{1,0:T(8,128)(2,1)S(1)} collective-permute-done((bf16[96,1536]{1,0:T(8,128)(2,1)S(1)}, bf16[96,1536]{1,0:T(8,128)(2,1)S(1)}, u32[]{:S(2)}, u32[]{:S(2)}) %collective-permute-start.51) | collective-permute-done | bytes 294944 | tf_op jit(solution)/shard_map/ppermute | solution.py:445
  247.2 6.4 %collective-permute-done.43.refs_2_ = bf16[96,768]{1,0:T(8,128)(2,1)} collective-permute-done((bf16[96,768]{1,0:T(8,128)(2,1)}, bf16[96,768]{1,0:T(8,128)(2,1)}, u32[]{:S(2)}, u32[]{:S(2)}) %collective-permute-start.43) | collective-permute-done | bytes 147488 | tf_op jit(solution)/shard_map/ppermute | solution.py:445
  (256 shorter events, 122.8 us)
Async XLA Ops:
  7.7 14.0 %collective-permute-start = (bf16[96,768]{1,0:T(8,128)(2,1)S(1)}, bf16[96,768]{1,0:T(8,128)(2,1)S(1)}, u32[]{:S(2)}, u32[]{:S(2)}) collective-permute-start(bf16[96,768]{1,0:T(8,128)(2,1)S(1)} %pack_self.1.refs_0_), channel_id=1, source_target_pairs={{0,8},{4,12},{8,0},{12,4},{16,24},{20,28},{24,16},{28,20},{1,9},{5... | collective-permute-start | bytes 442376 | tf_op jit(solution)/shard_map/ppermute | solution.py:445
  8.3 14.0 %collective-permute-start.3 = (bf16[96,768]{1,0:T(8,128)(2,1)S(1)}, bf16[96,768]{1,0:T(8,128)(2,1)S(1)}, u32[]{:S(2)}, u32[]{:S(2)}) collective-permute-start(bf16[96,768]{1,0:T(8,128)(2,1)S(1)} %pack_self.1.refs_0_), channel_id=1, source_target_pairs={{0,4},{4,0},{8,12},{12,8},{16,20},{20,16},{24,28},{28,24},{1,5},{5... | collective-permute-start | bytes 442376 | tf_op jit(solution)/shard_map/ppermute | solution.py:445
  43.1 13.9 %collective-permute-start.11 = (bf16[96,768]{1,0:T(8,128)(2,1)S(1)}, bf16[96,768]{1,0:T(8,128)(2,1)S(1)}, u32[]{:S(2)}, u32[]{:S(2)}) collective-permute-start(bf16[96,768]{1,0:T(8,128)(2,1)S(1)} %get-tuple-element.102.refs_0_), channel_id=1, source_target_pairs={{0,16},{4,20},{8,24},{12,28},{16,0},{20,4},{24,8},{28,12},{1,17},{... | collective-permute-start | bytes 442376 | tf_op jit(solution)/shard_map/ppermute | solution.py:445
  43.3 15.2 %collective-permute-start.10 = (bf16[96,768]{1,0:T(8,128)(2,1)S(1)}, bf16[96,768]{1,0:T(8,128)(2,1)S(1)}, u32[]{:S(2)}, u32[]{:S(2)}) collective-permute-start(bf16[96,768]{1,0:T(8,128)(2,1)S(1)} %get-tuple-element.102.refs_0_), channel_id=1, source_target_pairs={{0,8},{4,12},{8,0},{12,4},{16,24},{20,28},{24,16},{28,20},{1,9},{5... | collective-permute-start | bytes 442376 | tf_op jit(solution)/shard_map/ppermute | solution.py:445
  45.2 13.9 %collective-permute-start.8 = (bf16[128,768]{1,0:T(8,128)(2,1)S(1)}, bf16[128,768]{1,0:T(8,128)(2,1)S(1)}, u32[]{:S(2)}, u32[]{:S(2)}) collective-permute-start(bf16[128,768]{1,0:T(8,128)(2,1)S(1)} %add_convert_fusion.5.chip), channel_id=1, source_target_pairs={{0,2},{1,3},{2,0},{3,1},{4,6},{5,7},{6,4},{7,5},{8,10},{9,11},{10,... | collective-permute-start | bytes 589832 | tf_op jit(solution)/shard_map/ppermute | solution.py:445
  75.8 26.8 %collective-permute-start.21 = (bf16[96,1536]{1,0:T(8,128)(2,1)S(1)}, bf16[96,1536]{1,0:T(8,128)(2,1)S(1)}, u32[]{:S(2)}, u32[]{:S(2)}) collective-permute-start(bf16[96,1536]{1,0:T(8,128)(2,1)S(1)} %get-tuple-element.111.refs_0_), channel_id=1, source_target_pairs={{0,16},{4,20},{8,24},{12,28},{16,0},{20,4},{24,8},{28,12},{1,17},{... | collective-permute-start | bytes 884744 | tf_op jit(solution)/shard_map/ppermute | solution.py:445
  76.3 27.8 %collective-permute-start.20 = (bf16[96,1536]{1,0:T(8,128)(2,1)S(1)}, bf16[96,1536]{1,0:T(8,128)(2,1)S(1)}, u32[]{:S(2)}, u32[]{:S(2)}) collective-permute-start(bf16[96,1536]{1,0:T(8,128)(2,1)S(1)} %get-tuple-element.111.refs_0_), channel_id=1, source_target_pairs={{0,8},{4,12},{8,0},{12,4},{16,24},{20,28},{24,16},{28,20},{1,9},{5... | collective-permute-start | bytes 884744 | tf_op jit(solution)/shard_map/ppermute | solution.py:445
  78.8 25.9 %collective-permute-start.18 = (bf16[128,768]{1,0:T(8,128)(2,1)S(1)}, bf16[128,768]{1,0:T(8,128)(2,1)S(1)}, u32[]{:S(2)}, u32[]{:S(2)}) collective-permute-start(bf16[128,768]{1,0:T(8,128)(2,1)S(1)} %add_convert_fusion.4.chip), channel_id=1, source_target_pairs={{0,2},{1,3},{2,0},{3,1},{4,6},{5,7},{6,4},{7,5},{8,10},{9,11},{10,... | collective-permute-start | bytes 589832 | tf_op jit(solution)/shard_map/ppermute | solution.py:445
  80.3 25.2 %collective-permute-start.23 = (bf16[96,1536]{1,0:T(8,128)(2,1)S(1)}, bf16[96,1536]{1,0:T(8,128)(2,1)S(1)}, u32[]{:S(2)}, u32[]{:S(2)}) collective-permute-start(bf16[96,1536]{1,0:T(8,128)(2,1)S(1)} %get-tuple-element.111.refs_0_), channel_id=1, source_target_pairs={{0,4},{4,0},{8,12},{12,8},{16,20},{20,16},{24,28},{28,24},{1,5},{5... | collective-permute-start | bytes 884744 | tf_op jit(solution)/shard_map/ppermute | solution.py:445
  86.1 19.5 %collective-permute-start.26 = (bf16[96,1536]{1,0:T(8,128)(2,1)S(1)}, bf16[96,1536]{1,0:T(8,128)(2,1)S(1)}, u32[]{:S(2)}, u32[]{:S(2)}) collective-permute-start(bf16[96,1536]{1,0:T(8,128)(2,1)S(1)} %collective-permute-done.22.refs_3_), channel_id=1, source_target_pairs={{0,4},{4,0},{8,12},{12,8},{16,20},{20,16},{24,28},{28,24},{1,5},{5... | collective-permute-start | bytes 884744 | tf_op jit(solution)/shard_map/ppermute | solution.py:445
  104.1 13.4 %collective-permute-start.24 = (bf16[96,1536]{1,0:T(8,128)(2,1)S(1)}, bf16[96,1536]{1,0:T(8,128)(2,1)S(1)}, u32[]{:S(2)}, u32[]{:S(2)}) collective-permute-start(bf16[96,1536]{1,0:T(8,128)(2,1)S(1)} %collective-permute-done.20.refs_1_), channel_id=1, source_target_pairs={{0,4},{4,0},{8,12},{12,8},{16,20},{20,16},{24,28},{28,24},{1,5},{5... | collective-permute-start | bytes 884744 | tf_op jit(solution)/shard_map/ppermute | solution.py:445
  136.1 29.5 %collective-permute-start.27 = (bf16[128,768]{1,0:T(8,128)(2,1)}, bf16[128,768]{1,0:T(8,128)(2,1)}, u32[]{:S(2)}, u32[]{:S(2)}) collective-permute-start(bf16[128,768]{1,0:T(8,128)(2,1)} %get-tuple-element.116), channel_id=1, source_target_pairs={{0,1},{1,0},{2,3},{3,2},{4,5},{5,4},{6,7},{7,6},{8,9},{9,8},{10,11... | collective-permute-start | bytes 589832 | tf_op jit(solution)/shard_map/ppermute | solution.py:445
  141.3 46.3 %collective-permute-start.39 = (bf16[2304,384]{1,0:T(8,128)(2,1)}, bf16[2304,384]{1,0:T(8,128)(2,1)}, u32[]{:S(2)}, u32[]{:S(2)}) collective-permute-start(bf16[2304,384]{1,0:T(8,128)(2,1)} %get-tuple-element.145), channel_id=1, source_target_pairs={{0,1},{1,0},{2,3},{3,2},{4,5},{5,4},{6,7},{7,6},{8,9},{9,8},{10,11... | collective-permute-start | bytes 5308424 | tf_op jit(solution)/shard_map/ppermute | solution.py:445
  144.0 53.8 %collective-permute-start.49 = (bf16[4,96,1536]{2,1,0:T(8,128)(2,1)}, bf16[4,96,1536]{2,1,0:T(8,128)(2,1)}, u32[]{:S(2)}, u32[]{:S(2)}) collective-permute-start(bf16[4,96,1536]{2,1,0:T(8,128)(2,1)} %get-tuple-element.173), channel_id=1, source_target_pairs={{0,4},{4,0},{8,12},{12,8},{16,20},{20,16},{24,28},{28,24},{1,5},{5... | collective-permute-start | bytes 3538952 | tf_op jit(solution)/shard_map/ppermute | solution.py:445
  154.2 31.5 %collective-permute-start.45 = (bf16[4,96,768]{2,1,0:T(8,128)(2,1)}, bf16[4,96,768]{2,1,0:T(8,128)(2,1)}, u32[]{:S(2)}, u32[]{:S(2)}) collective-permute-start(bf16[4,96,768]{2,1,0:T(8,128)(2,1)} %get-tuple-element.161), channel_id=1, source_target_pairs={{0,4},{4,0},{8,12},{12,8},{16,20},{20,16},{24,28},{28,24},{1,5},{5... | collective-permute-start | bytes 1769480 | tf_op jit(solution)/shard_map/ppermute | solution.py:445
  178.0 14.1 %collective-permute-start.29 = (bf16[128,768]{1,0:T(8,128)(2,1)S(1)}, bf16[128,768]{1,0:T(8,128)(2,1)S(1)}, u32[]{:S(2)}, u32[]{:S(2)}) collective-permute-start(bf16[128,768]{1,0:T(8,128)(2,1)S(1)} %layer_out.1.own), channel_id=1, source_target_pairs={{0,1},{1,0},{2,3},{3,2},{4,5},{5,4},{6,7},{7,6},{8,9},{9,8},{10,11... | collective-permute-start | bytes 589832 | tf_op jit(solution)/shard_map/ppermute | solution.py:445
  186.9 17.4 %collective-permute-start.46 = (bf16[96,768]{1,0:T(8,128)(2,1)S(1)}, bf16[96,768]{1,0:T(8,128)(2,1)S(1)}, u32[]{:S(2)}, u32[]{:S(2)}) collective-permute-start(bf16[96,768]{1,0:T(8,128)(2,1)S(1)} %get-tuple-element.163), channel_id=1, source_target_pairs={{0,8},{4,12},{8,0},{12,4},{16,24},{20,28},{24,16},{28,20},{1,9},{5... | collective-permute-start | bytes 442376 | tf_op jit(solution)/shard_map/ppermute | solution.py:445
  187.6 34.3 %collective-permute-start.41 = (bf16[4,96,768]{2,1,0:T(8,128)(2,1)S(1)}, bf16[4,96,768]{2,1,0:T(8,128)(2,1)S(1)}, u32[]{:S(2)}, u32[]{:S(2)}) collective-permute-start(bf16[4,96,768]{2,1,0:T(8,128)(2,1)S(1)} %copy-done.51), channel_id=1, source_target_pairs={{0,4},{4,0},{8,12},{12,8},{16,20},{20,16},{24,28},{28,24},{1,5},{5... | collective-permute-start | bytes 1769480 | tf_op jit(solution)/shard_map/ppermute | solution.py:445
  193.6 63.4 %collective-permute-start.40 = (bf16[1152,384]{1,0:T(8,128)(2,1)}, bf16[1152,384]{1,0:T(8,128)(2,1)S(1)}, u32[]{:S(2)}, u32[]{:S(2)}) collective-permute-start(bf16[1152,384]{1,0:T(8,128)(2,1)} %get-tuple-element.147), channel_id=1, source_target_pairs={{0,2},{1,3},{2,0},{3,1},{4,6},{5,7},{6,4},{7,5},{8,10},{9,11},{10,... | collective-permute-start | bytes 2654216 | tf_op jit(solution)/shard_map/ppermute | solution.py:445
  196.2 23.3 %collective-permute-start.37 = (bf16[128,768]{1,0:T(8,128)(2,1)S(1)}, bf16[128,768]{1,0:T(8,128)(2,1)S(1)}, u32[]{:S(2)}, u32[]{:S(2)}) collective-permute-start(bf16[128,768]{1,0:T(8,128)(2,1)S(1)} %add_convert_fusion.chip), channel_id=1, source_target_pairs={{0,2},{1,3},{2,0},{3,1},{4,6},{5,7},{6,4},{7,5},{8,10},{9,11},{10,... | collective-permute-start | bytes 589832 | tf_op jit(solution)/shard_map/ppermute | solution.py:445
  214.8 26.7 %collective-permute-start.51 = (bf16[96,1536]{1,0:T(8,128)(2,1)S(1)}, bf16[96,1536]{1,0:T(8,128)(2,1)S(1)}, u32[]{:S(2)}, u32[]{:S(2)}) collective-permute-start(bf16[96,1536]{1,0:T(8,128)(2,1)S(1)} %get-tuple-element.176), channel_id=1, source_target_pairs={{0,16},{4,20},{8,24},{12,28},{16,0},{20,4},{24,8},{28,12},{1,17},{... | collective-permute-start | bytes 884744 | tf_op jit(solution)/shard_map/ppermute | solution.py:445
  219.5 22.0 %collective-permute-start.52 = (bf16[96,1536]{1,0:T(8,128)(2,1)S(1)}, bf16[96,1536]{1,0:T(8,128)(2,1)S(1)}, u32[]{:S(2)}, u32[]{:S(2)}) collective-permute-start(bf16[96,1536]{1,0:T(8,128)(2,1)S(1)} %get-tuple-element.177), channel_id=1, source_target_pairs={{0,24},{4,28},{8,16},{12,20},{16,8},{20,12},{24,0},{28,4},{1,25},{... | collective-permute-start | bytes 884744 | tf_op jit(solution)/shard_map/ppermute | solution.py:445
  221.9 33.5 %collective-permute-start.38 = (f32[128,768]{1,0:T(8,128)S(1)}, f32[128,768]{1,0:T(8,128)S(1)}, u32[]{:S(2)}, u32[]{:S(2)}) collective-permute-start(f32[128,768]{1,0:T(8,128)S(1)} %text_grad.1.own), channel_id=1, source_target_pairs={{0,1},{1,0},{2,3},{3,2},{4,5},{5,4},{6,7},{7,6},{8,9},{9,8},{10,11... | collective-permute-start | bytes 1179656 | tf_op jit(solution)/shard_map/ppermute | solution.py:445
  225.9 21.3 %collective-permute-start.42 = (bf16[96,768]{1,0:T(8,128)(2,1)}, bf16[96,768]{1,0:T(8,128)(2,1)S(1)}, u32[]{:S(2)}, u32[]{:S(2)}) collective-permute-start(bf16[96,768]{1,0:T(8,128)(2,1)} %get-tuple-element.151), channel_id=1, source_target_pairs={{0,8},{4,12},{8,0},{12,4},{16,24},{20,28},{24,16},{28,20},{1,9},{5... | collective-permute-start | bytes 442376 | tf_op jit(solution)/shard_map/ppermute | solution.py:445
  (90 other events, 890.5 us)

commit v2 on v1

v2 whole, which is shorter than its diff:
```python
import functools
import math

import jax
import jax.numpy as jnp
from jax import lax
from jax.experimental import pallas as pl
from jax.experimental.pallas import tpu as pltpu
from jax.sharding import PartitionSpec as P

BF = jnp.bfloat16
F32 = jnp.float32
HEAD_DIM = 64
SCALE = HEAD_DIM ** (-0.5)
NORM_EPS = 1e-05
NEG_FILL = -1e30
INV_ROOT_TWO = 1.0 / math.sqrt(2.0)
INV_ROOT_TAU = 1.0 / math.sqrt(2.0 * math.pi)
VMEM_LIMIT = 24 * 1024 * 1024
COST_PER_BYTE = 1
COST = pl.CostEstimate(flops=1, bytes_accessed=10**7, transcendentals=0)


def nn(a, b):
    return lax.dot_general(a, b, (((1,), (0,)), ((), ())), preferred_element_type=F32)


def nt(a, b):
    return lax.dot_general(a, b, (((1,), (1,)), ((), ())), preferred_element_type=F32)


def tn(a, b):
    return lax.dot_general(a, b, (((0,), (0,)), ((), ())), preferred_element_type=F32)


def norm_parts(values):
    centered = values - jnp.mean(values, axis=-1, keepdims=True)
    inv_std = lax.rsqrt(jnp.mean(centered * centered, axis=-1, keepdims=True) + NORM_EPS)
    return centered * inv_std, inv_std


def norm_back(grad, normed, inv_std, gain_row):
    scaled = grad * gain_row
    first = jnp.mean(scaled, axis=-1, keepdims=True)
    second = jnp.mean(scaled * normed, axis=-1, keepdims=True)
    return inv_std * (scaled - first - normed * second)


def head_masks(width, kind):
    column = lax.broadcasted_iota(jnp.int32, (1, width), 1) // HEAD_DIM
    return [(column == h).astype(F32).astype(kind) for h in range(width // HEAD_DIM)]


def stack_heads(rows, masks):
    return jnp.concatenate([rows * m for m in masks], axis=0)


def unstack_heads(stacked, masks):
    count = stacked.shape[0] // len(masks)
    total = stacked[:count] * masks[0]
    for h in range(1, len(masks)):
        total = total + stacked[h * count : (h + 1) * count] * masks[h]
    return total


def call(body, name, outs, scalars, arrays, scratch=(), flops=0):
    nbytes = sum(a.size * a.dtype.itemsize for a in arrays)
    nbytes += sum(math.prod(s) * jnp.dtype(d).itemsize for s, d in outs)
    return pl.pallas_call(
        body,
        out_shape=[jax.ShapeDtypeStruct(s, d) for s, d in outs],
        in_specs=[pl.BlockSpec(memory_space=pltpu.SMEM)] * len(scalars)
        + [pl.BlockSpec(memory_space=pltpu.VMEM)] * len(arrays),
        out_specs=[pl.BlockSpec(memory_space=pltpu.VMEM)] * len(outs),
        scratch_shapes=list(scratch),
        compiler_params=pltpu.CompilerParams(vmem_limit_bytes=VMEM_LIMIT),
        cost_estimate=pl.CostEstimate(
            flops=1, bytes_accessed=int(nbytes * COST_PER_BYTE) + 1, transcendentals=0
        ),
        name=name,
    )(*scalars, *arrays)


def turns_of(one, two, three):
    return [a ^ b ^ c for a in (0, one) for c in (0, three) for b in (0, two)]


X_FIRST = (1, 2, 4)
Z_FIRST = (2, 4, 1)


def block_rows(turn, height):
    at = (lax.axis_index("dp") ^ turn) * height
    return pl.ds(pl.multiple_of(at, 32), height)


def half_rows(height, away=False):
    core = lax.axis_index("mp") & 1
    at = (1 - core if away else core) * height
    return pl.ds(pl.multiple_of(at, 128), height)


def ring_rows(hops, height):
    index = lax.axis_index("dp")
    spot = jnp.where((index & 1) == 0, index >> 1, 7 - (index >> 1))
    spot = (spot + hops + 8) & 7
    at = jnp.where(spot < 4, 2 * spot, 15 - 2 * spot) * height
    return pl.ds(pl.multiple_of(at, 32), height)


def place_pieces(pieces, targets):
    if len(pieces) == 1:
        blocks = [(slice(None), pieces[0])]
    else:
        height = pieces[0].shape[0]
        side = 2 * (lax.axis_index("mp") & 1) - 1
        blocks = [(ring_rows(0, height), pieces[0]), (ring_rows(4, height), pieces[7])]
        for k in (1, 2, 3):
            blocks.append((ring_rows(side * k, height), pieces[k].at[0]))
            blocks.append((ring_rows(-side * k, height), pieces[3 + k].at[1]))
    for rows, piece in blocks:
        start = 0
        for target in targets:
            width = target.shape[1]
            target[rows, :] = piece[:, start : start + width]
            start += width


def join_halves(own, other, target):
    half = own.shape[0]
    target[half_rows(half), :] = own[...]
    target[half_rows(half, True), :] = other[...]


def split_halves(full, send, keep):
    half = full.shape[0] // 2
    keep[:half] = full[half_rows(half), :].astype(keep.dtype)
    send[:half] = full[half_rows(half, True), :].astype(send.dtype)


def pack_self_kernel(qkv, out, packed):
    width = qkv.shape[2]
    for j in range(3):
        packed[:, j * width : (j + 1) * width] = qkv[j]
    packed[:, 3 * width :] = out[...].astype(F32).T.astype(BF)


def pack_cross_kernel(query, keyval, out, cross):
    width = query.shape[1]
    cross[:, :width] = query[...]
    cross[:, width : 2 * width] = keyval[0]
    cross[:, 2 * width : 3 * width] = keyval[1]
    cross[:, 3 * width :] = out[...].astype(F32).T.astype(BF)


def pack_ffn_kernel(up, down, ffn):
    hidden = up.shape[1]
    ffn[:, :hidden] = up[...]
    ffn[:, hidden:] = down[...]


def pair_kernel(own, other, out):
    out[0] = own[...]
    out[1] = other[...]


def take_kernel(pair, out):
    out[...] = pair[0]


def self_forward_kernel(
    count, seqs, lens, text, gain, bias, *refs
):
    pieces, (weights, saved, send, keep, w, qkv, full, sems) = refs[:count], refs[count:]
    place_pieces(pieces, (w,))
    save_w = pltpu.make_async_copy(w, weights, sems.at[0])
    save_w.start()
    n, _ = norm_parts(text[...].astype(F32))
    low = (n * gain[0:1] + bias[0:1]).astype(BF)
    width = w.shape[1] // 4
    qkv[:, : 3 * width] = nn(low, w[:, : 3 * width]).astype(BF)
    low_masks, masks = head_masks(width, BF), head_masks(width, F32)
    rows = text.shape[0] // seqs
    for b in range(seqs):
        at = slice(b * rows, (b + 1) * rows)
        q_stack = stack_heads(qkv[at, :width], low_masks)
        p = self_softmax(q_stack, qkv[at, width : 2 * width], lens[b], rows)
        qkv[at, 3 * width :] = unstack_heads(
            nn(p.astype(BF), qkv[at, 2 * width : 3 * width]), masks
        ).astype(BF)
    save_q = pltpu.make_async_copy(qkv, saved, sems.at[1])
    save_q.start()
    full[...] = nt(qkv[:, 3 * width :], w[:, 3 * width :])
    split_halves(full, send, keep)
    save_w.wait()
    save_q.wait()


def self_softmax(q_stack, keys, length, rows):
    shape = (q_stack.shape[0], rows)
    query_at = lax.broadcasted_iota(jnp.int32, shape, 0) % rows
    key_at = lax.broadcasted_iota(jnp.int32, shape, 1)
    allowed = (key_at <= query_at) & (key_at < length)
    scores = jnp.where(allowed, nt(q_stack, keys) * SCALE, NEG_FILL)
    raised = jnp.exp(scores - jnp.max(scores, axis=-1, keepdims=True))
    return raised / jnp.sum(raised, axis=-1, keepdims=True)


def keyval_kernel(count, image, *refs):
    pieces, (wq, wk, wv, wo, keys, values) = refs[:count], refs[count:]

    @pl.when(pl.program_id(0) == 0)
    def _():
        place_pieces(pieces, (wq, wk, wv, wo))

    keys[...] = nn(image[...], wk[...]).astype(BF)
    values[...] = nn(image[...], wv[...]).astype(BF)


def norm_kernel(index, sliced, chip, other, resid, out_bias, gain, bias, hidden, normed):
    half = chip.shape[0]
    if sliced:
        base = resid[half_rows(half), :].astype(F32)
    else:
        base = resid[...]
    value = (
        base
        + (chip[...].astype(F32) + other[...].astype(F32))
        + out_bias[index : index + 1]
    )
    hidden[...] = value
    n, _ = norm_parts(value)
    normed[...] = (n * gain[index + 1 : index + 2] + bias[index + 1 : index + 2]).astype(BF)


def cross_forward_kernel(
    seqs, counts, own, other, wq, wo, keys, values, normed, q, prob, ctx, send, keep, full
):
    join_halves(own, other, normed)
    q[...] = nn(normed[...], wq[...]).astype(BF)
    width = q.shape[1]
    low_masks, masks = head_masks(width, BF), head_masks(width, F32)
    rows = normed.shape[0] // seqs
    patches = keys.shape[0] // seqs
    patch_at = lax.broadcasted_iota(jnp.int32, (rows * len(masks), patches), 1)
    for b in range(seqs):
        at = slice(b * rows, (b + 1) * rows)
        ks = slice(b * patches, (b + 1) * patches)
        scores = nt(stack_heads(q[at], low_masks), keys[ks]) * SCALE
        scores = jnp.where(patch_at < counts[b], scores, NEG_FILL)
        raised = jnp.exp(scores - jnp.max(scores, axis=-1, keepdims=True))
        p = raised / jnp.sum(raised, axis=-1, keepdims=True)
        prob[b] = p
        ctx[at] = unstack_heads(nn(p.astype(BF), values[ks]), masks).astype(BF)
    full[...] = nt(ctx[...], wo[...])
    split_halves(full, send, keep)


def ffn_ready_kernel(count, grad, *refs):
    pieces, (up, down, grad_act) = refs[:count], refs[count:]
    place_pieces(pieces, (up, down))
    grad_act[...] = nn(grad[...], down[...])


def ffn_kernel(
    own, other, up, down, grad_act, up_bias,
    normed, act, grad_low, bias_sum, send, keep, out_send, out_keep, full,
):
    join_halves(own, other, normed)
    pre = nn(normed[...], up[...]) + up_bias[...]
    cdf = 0.5 * (1.0 + lax.erf(pre * INV_ROOT_TWO))
    density = jnp.exp(-0.5 * pre * pre) * INV_ROOT_TAU
    grad_pre = grad_act[...] * (cdf + pre * density)
    grad_low[...] = grad_pre.astype(BF)
    act[...] = (pre * cdf).astype(BF)
    bias_sum[...] = jnp.sum(grad_pre, axis=0, keepdims=True)
    full[...] = nt(grad_low[...], up[...])
    split_halves(full, send, keep)
    full[...] = nt(act[...], down[...])
    split_halves(full, out_send, out_keep)


def scatter_blocks(matrix, column, outs, order=X_FIRST):
    blocks = sum(o.shape[0] for o in outs)
    height = outs[0].shape[1]
    width = matrix.shape[1]
    turns = turns_of(*order)
    for k in range(blocks):
        rows = block_rows(turns[k], height) if blocks > 1 else slice(None)
        target = outs[k // outs[0].shape[0]]
        target[k % outs[0].shape[0], :, column : column + width] = matrix[rows, :].astype(BF)


def ffn_weight_kernel(parts, normed, grad_low, grad, act, *refs):
    ups, downs, full = refs[:parts], refs[parts : 2 * parts], refs[2 * parts]
    full[...] = tn(normed[...], grad_low[...])
    scatter_blocks(full, 0, ups, Z_FIRST)
    full[...] = tn(grad[...], act[...])
    scatter_blocks(full, 0, downs)


def norm_back_kernel(index, sliced, chip, other, hidden, resid, gain, total, low, vec):
    half = chip.shape[0]
    if sliced:
        base = resid[half_rows(half), :].astype(F32)
    else:
        base = resid[...]
    grad = chip[...].astype(F32) + other[...].astype(F32)
    n, inv_std = norm_parts(hidden[...])
    value = base + norm_back(grad, n, inv_std, gain[index : index + 1])
    total[...] = value
    low[...] = value.astype(BF)
    vec[...] = jnp.zeros_like(vec)
    vec[0:1] = 0.5 * jnp.sum(grad * n, axis=0, keepdims=True)
    vec[1:2] = 0.5 * jnp.sum(grad, axis=0, keepdims=True)
    vec[2:3] = 0.5 * jnp.sum(value, axis=0, keepdims=True)
    if sliced:
        vec[3:4] = 0.5 * jnp.sum(base, axis=0, keepdims=True)


def score_grad(p, values, grad_stack):
    grad_p = nt(grad_stack, values)
    inner = jnp.sum(p * grad_p, axis=-1, keepdims=True)
    return (p * (grad_p - inner)).astype(BF)


def cross_back_kernel(
    seqs, own, other, wq, wo, keys, values, q, prob, grad_two, dq, dkt, dvt, send, keep, full
):
    join_halves(own, other, grad_two)
    grad_ctx = nn(grad_two[...], wo[...]).astype(BF)
    width = q.shape[1]
    low_masks, masks = head_masks(width, BF), head_masks(width, F32)
    rows = q.shape[0] // seqs
    patches = keys.shape[0] // seqs
    for b in range(seqs):
        at = slice(b * rows, (b + 1) * rows)
        ks = slice(b * patches, (b + 1) * patches)
        p = prob[b]
        q_stack = stack_heads(q[at], low_masks)
        grad_stack = stack_heads(grad_ctx[at], low_masks)
        ds = score_grad(p, values[ks], grad_stack)
        dq[at] = unstack_heads(nn(ds, keys[ks]) * SCALE, masks).astype(BF)
        dkt[:, ks] = (tn(q_stack, ds) * SCALE).astype(BF)
        dvt[:, ks] = tn(grad_stack, p.astype(BF)).astype(BF)
    full[...] = nt(dq[...], wq[...])
    split_halves(full, send, keep)


def cross_weight_kernel(parts, image, dkt, dvt, normed, dq, grad_two, ctx, *refs):
    outs, turned = refs[:parts], refs[parts]
    width = dq.shape[1]
    turned[...] = tn(normed[...], dq[...])
    scatter_blocks(turned, 0, outs)
    turned[...] = nn(dkt[...], image[...]).T
    scatter_blocks(turned, width, outs)
    turned[...] = nn(dvt[...], image[...]).T
    scatter_blocks(turned, 2 * width, outs)
    turned[...] = tn(grad_two[...], ctx[...])
    scatter_blocks(turned, 3 * width, outs)


def image_part_kernel(dkt, dvt, wk, wv, send_away, send_own, keep_away, keep_own):
    width = wk.shape[1]
    for k, target in enumerate((keep_own, keep_away, send_own, send_away)):
        core, level = lax.axis_index("mp") & 1, lax.axis_index("mp") >> 1
        at = (2 * (level ^ (k & 1)) + (core ^ (k >> 1))) * width
        rows = pl.ds(pl.multiple_of(at, 64), width)
        target[...] = (nn(wk[rows, :], dkt[...]) + nn(wv[rows, :], dvt[...])).astype(BF)


def add_pair_kernel(one, two, out):
    out[...] = (one[...].astype(F32) + two[...].astype(F32)).astype(BF)


def image_chip_kernel(keep_own, own, keep_away, away, out_own, out_away):
    out_own[...] = keep_own[...].astype(F32) + own[...].astype(F32)
    out_away[...] = (keep_away[...].astype(F32) + away[...].astype(F32)).astype(BF)


def image_sum_kernel(own, away, out):
    patches = out.shape[2]
    for b in range(out.shape[0]):
        ks = slice(b * patches, (b + 1) * patches)
        out[b] = own[:, ks] + away[:, ks].astype(F32)


def self_back_kernel(
    seqs, parts, lens, own, other, text, gain, bias, w, qkv,
    out_send, out_keep, one, two, ups, *refs
):
    outs = refs[:parts]
    send, keep, low, dqkv, full, narrow, vec = refs[parts:]
    join_halves(own, other, low)
    width = w.shape[1] // 4
    grad_ctx = nn(low[...], w[:, 3 * width :]).astype(BF)
    low_masks, masks = head_masks(width, BF), head_masks(width, F32)
    rows = text.shape[0] // seqs
    for b in range(seqs):
        at = slice(b * rows, (b + 1) * rows)
        q_stack = stack_heads(qkv[at, :width], low_masks)
        keys = qkv[at, width : 2 * width]
        p = self_softmax(q_stack, keys, lens[b], rows)
        grad_stack = stack_heads(grad_ctx[at], low_masks)
        ds = score_grad(p, qkv[at, 2 * width : 3 * width], grad_stack)
        dqkv[0, at] = unstack_heads(nn(ds, keys) * SCALE, masks).astype(BF)
        dqkv[1, at] = (tn(ds, q_stack) * SCALE).astype(BF)
        dqkv[2, at] = tn(p.astype(BF), grad_stack).astype(BF)
    n, _ = norm_parts(text[...].astype(F32))
    normed = (n * gain[0:1] + bias[0:1]).astype(BF)
    for j in range(3):
        narrow[...] = tn(normed, dqkv[j])
        scatter_blocks(narrow, j * width, outs)
    narrow[...] = tn(low[...], qkv[:, 3 * width :])
    scatter_blocks(narrow, 3 * width, outs)
    part = nt(dqkv[0], w[:, :width])
    for j in (1, 2):
        part = part + nt(dqkv[j], w[:, j * width : (j + 1) * width])
    full[...] = part
    split_halves(full, send, keep)
    half = own.shape[0]
    send[half : 2 * half] = out_send[...]
    keep[half : 2 * half] = out_keep[...]
    vec[...] = jnp.zeros_like(vec)
    vec[0:1] = jnp.sum(part * n, axis=0, keepdims=True)
    vec[1:2], vec[2:3] = one[0:1], two[0:1]
    vec[3:4] = jnp.sum(part, axis=0, keepdims=True)
    vec[4:5], vec[5:6] = one[1:2], two[1:2]
    vec[6:7], vec[7:8], vec[8:9] = one[2:3], two[2:3], two[3:4]
    vec[pl.ds(9 + lax.axis_index("mp"), 1), :] = ups[...]
    send[2 * half :] = vec[...].astype(BF)
    keep[2 * half :] = vec[...].astype(BF)


def finish_kernel(chip, other, text, resid, gain, hidden, out_bias, grad_out, layer_out, vec):
    half = resid.shape[0]
    grad = chip[:half].astype(F32) + other[:half].astype(F32)
    base = text[half_rows(half), :].astype(F32)
    n, inv_std = norm_parts(base)
    grad_out[...] = resid[...] + norm_back(grad, n, inv_std, gain[0:1])
    mid = slice(half, 2 * half)
    layer_out[...] = (
        hidden[...] + (chip[mid].astype(F32) + other[mid].astype(F32)) + out_bias[2:3]
    ).astype(BF)
    vec[...] = (chip[2 * half :].astype(F32) + other[2 * half :].astype(F32)).astype(BF)


def join_both_kernel(own, other, own_low, other_low, out, out_low):
    join_halves(own, other, out)
    join_halves(own_low, other_low, out_low)


def fold_kernel(keep, other, stay, send):
    for k in range(keep.shape[0]):
        target = send if k % 2 else stay
        value = (keep[k].astype(F32) + other[k].astype(F32)).astype(target.dtype)
        if len(target.shape) == 3:
            target[k // 2] = value
        else:
            target[...] = value


def fold_self_one_kernel(keep, other, vec, vec_other, stay, send, vec_sum):
    height = keep.shape[1]
    for k in range(4):
        value = (keep[k].astype(F32) + other[k].astype(F32)).astype(BF)
        at = (k // 2) * height
        (send if k % 2 else stay)[at : at + height] = value
    total = (vec[...].astype(F32) + vec_other[...].astype(F32)).astype(BF)
    vec_sum[...] = total
    send[2 * height :] = total


def fold_self_two_kernel(keep, other, vec, stay, send, vec_sum):
    height = stay.shape[0]
    stay[...] = keep[:height].astype(F32) + other[:height].astype(F32)
    rest = slice(height, 2 * height)
    send[:height] = (keep[rest].astype(F32) + other[rest].astype(F32)).astype(BF)
    total = (vec[...].astype(F32) + other[2 * height :].astype(F32)).astype(BF)
    vec_sum[...] = total
    send[height:] = total


def vector_parts(total, gains, shifts, biases, ups):
    gains[...] = total[0:3]
    shifts[...] = total[3:6]
    biases[...] = total[6:9]
    full = total[9]
    for k in range(1, 4):
        full = jnp.where(lax.axis_index("mp") == k, total[9 + k], full)
    ups[...] = full


def vector_kernel(vec, gains, shifts, biases, ups):
    vector_parts(vec[...], gains, shifts, biases, ups)


def close_cross_kernel(*refs):
    own, other, query, keyval, out = refs
    total = own[...] + other[...].astype(F32)
    width = out.shape[0]
    query[...] = total[:, :width]
    keyval[0] = total[:, width : 2 * width]
    keyval[1] = total[:, 2 * width : 3 * width]
    out[...] = total[:, 3 * width :].T


def close_ffn_kernel(own, other, out):
    out[...] = own[...] + other[...].astype(F32)


def close_self_kernel(own, other, vec, qkv, out, gains, shifts, biases, ups):
    height = own.shape[0]
    total = own[...] + other[:height].astype(F32)
    width = out.shape[0]
    for j in range(3):
        qkv[j] = total[:, j * width : (j + 1) * width]
    out[...] = total[:, 3 * width :].T
    vector_parts(vec[...].astype(F32) + other[height:].astype(F32), gains, shifts, biases, ups)


def swap(value, axis, size, bits):
    return lax.ppermute(value, axis, [(i, i ^ bits) for i in range(size)])


def gate_all(values, *first):
    return list(lax.optimization_barrier((*values, *first)))[: len(values)]


def gate(value, *first):
    return lax.optimization_barrier((value, *first))[0]


def per_device(
    dp_size,
    mp_size,
    text_tokens,
    image_tokens,
    text_lengths,
    patch_counts,
    self_qkv,
    self_out,
    cross_query,
    cross_keyval,
    cross_out,
    mlp_up,
    mlp_down,
    norm_gain,
    norm_bias,
    out_bias,
    up_bias,
    out_grad,
):
    seqs, positions, model = text_tokens.shape
    patches = image_tokens.shape[1]
    rows = seqs * positions
    half = rows // 2
    width = cross_query.shape[1]
    hidden = mlp_up.shape[1]
    image_rows = seqs * patches
    quick = dp_size == 8
    height = model // dp_size
    parts, blocks = (2, (4, height)) if quick else (1, (1, model))

    spots = [0, 2, 4, 6, 7, 5, 3, 1]
    turns = [
        (spots[p] * mp_size + m, spots[(p + (1 if m % 2 == 0 else -1)) % 8] * mp_size + m)
        for p in range(8)
        for m in range(mp_size)
    ]

    def around(value):
        return lax.ppermute(value, ("dp", "mp"), turns)

    def pair_up(shard, name):
        return call(
            pair_kernel, name, [((2,) + shard.shape, BF)], (), (shard, core_swap(shard))
        )[0]

    def last_hop(pair, name):
        (own,) = call(take_kernel, name, [(pair.shape[1:], BF)], (), (pair,))
        return around(own)

    def collect(shard, hops, swaps=None):
        swaps = swaps or [core_swap(hop) for hop in hops[:3]]
        return [shard] + hops[:3] + swaps + [hops[3]]

    def send_blocks(outs, bits):
        return (outs[0], swap(outs[1], "dp", 8, bits)) if quick else outs

    def fold(halves, bits, name, *first):
        if not quick:
            return halves
        keep, other = halves
        count, shape = keep.shape[0] // 2, keep.shape[1:]
        kinds = [((2,) + shape, BF)] * 2 if count == 2 else [(shape, F32), (shape, BF)]
        stay, send = call(fold_kernel, name, kinds, (), (gate(keep, *first), other))
        return stay, swap(send, "dp", 8, bits)

    def whole_sum(halves):
        return lax.psum_scatter(halves[0][0], "dp", scatter_dimension=0, tiled=True).astype(F32)

    def core_swap(value):
        return swap(value, "mp", mp_size, 1)

    def level_swap(value):
        return swap(value, "mp", mp_size, 2)

    def add_pair(one, two):
        return call(add_pair_kernel, "add_pair", [(one.shape, BF)], (), (one, two))[0]

    def mp_sum(send, keep):
        chip = add_pair(keep, core_swap(send))
        return chip, level_swap(chip)

    text = text_tokens.reshape(rows, model)
    image = image_tokens.reshape(image_rows, model)
    grad = out_grad.reshape(rows, model)

    if quick:
        (self_shard,) = call(
            pack_self_kernel, "pack_self", [((height, 4 * width), BF)], (), (self_qkv, self_out)
        )
        (cross_shard,) = call(
            pack_cross_kernel,
            "pack_cross",
            [((height, 4 * width), BF)],
            (),
            (cross_query, cross_keyval, cross_out),
        )
        (ffn_shard,) = call(
            pack_ffn_kernel, "pack_ffn", [((height, 2 * hidden), BF)], (), (mlp_up, mlp_down.T)
        )
        self_pair = pair_up(self_shard, "pairA")
        self_hops = [around(self_pair)]
        cross_hops = [around(pair_up(gate(cross_shard, self_pair), "pairB"))]
        for k in range(2):
            self_hops.append(around(self_hops[-1]))
            cross_hops.append(around(cross_hops[-1]))
        self_hops.append(last_hop(self_hops[-1], "takeA"))
        cross_hops.append(last_hop(cross_hops[-1], "takeB"))
        self_swaps = [core_swap(hop) for hop in self_hops[:3]]
        self_pieces = collect(self_shard, self_hops, self_swaps)
        cross_pieces = collect(cross_shard, cross_hops)
        ffn_pair = pair_up(gate(ffn_shard, self_hops[0]), "pairF")
        ffn_hops = [around(gate(ffn_pair, cross_hops[1]))]
        ffn_hops.append(around(ffn_hops[0]))
        text_in = gate(text, ffn_hops[0], cross_hops[2])
    else:
        gather = lambda shard: [lax.all_gather(shard, "dp", axis=0, tiled=True)]
        self_pieces = gather(
            jnp.concatenate([self_qkv[0], self_qkv[1], self_qkv[2], self_out.T], 1)
        )
        cross_pieces = gather(
            jnp.concatenate([cross_query, cross_keyval[0], cross_keyval[1], cross_out.T], 1)
        )
        text_in = text
        ffn_pieces = gather(jnp.concatenate([mlp_up, mlp_down.T], 1))

    square = ((model, width), BF)
    narrow = ((rows, width), BF)
    wide = ((rows, model), BF)
    halves = [((half, model), BF)] * 2
    half_f32 = ((half, model), F32)
    half_low = ((half, model), BF)
    heads = width // HEAD_DIM
    full = pltpu.VMEM((rows, model), F32)

    vmem = pl.BlockSpec(memory_space=pltpu.VMEM)
    smem = pl.BlockSpec(memory_space=pltpu.SMEM)
    hbm = pl.BlockSpec(memory_space=pltpu.HBM)
    w_self, saved, send, keep = pl.pallas_call(
        functools.partial(self_forward_kernel, len(self_pieces), seqs),
        out_shape=[
            jax.ShapeDtypeStruct((model, 4 * width), BF),
            jax.ShapeDtypeStruct((rows, 4 * width), BF),
            jax.ShapeDtypeStruct((half, model), BF),
            jax.ShapeDtypeStruct((half, model), BF),
        ],
        in_specs=[smem] + [vmem] * (3 + len(self_pieces)),
        out_specs=[hbm, hbm, vmem, vmem],
        scratch_shapes=[
            pltpu.VMEM((model, 4 * width), BF),
            pltpu.VMEM((rows, 4 * width), BF),
            full,
            pltpu.SemaphoreType.DMA((2,)),
        ],
        compiler_params=pltpu.CompilerParams(vmem_limit_bytes=VMEM_LIMIT),
        cost_estimate=COST,
        name="self_forward",
    )(text_lengths, text_in, norm_gain, norm_bias, *self_pieces)
    chip, other = mp_sum(send, keep)

    whole = lambda shape: pl.BlockSpec(shape, lambda b: (0,) * len(shape))
    per_seq = lambda b: (b, 0)
    cq, ck, cv, co, keys, values = pl.pallas_call(
        functools.partial(keyval_kernel, len(cross_pieces)),
        grid=(seqs,),
        out_shape=[jax.ShapeDtypeStruct((model, width), BF)] * 4
        + [jax.ShapeDtypeStruct((image_rows, width), BF)] * 2,
        in_specs=[pl.BlockSpec((patches, model), per_seq)]
        + [whole(piece.shape) for piece in cross_pieces],
        out_specs=[whole((model, width))] * 4 + [pl.BlockSpec((patches, width), per_seq)] * 2,
        compiler_params=pltpu.CompilerParams(vmem_limit_bytes=VMEM_LIMIT),
        cost_estimate=COST,
        name="keyval",
    )(image, *cross_pieces)

    hidden_one, normed_half = call(
        functools.partial(norm_kernel, 0, True),
        "norm_mid",
        [half_f32, half_low],
        (),
        (gate(chip, keys, ffn_hops[1]) if quick else chip, other, text, out_bias, norm_gain, norm_bias),
    )
    if quick:
        ffn_hops.append(around(gate(ffn_hops[1], normed_half)))
    normed_mid, xq, cross_prob, cross_ctx, send, keep = call(
        functools.partial(cross_forward_kernel, seqs),
        "cross_forward",
        [wide, narrow, ((seqs, heads * positions, patches), F32), narrow] + halves,
        (patch_counts,),
        (normed_half, core_swap(normed_half), cq, co, keys, values),
        [full],
        flops=2 * rows * model * width * 2,
    )
    chip, other = mp_sum(send, keep)
    if quick:
        ffn_hops.append(last_hop(gate(ffn_hops[2], chip), "takeF"))
        ffn_pieces = collect(ffn_shard, ffn_hops)
    w_up, w_down, grad_act = call(
        functools.partial(ffn_ready_kernel, len(ffn_pieces)),
        "ffn_ready",
        [((model, hidden), BF)] * 2 + [((rows, hidden), F32)],
        (),
        (grad, *ffn_pieces),
        flops=2 * rows * model * hidden,
    )
    hidden_two, normed_half = call(
        functools.partial(norm_kernel, 1, False),
        "norm_ffn",
        [half_f32, half_low],
        (),
        (chip, other, hidden_one, out_bias, norm_gain, norm_bias),
    )
    (normed_ffn, act, grad_low, up_sum, send, keep, out_send, out_keep) = call(
        ffn_kernel,
        "ffn",
        [wide, ((rows, hidden), BF), ((rows, hidden), BF), ((1, hidden), F32)] + halves + halves,
        (),
        (
            normed_half,
            core_swap(normed_half),
            w_up,
            w_down,
            grad_act,
            up_bias.reshape(1, hidden),
        ),
        [full],
        flops=2 * rows * model * hidden * 3,
    )
    chip, other = mp_sum(send, keep)

    ffn_blocks = call(
        functools.partial(ffn_weight_kernel, parts),
        "ffn_weights",
        [(blocks + (hidden,), BF)] * (2 * parts),
        (),
        (normed_ffn, grad_low, grad, act),
        [pltpu.VMEM((model, hidden), F32)],
        flops=2 * rows * model * hidden * 2,
    )
    up_sums = send_blocks(ffn_blocks[:parts], 2)
    down_sums = send_blocks(ffn_blocks[parts:], 1)
    vec_shape = ((8, model), F32)
    grad_two, low_half, vec_two = call(
        functools.partial(norm_back_kernel, 2, True),
        "norm_back_ffn",
        [half_f32, half_low, vec_shape],
        (),
        (gate(chip, *ffn_blocks), other, hidden_two, grad, norm_gain),
    )
    turned = ((width, image_rows), BF)
    grad_two_low, dq, dkt, dvt, send, keep = call(
        functools.partial(cross_back_kernel, seqs),
        "cross_back",
        [wide, narrow, turned, turned] + halves,
        (),
        (low_half, core_swap(low_half), cq, co, keys, values, xq, cross_prob),
        [full],
        flops=2 * rows * model * width * 2,
    )
    chip, other = mp_sum(send, keep)
    up_sums = fold(up_sums, 4, "fold_up", chip)
    down_sums = fold(down_sums, 2, "fold_down", up_sums[0])
    send_away, send_own, keep_away, keep_own = call(
        image_part_kernel,
        "image_part",
        [turned] * 4,
        (),
        (gate(dkt, chip), dvt, ck, cv),
    )

    cross_blocks = call(
        functools.partial(cross_weight_kernel, parts),
        "cross_weights",
        [(blocks + (4 * width,), BF)] * parts,
        (),
        (image, gate(dkt, down_sums[0]), dvt, normed_mid, dq, grad_two_low, cross_ctx),
        [pltpu.VMEM((model, width), F32)],
        flops=2 * image_rows * model * width * 2,
    )
    cross_sums = send_blocks(cross_blocks, 1)
    grad_one, low_half, vec_one = call(
        functools.partial(norm_back_kernel, 1, False),
        "norm_back_mid",
        [half_f32, half_low, vec_shape],
        (),
        (gate(chip, *cross_blocks), other, hidden_one, grad_two, norm_gain),
    )
    tall = ((rows + 16, model), BF)
    self_back = call(
        functools.partial(self_back_kernel, seqs, parts),
        "self_back",
        [(blocks + (4 * width,), BF)] * parts + [tall] * 2,
        (text_lengths,),
        (
            low_half,
            core_swap(low_half),
            text,
            norm_gain,
            norm_bias,
            w_self,
            saved,
            out_send,
            out_keep,
            vec_one,
            vec_two,
            up_sum,
        ),
        [
            pltpu.VMEM((rows, model), BF),
            pltpu.VMEM((3, rows, width), BF),
            full,
            pltpu.VMEM((model, width), F32),
            pltpu.VMEM((16, model), F32),
        ],
    )
    self_blocks, (send, keep) = self_back[:parts], self_back[parts:]
    self_sums = send_blocks(self_blocks, 1)
    chip_own, chip_away = call(
        image_chip_kernel,
        "image_chip",
        [((width, image_rows), F32), turned],
        (),
        (gate(keep_own, keep), core_swap(send_own), keep_away, core_swap(send_away)),
    )
    chip, other = mp_sum(send, gate(keep, chip_away))
    up_sums = fold(up_sums, 1, "fold_up", chip)
    cross_sums = fold(cross_sums, 2, "fold_cross", up_sums[0])
    down_sums = fold(down_sums, 4, "fold_down", cross_sums[0])
    text_half, out_half, vec = call(
        finish_kernel,
        "finish",
        [half_f32, half_low, ((16, model), BF)],
        (),
        (gate(chip, down_sums[0]), other, text, grad_one, norm_gain, hidden_two, out_bias),
    )
    image_away = level_swap(gate(chip_away, vec))
    if quick:
        low_rows = lambda count: ((count, 4 * width), BF)
        near, send, vec = call(
            fold_self_one_kernel,
            "fold_self",
            [low_rows(2 * height), low_rows(2 * height + 16), low_rows(16)],
            (),
            (*self_sums, vec, swap(vec, "dp", 8, 1)),
        )
        self_sums = near, swap(send, "dp", 8, 2)
        cross_sums = fold(cross_sums, 4, "fold_cross", near)
    text_grad, layer_out = call(
        join_both_kernel,
        "join",
        [((rows, model), F32), wide],
        (),
        (gate(text_half, cross_sums[0]), core_swap(text_half), out_half, core_swap(out_half)),
    )
    if quick:
        close = lambda sums, first, name: call(
            close_ffn_kernel, name, [((height, hidden), F32)], (), (gate(sums[0], first), sums[1])
        )[0]
        up_grad = close(up_sums, text_grad, "close_up")
        down_turned = close(down_sums, up_grad, "close_down")
        down_grad = down_turned.T
        near, send, vec = call(
            fold_self_two_kernel,
            "fold_self",
            [((height, 4 * width), F32), low_rows(height + 16), low_rows(16)],
            (),
            (gate(self_sums[0], down_turned), self_sums[1], vec),
        )
        self_sums = near, swap(send, "dp", 8, 4)
        query_grad, keyval_grad, cross_out_grad = call(
            close_cross_kernel,
            "close_cross",
            [((height, width), F32), ((2, height, width), F32), ((width, height), F32)],
            (),
            (gate(cross_sums[0], near), cross_sums[1]),
        )
    (image_grad,) = call(
        image_sum_kernel,
        "image_sum",
        [((seqs, width, patches), F32)],
        (),
        (gate(chip_own, cross_sums[0]), image_away),
    )
    vec_outs = [((3, model), F32)] * 3 + [((hidden,), F32)]
    if quick:
        qkv_grad, self_out_grad, gains, shifts, biases, ups = call(
            close_self_kernel,
            "close_self",
            [((3, height, width), F32), ((width, height), F32)] + vec_outs,
            (),
            (gate(self_sums[0], image_grad), self_sums[1], vec),
        )
    else:
        gains, shifts, biases, ups = call(
            vector_kernel, "close_vector", vec_outs, (), (lax.psum(vec.astype(F32), "dp"),)
        )
        total = whole_sum(self_sums)
        qkv_grad = jnp.stack([total[:, j * width : (j + 1) * width] for j in range(3)])
        self_out_grad = total[:, 3 * width :].T
        total = whole_sum(cross_sums)
        query_grad = total[:, :width]
        keyval_grad = jnp.stack([total[:, j * width : (j + 1) * width] for j in (1, 2)])
        cross_out_grad = total[:, 3 * width :].T
        up_grad, down_grad = whole_sum(up_sums), whole_sum(down_sums).T
    return (
        layer_out.reshape(seqs, positions, model),
        text_grad.reshape(seqs, positions, model),
        image_grad.transpose(0, 2, 1),
        qkv_grad,
        self_out_grad,
        query_grad,
        keyval_grad,
        cross_out_grad,
        up_grad,
        down_grad,
        gains,
        shifts,
        biases,
        ups.reshape(hidden),
    )


def solution(mesh):
    placed = (
        P("dp", None, None),
        P("dp", None, None),
        P("dp"),
        P("dp"),
        P(None, "dp", "mp"),
        P("mp", "dp"),
        P("dp", "mp"),
        P(None, "dp", "mp"),
        P("mp", "dp"),
        P("dp", "mp"),
        P("mp", "dp"),
        P(),
        P(),
        P(),
        P("mp"),
        P("dp", None, None),
    )
    return jax.shard_map(
        functools.partial(per_device, mesh.shape["dp"], mesh.shape["mp"]),
        mesh=mesh,
        in_specs=placed,
        out_specs=(
            P("dp", None, None),
            P("dp", None, None),
            P("dp", None, "mp"),
            P(None, "dp", "mp"),
            P("mp", "dp"),
            P("dp", "mp"),
            P(None, "dp", "mp"),
            P("mp", "dp"),
            P("dp", "mp"),
            P("mp", "dp"),
            P(),
            P(),
            P(),
            P("mp"),
        ),
        check_vma=False,
    )
```

time: 262 us -> 182 us (0.69)
  waiting for transfers between devices: 118 us -> 91.4 us
  local copies, waits for them, and re-layouts: 26.8 us -> 4.25 us
  Pallas kernels: 51.1 us -> 33.3 us
  starting transfers between devices: 62 us -> 51.3 us
    ppermute x58 -> x44, waiting for transfers between devices: 118 us -> 60.8 us  [swap(): return lax.ppermute(value, axis, [(i, i ^ bits) for i in range(size)])]
    ppermute x58 -> x44, starting transfers between devices: 62 us -> 27.9 us  [swap(): return lax.ppermute(value, axis, [(i, i ^ bits) for i in range(size)])]
    ppermute x0 -> x12, waiting for transfers between devices: none -> 30.6 us  [around(): return lax.ppermute(value, ('dp', 'mp'), turns)]
    ppermute x0 -> x12, starting transfers between devices: none -> 23.4 us  [around(): return lax.ppermute(value, ('dp', 'mp'), turns)]
    unnamed x115 -> x32, local copies, waits for them, and re-layouts: 22.1 us -> 4.25 us
    pallas_call x25 -> x42, Pallas kernels: 37 us -> 27.2 us  [call(): pl.pallas_call(body, out_shape=[jax.ShapeDtypeStruct(s, d) for s, d in ou...]
    pallas_call x3 -> x2, Pallas kernels: 14.1 us -> 6.03 us  [the longest x1 3.16 us: per_device(): pl.pallas_call(functools.partial(self_forward_kernel, len(self_pieces), s...]
    slice x6 -> x0, local copies, waits for them, and re-layouts: 3.04 us -> none  [the longest x1 0.63 us: per_device(): vec_one[2:3]]
  transfers between devices with their start and end apart: 58 -> 56, of which waited for: 25 -> 25; matrix products, arithmetic and copies ran while one was open for 3% -> 0% of each run, Pallas kernels for 14% -> 17%
where the time goes in v2:
time: 182 us; the launch traced here: 181 us
  waiting for transfers between devices  91.4 us (50%)
  starting transfers between devices  51.3 us (28%)
  Pallas kernels  33.3 us (18%)
  local copies, waits for them, and re-layouts  4.25 us (2%)
    ppermute x44, waiting for transfers between devices, swap(): return lax.ppermute(value, axis, [(i, i ^ bits) for i in range(size)])  60.8 us
    ppermute x12, waiting for transfers between devices, around(): return lax.ppermute(value, ('dp', 'mp'), turns)  30.6 us
    ppermute x44, starting transfers between devices, swap(): return lax.ppermute(value, axis, [(i, i ^ bits) for i in range(size)])  27.9 us
    pallas_call x42, Pallas kernels, call(): pl.pallas_call(body, out_shape=[jax.ShapeDtypeStruct(s, d) for s, d in ou...  27.2 us
    ppermute x12, starting transfers between devices, around(): return lax.ppermute(value, ('dp', 'mp'), turns)  23.4 us
    unnamed x32, local copies, waits for them, and re-layouts  4.25 us
  transfers between devices with their start and end apart: 56, of which 25 were waited for; matrix products, arithmetic and copies ran while one was open for 0% of the time, Pallas kernels for 17%

profile of v2, /device:TPU:0, one launch (start us, length us, event | category | flops | bytes accessed | tf_op | source)
XLA Modules:
  0.0 181.3 jit_solution(10419142997216048342)
XLA Ops:
  5.9 3.0 %collective-permute-start.1 = (bf16[2,96,768]{2,1,0:T(8,128)(2,1)S(1)}, bf16[2,96,768]{2,1,0:T(8,128)(2,1)S(1)}, u32[]{:S(2)}, u32[]{:S(2)}) collective-permute-start(bf16[2,96,768]{2,1,0:T(8,128)(2,1)S(1)} %pairA.1), channel_id=1, source_target_pairs={{0,8},{1,5},{2,10},{3,7},{8,16},{9,1},{10,18},{11,3},{16,24},{17,9... | collective-permute-start | bytes 884744 | tf_op jit(solution)/shard_map/ppermute | solution.py:573
  10.6 2.9 %collective-permute-done.1.refs_1_ = bf16[2,96,768]{2,1,0:T(8,128)(2,1)S(1)} collective-permute-done((bf16[2,96,768]{2,1,0:T(8,128)(2,1)S(1)}, bf16[2,96,768]{2,1,0:T(8,128)(2,1)S(1)}, u32[]{:S(2)}, u32[]{:S(2)}) %collective-permute-start.1) | collective-permute-done | bytes 294944 | tf_op jit(solution)/shard_map/ppermute | solution.py:573
  13.5 3.2 %collective-permute-done.4.refs_1_ = bf16[2,96,768]{2,1,0:T(8,128)(2,1)S(1)} collective-permute-done((bf16[2,96,768]{2,1,0:T(8,128)(2,1)S(1)}, bf16[2,96,768]{2,1,0:T(8,128)(2,1)S(1)}, u32[]{:S(2)}, u32[]{:S(2)}) %collective-permute-start.4) | collective-permute-done | bytes 294944 | tf_op jit(solution)/shard_map/ppermute | solution.py:573
  20.4 3.0 %collective-permute-done.5.refs_2_ = bf16[2,96,768]{2,1,0:T(8,128)(2,1)S(1)} collective-permute-done((bf16[2,96,768]{2,1,0:T(8,128)(2,1)S(1)}, bf16[2,96,768]{2,1,0:T(8,128)(2,1)S(1)}, u32[]{:S(2)}, u32[]{:S(2)}) %collective-permute-start.5) | collective-permute-done | bytes 294944 | tf_op jit(solution)/shard_map/ppermute | solution.py:573
  30.2 6.2 %collective-permute-done.9.pair.refs_3_ = bf16[2,96,768]{2,1,0:T(8,128)(2,1)S(1)} collective-permute-done((bf16[2,96,768]{2,1,0:T(8,128)(2,1)S(1)}, bf16[2,96,768]{2,1,0:T(8,128)(2,1)S(1)}, u32[]{:S(2)}, u32[]{:S(2)}) %collective-permute-start.9) | collective-permute-done | bytes 294944 | tf_op jit(solution)/shard_map/ppermute | solution.py:573
  40.2 7.7 %collective-permute-done.13.refs_7_ = bf16[96,768]{1,0:T(8,128)(2,1)S(1)} collective-permute-done((bf16[96,768]{1,0:T(8,128)(2,1)S(1)}, bf16[96,768]{1,0:T(8,128)(2,1)S(1)}, u32[]{:S(2)}, u32[]{:S(2)}) %collective-permute-start.13) | collective-permute-done | bytes 147488 | tf_op jit(solution)/shard_map/ppermute | solution.py:573
  47.9 3.2 %self_forward.1 = (bf16[768,768]{1,0:T(8,128)(2,1)S(1)}, bf16[256,768]{1,0:T(8,128)(2,1)S(1)}, bf16[128,768]{1,0:T(8,128)(2,1)S(1)}, bf16[128,768]{1,0:T(8,128)(2,1)S(1)}) custom-call(s32[4]{0:T(128)S(1)} %copy-done.13, bf16[256,768]{1,0:T(8,128)(2,1)S(1)} %bitcast.10, f32[3,768]{1,0:T(4,128)S(1)} %copy-done.3, f32[3,768]{1,0:T(4,128)S(1)} %copy-done.4, ...), custom_call_target="tpu_custom_call" | custom-call | flops 1 | bytes 10000000 | tf_op jit(solution)/shard_map/self_forward/pallas_call | solution.py:672
  56.4 3.6 %collective-permute-done.18.refs_7_ = bf16[96,768]{1,0:T(8,128)(2,1)S(1)} collective-permute-done((bf16[96,768]{1,0:T(8,128)(2,1)S(1)}, bf16[96,768]{1,0:T(8,128)(2,1)S(1)}, u32[]{:S(2)}, u32[]{:S(2)}) %collective-permute-start.18) | collective-permute-done | bytes 147488 | tf_op jit(solution)/shard_map/ppermute | solution.py:573
  60.0 2.9 %keyval.3 = (bf16[768,192]{1,0:T(8,128)(2,1)S(1)}, bf16[768,192]{1,0:T(8,128)(2,1)S(1)}, bf16[768,192]{1,0:T(8,128)(2,1)S(1)}, bf16[768,192]{1,0:T(8,128)(2,1)S(...) custom-call(bf16[2304,768]{1,0:T(8,128)(2,1)S(1)} %bitcast.8, ...), custom_call_target="tpu_custom_call" | custom-call | flops 1 | bytes 10000000 | tf_op jit(solution)/shard_map/keyval/pallas_call | solution.py:696
  66.3 3.0 %cross_forward.1 = (bf16[256,768]{1,0:T(8,128)(2,1)S(1)}, bf16[256,192]{1,0:T(8,128)(2,1)S(1)}, f32[4,192,576]{2,1,0:T(8,128)S(1)}, bf16[256,192]{1,0:T(8,128)(2...) custom-call(s32[4]{0:T(128)S(1)} %copy-done.14, bf16[128,768]{1,0:T(8,128)(2,1)S(1)} %get-tuple-element.141.own, ...), custom_call_target="tpu_custom_call" | custom-call | flops 1 | bytes 5505025 | tf_op jit(solution)/shard_map/cross_forward/pallas_call | solution.py:69
  70.1 3.1 %collective-permute-done.25.pair.refs_3_ = bf16[2,96,1536]{2,1,0:T(8,128)(2,1)S(1)} collective-permute-done((bf16[2,96,1536]{2,1,0:T(8,128)(2,1)S(1)}, bf16[2,96,1536]{2,1,0:T(8,128)(2,1)S(1)}, u32[]{:S(2)}, u32[]{:S(2)}) %collective-permute-start.25) | collective-permute-done | bytes 589856 | tf_op jit(solution)/shard_map/ppermute | solution.py:573
  73.3 2.3 %collective-permute-start.29 = (bf16[96,1536]{1,0:T(8,128)(2,1)S(1)}, bf16[96,1536]{1,0:T(8,128)(2,1)S(1)}, u32[]{:S(2)}, u32[]{:S(2)}) collective-permute-start(bf16[96,1536]{1,0:T(8,128)(2,1)S(1)} %takeF.1), channel_id=1, source_target_pairs={{0,8},{1,5},{2,10},{3,7},{8,16},{9,1},{10,18},{11,3},{16,24},{17,9... | collective-permute-start | bytes 884744 | tf_op jit(solution)/shard_map/ppermute | solution.py:573
  75.6 5.0 %collective-permute-done.23.other = bf16[128,768]{1,0:T(8,128)(2,1)S(1)} collective-permute-done((bf16[128,768]{1,0:T(8,128)(2,1)S(1)}, bf16[128,768]{1,0:T(8,128)(2,1)S(1)}, u32[]{:S(2)}, u32[]{:S(2)}) %collective-permute-start.23) | collective-permute-done | bytes 196640 | tf_op jit(solution)/shard_map/ppermute | solution.py:523
  87.1 5.3 %collective-permute-done.31.other = bf16[128,768]{1,0:T(8,128)(2,1)S(1)} collective-permute-done((bf16[128,768]{1,0:T(8,128)(2,1)S(1)}, bf16[128,768]{1,0:T(8,128)(2,1)S(1)}, u32[]{:S(2)}, u32[]{:S(2)}) %collective-permute-start.31) | collective-permute-done | bytes 196640 | tf_op jit(solution)/shard_map/ppermute | solution.py:523
  96.0 2.9 %cross_back.1 = (bf16[256,768]{1,0:T(8,128)(2,1)S(1)}, bf16[256,192]{1,0:T(8,128)(2,1)S(1)}, bf16[192,2304]{1,0:T(8,128)(2,1)S(1)}, bf16[192,2304]{1,0:T(8,128)(...) custom-call(bf16[128,768]{1,0:T(8,128)(2,1)S(1)} %get-tuple-element.165.own, ...), custom_call_target="tpu_custom_call" | custom-call | flops 1 | bytes 7274497 | tf_op jit(solution)/shard_map/cross_back/pallas_call | solution.py:69
  103.7 4.9 %collective-permute-done.34.other = bf16[4,96,768]{2,1,0:T(8,128)(2,1)S(1)} collective-permute-done((bf16[4,96,768]{2,1,0:T(8,128)(2,1)S(1)}, bf16[4,96,768]{2,1,0:T(8,128)(2,1)S(1)}, u32[]{:S(2)}, u32[]{:S(2)}) %collective-permute-start.34) | collective-permute-done | bytes 589856 | tf_op jit(solution)/shard_map/ppermute | solution.py:523
  114.2 4.3 %self_back.1 = (bf16[4,96,768]{2,1,0:T(8,128)(2,1)S(1)}, bf16[4,96,768]{2,1,0:T(8,128)(2,1)S(1)}, bf16[272,768]{1,0:T(8,128)(2,1)S(1)}, bf16[272,768]{1,0:T(8,128)(2,1)S(1)}) custom-call(s32[4]{0:T(128)S(1)} %copy-done.13, bf16[128,768]{1,0:T(8,128)(2,1)S(1)} %get-tuple-element.185.own, bf16[128,768]{1,0:T(8,128)(2,1)S(1)} %collective-permute-done.37.other, ...), custom_call_target="tpu_custom_call" | custom-call | flops 1 | bytes 4838401 | tf_op jit(solution)/shard_map/self_back/pallas_call | solution.py:69
  121.4 2.6 %collective-permute-start.41 = (bf16[2,96,768]{2,1,0:T(8,128)(2,1)S(1)}, bf16[2,96,768]{2,1,0:T(8,128)(2,1)S(1)}, u32[]{:S(2)}, u32[]{:S(2)}) collective-permute-start(bf16[2,96,768]{2,1,0:T(8,128)(2,1)S(1)} %get-tuple-element.206), channel_id=1, source_target_pairs={{0,16},{4,20},{8,24},{12,28},{16,0},{20,4},{24,8},{28,12},{1,17},{... | collective-permute-start | bytes 884744 | tf_op jit(solution)/shard_map/ppermute | solution.py:523
  125.6 11.7 %collective-permute-done.41.other = bf16[2,96,768]{2,1,0:T(8,128)(2,1)S(1)} collective-permute-done((bf16[2,96,768]{2,1,0:T(8,128)(2,1)S(1)}, bf16[2,96,768]{2,1,0:T(8,128)(2,1)S(1)}, u32[]{:S(2)}, u32[]{:S(2)}) %collective-permute-start.41) | collective-permute-done | bytes 294944 | tf_op jit(solution)/shard_map/ppermute | solution.py:523
  141.6 5.3 %collective-permute-done.45.other = bf16[4,96,768]{2,1,0:T(8,128)(2,1)S(1)} collective-permute-done((bf16[4,96,768]{2,1,0:T(8,128)(2,1)S(1)}, bf16[4,96,768]{2,1,0:T(8,128)(2,1)S(1)}, u32[]{:S(2)}, u32[]{:S(2)}) %collective-permute-start.45) | collective-permute-done | bytes 589856 | tf_op jit(solution)/shard_map/ppermute | solution.py:523
  148.4 2.3 %collective-permute-done.46.vec_other = bf16[16,768]{1,0:T(8,128)(2,1)S(1)} collective-permute-done((bf16[16,768]{1,0:T(8,128)(2,1)S(1)}, bf16[16,768]{1,0:T(8,128)(2,1)S(1)}, u32[]{:S(2)}, u32[]{:S(2)}) %collective-permute-start.46) | collective-permute-done | bytes 24608 | tf_op jit(solution)/shard_map/ppermute | solution.py:523
  152.9 2.6 %collective-permute-start.52 = (bf16[96,768]{1,0:T(8,128)(2,1)S(1)}, bf16[96,768]{1,0:T(8,128)(2,1)S(1)}, u32[]{:S(2)}, u32[]{:S(2)}) collective-permute-start(bf16[96,768]{1,0:T(8,128)(2,1)S(1)} %get-tuple-element.233), channel_id=1, source_target_pairs={{0,16},{4,20},{8,24},{12,28},{16,0},{20,4},{24,8},{28,12},{1,17},{... | collective-permute-start | bytes 442376 | tf_op jit(solution)/shard_map/ppermute | solution.py:523
  157.4 2.8 %collective-permute-done.52.other = bf16[96,768]{1,0:T(8,128)(2,1)S(1)} collective-permute-done((bf16[96,768]{1,0:T(8,128)(2,1)S(1)}, bf16[96,768]{1,0:T(8,128)(2,1)S(1)}, u32[]{:S(2)}, u32[]{:S(2)}) %collective-permute-start.52) | collective-permute-done | bytes 147488 | tf_op jit(solution)/shard_map/ppermute | solution.py:523
  165.3 12.7 %collective-permute-done.55.refs_1_ = bf16[96,768]{1,0:T(8,128)(2,1)S(1)} collective-permute-done((bf16[96,768]{1,0:T(8,128)(2,1)S(1)}, bf16[96,768]{1,0:T(8,128)(2,1)S(1)}, u32[]{:S(2)}, u32[]{:S(2)}) %collective-permute-start.55) | collective-permute-done | bytes 147488 | tf_op jit(solution)/shard_map/ppermute | solution.py:523
  (165 shorter events, 73.8 us)
Async XLA Ops:
  23.4 13.0 %collective-permute-start.6 = (bf16[2,96,1536]{2,1,0:T(8,128)(2,1)S(1)}, bf16[2,96,1536]{2,1,0:T(8,128)(2,1)S(1)}, u32[]{:S(2)}, u32[]{:S(2)}) collective-permute-start(bf16[2,96,1536]{2,1,0:T(8,128)(2,1)S(1)} %pairF.1), channel_id=1, source_target_pairs={{0,8},{1,5},{2,10},{3,7},{8,16},{9,1},{10,18},{11,3},{16,24},{17,9... | collective-permute-start | bytes 1769480 | tf_op jit(solution)/shard_map/ppermute | solution.py:573
  28.7 11.5 %collective-permute-start.7 = (bf16[2,96,768]{2,1,0:T(8,128)(2,1)S(1)}, bf16[2,96,768]{2,1,0:T(8,128)(2,1)S(1)}, u32[]{:S(2)}, u32[]{:S(2)}) collective-permute-start(bf16[2,96,768]{2,1,0:T(8,128)(2,1)S(1)} %collective-permute-done.5.refs_2_), channel_id=1, source_target_pairs={{0,8},{1,5},{2,10},{3,7},{8,16},{9,1},{10,18},{11,3},{16,24},{17,9... | collective-permute-start | bytes 884744 | tf_op jit(solution)/shard_map/ppermute | solution.py:573
  36.4 11.5 %collective-permute-start.12 = (bf16[2,96,768]{2,1,0:T(8,128)(2,1)S(1)}, bf16[2,96,768]{2,1,0:T(8,128)(2,1)S(1)}, u32[]{:S(2)}, u32[]{:S(2)}) collective-permute-start(bf16[2,96,768]{2,1,0:T(8,128)(2,1)S(1)} %collective-permute-done.9.pair.refs_3_), channel_id=1, source_target_pairs={{0,1},{1,0},{2,3},{3,2},{4,5},{5,4},{6,7},{7,6},{8,9},{9,8},{10,11... | collective-permute-start | bytes 884744 | tf_op jit(solution)/shard_map/ppermute | solution.py:523
  36.4 26.5 %collective-permute-start.19 = (bf16[2,96,1536]{2,1,0:T(8,128)(2,1)S(1)}, bf16[2,96,1536]{2,1,0:T(8,128)(2,1)S(1)}, u32[]{:S(2)}, u32[]{:S(2)}) collective-permute-start(bf16[2,96,1536]{2,1,0:T(8,128)(2,1)S(1)} %collective-permute-done.6.refs_1_), channel_id=1, source_target_pairs={{0,8},{1,5},{2,10},{3,7},{8,16},{9,1},{10,18},{11,3},{16,24},{17,9... | collective-permute-start | bytes 1769480 | tf_op jit(solution)/shard_map/ppermute | solution.py:573
  40.2 14.6 %collective-permute-start.15 = (bf16[2,96,768]{2,1,0:T(8,128)(2,1)S(1)}, bf16[2,96,768]{2,1,0:T(8,128)(2,1)S(1)}, u32[]{:S(2)}, u32[]{:S(2)}) collective-permute-start(bf16[2,96,768]{2,1,0:T(8,128)(2,1)S(1)} %collective-permute-done.4.refs_1_), channel_id=1, source_target_pairs={{0,1},{1,0},{2,3},{3,2},{4,5},{5,4},{6,7},{7,6},{8,9},{9,8},{10,11... | collective-permute-start | bytes 884744 | tf_op jit(solution)/shard_map/ppermute | solution.py:523
  52.7 10.3 %collective-permute-start.20 = (bf16[128,768]{1,0:T(8,128)(2,1)S(1)}, bf16[128,768]{1,0:T(8,128)(2,1)S(1)}, u32[]{:S(2)}, u32[]{:S(2)}) collective-permute-start(bf16[128,768]{1,0:T(8,128)(2,1)S(1)} %add_pair.5.chip), channel_id=1, source_target_pairs={{0,2},{1,3},{2,0},{3,1},{4,6},{5,7},{6,4},{7,5},{8,10},{9,11},{10,... | collective-permute-start | bytes 589832 | tf_op jit(solution)/shard_map/ppermute | solution.py:523
  69.6 11.4 %collective-permute-start.26 = (bf16[2,96,1536]{2,1,0:T(8,128)(2,1)S(1)}, bf16[2,96,1536]{2,1,0:T(8,128)(2,1)S(1)}, u32[]{:S(2)}, u32[]{:S(2)}) collective-permute-start(bf16[2,96,1536]{2,1,0:T(8,128)(2,1)S(1)} %collective-permute-done.6.refs_1_), channel_id=1, source_target_pairs={{0,1},{1,0},{2,3},{3,2},{4,5},{5,4},{6,7},{7,6},{8,9},{9,8},{10,11... | collective-permute-start | bytes 1769480 | tf_op jit(solution)/shard_map/ppermute | solution.py:523
  69.9 11.0 %collective-permute-start.27 = (bf16[2,96,1536]{2,1,0:T(8,128)(2,1)S(1)}, bf16[2,96,1536]{2,1,0:T(8,128)(2,1)S(1)}, u32[]{:S(2)}, u32[]{:S(2)}) collective-permute-start(bf16[2,96,1536]{2,1,0:T(8,128)(2,1)S(1)} %collective-permute-done.19.refs_2_), channel_id=1, source_target_pairs={{0,1},{1,0},{2,3},{3,2},{4,5},{5,4},{6,7},{7,6},{8,9},{9,8},{10,11... | collective-permute-start | bytes 1769480 | tf_op jit(solution)/shard_map/ppermute | solution.py:523
  92.9 15.7 %collective-permute-start.34 = (bf16[4,96,768]{2,1,0:T(8,128)(2,1)S(1)}, bf16[4,96,768]{2,1,0:T(8,128)(2,1)S(1)}, u32[]{:S(2)}, u32[]{:S(2)}) collective-permute-start(bf16[4,96,768]{2,1,0:T(8,128)(2,1)S(1)} %get-tuple-element.160), channel_id=1, source_target_pairs={{0,8},{4,12},{8,0},{12,4},{16,24},{20,28},{24,16},{28,20},{1,9},{5... | collective-permute-start | bytes 1769480 | tf_op jit(solution)/shard_map/ppermute | solution.py:523
  94.5 15.4 %collective-permute-start.35 = (bf16[4,96,768]{2,1,0:T(8,128)(2,1)S(1)}, bf16[4,96,768]{2,1,0:T(8,128)(2,1)S(1)}, u32[]{:S(2)}, u32[]{:S(2)}) collective-permute-start(bf16[4,96,768]{2,1,0:T(8,128)(2,1)S(1)} %get-tuple-element.162), channel_id=1, source_target_pairs={{0,4},{4,0},{8,12},{12,8},{16,20},{20,16},{24,28},{28,24},{1,5},{5... | collective-permute-start | bytes 1769480 | tf_op jit(solution)/shard_map/ppermute | solution.py:523
  102.5 17.7 %collective-permute-start.38 = (bf16[192,2304]{1,0:T(8,128)(2,1)S(1)}, bf16[192,2304]{1,0:T(8,128)(2,1)S(1)}, u32[]{:S(2)}, u32[]{:S(2)}) collective-permute-start(bf16[192,2304]{1,0:T(8,128)(2,1)S(1)} %get-tuple-element.199), channel_id=1, source_target_pairs={{0,1},{1,0},{2,3},{3,2},{4,5},{5,4},{6,7},{7,6},{8,9},{9,8},{10,11... | collective-permute-start | bytes 2654216 | tf_op jit(solution)/shard_map/ppermute | solution.py:523
  102.7 17.5 %collective-permute-start.39 = (bf16[192,2304]{1,0:T(8,128)(2,1)S(1)}, bf16[192,2304]{1,0:T(8,128)(2,1)S(1)}, u32[]{:S(2)}, u32[]{:S(2)}) collective-permute-start(bf16[192,2304]{1,0:T(8,128)(2,1)S(1)} %get-tuple-element.201), channel_id=1, source_target_pairs={{0,1},{1,0},{2,3},{3,2},{4,5},{5,4},{6,7},{7,6},{8,9},{9,8},{10,11... | collective-permute-start | bytes 2654216 | tf_op jit(solution)/shard_map/ppermute | solution.py:523
  118.7 18.7 %collective-permute-start.42 = (bf16[4,96,768]{2,1,0:T(8,128)(2,1)S(1)}, bf16[4,96,768]{2,1,0:T(8,128)(2,1)S(1)}, u32[]{:S(2)}, u32[]{:S(2)}) collective-permute-start(bf16[4,96,768]{2,1,0:T(8,128)(2,1)S(1)} %get-tuple-element.182), channel_id=1, source_target_pairs={{0,4},{4,0},{8,12},{12,8},{16,20},{20,16},{24,28},{28,24},{1,5},{5... | collective-permute-start | bytes 1769480 | tf_op jit(solution)/shard_map/ppermute | solution.py:523
  120.7 18.0 %collective-permute-start.44 = (bf16[272,768]{1,0:T(8,128)(2,1)S(1)}, bf16[272,768]{1,0:T(8,128)(2,1)S(1)}, u32[]{:S(2)}, u32[]{:S(2)}) collective-permute-start(bf16[272,768]{1,0:T(8,128)(2,1)S(1)} %add_pair.9.chip), channel_id=1, source_target_pairs={{0,2},{1,3},{2,0},{3,1},{4,6},{5,7},{6,4},{7,5},{8,10},{9,11},{10,... | collective-permute-start | bytes 1253384 | tf_op jit(solution)/shard_map/ppermute | solution.py:523
  121.4 15.9 %collective-permute-start.41 = (bf16[2,96,768]{2,1,0:T(8,128)(2,1)S(1)}, bf16[2,96,768]{2,1,0:T(8,128)(2,1)S(1)}, u32[]{:S(2)}, u32[]{:S(2)}) collective-permute-start(bf16[2,96,768]{2,1,0:T(8,128)(2,1)S(1)} %get-tuple-element.206), channel_id=1, source_target_pairs={{0,16},{4,20},{8,24},{12,28},{16,0},{20,4},{24,8},{28,12},{1,17},{... | collective-permute-start | bytes 884744 | tf_op jit(solution)/shard_map/ppermute | solution.py:523
  123.9 14.7 %collective-permute-start.43 = (bf16[2,96,768]{2,1,0:T(8,128)(2,1)S(1)}, bf16[2,96,768]{2,1,0:T(8,128)(2,1)S(1)}, u32[]{:S(2)}, u32[]{:S(2)}) collective-permute-start(bf16[2,96,768]{2,1,0:T(8,128)(2,1)S(1)} %get-tuple-element.211), channel_id=1, source_target_pairs={{0,8},{4,12},{8,0},{12,4},{16,24},{20,28},{24,16},{28,20},{1,9},{5... | collective-permute-start | bytes 884744 | tf_op jit(solution)/shard_map/ppermute | solution.py:523
  124.4 22.5 %collective-permute-start.45 = (bf16[4,96,768]{2,1,0:T(8,128)(2,1)S(1)}, bf16[4,96,768]{2,1,0:T(8,128)(2,1)S(1)}, u32[]{:S(2)}, u32[]{:S(2)}) collective-permute-start(bf16[4,96,768]{2,1,0:T(8,128)(2,1)S(1)} %get-tuple-element.217), channel_id=1, source_target_pairs={{0,4},{4,0},{8,12},{12,8},{16,20},{20,16},{24,28},{28,24},{1,5},{5... | collective-permute-start | bytes 1769480 | tf_op jit(solution)/shard_map/ppermute | solution.py:523
  139.2 39.6 %collective-permute-start.50 = (bf16[192,2304]{1,0:T(8,128)(2,1)S(1)}, bf16[192,2304]{1,0:T(8,128)(2,1)S(1)}, u32[]{:S(2)}, u32[]{:S(2)}) collective-permute-start(bf16[192,2304]{1,0:T(8,128)(2,1)S(1)} %get-tuple-element.229), channel_id=1, source_target_pairs={{0,2},{1,3},{2,0},{3,1},{4,6},{5,7},{6,4},{7,5},{8,10},{9,11},{10,... | collective-permute-start | bytes 2654216 | tf_op jit(solution)/shard_map/ppermute | solution.py:523
  140.6 10.8 %collective-permute-start.47 = (bf16[2,96,768]{2,1,0:T(8,128)(2,1)S(1)}, bf16[2,96,768]{2,1,0:T(8,128)(2,1)S(1)}, u32[]{:S(2)}, u32[]{:S(2)}) collective-permute-start(bf16[2,96,768]{2,1,0:T(8,128)(2,1)S(1)} %get-tuple-element.221), channel_id=1, source_target_pairs={{0,8},{4,12},{8,0},{12,4},{16,24},{20,28},{24,16},{28,20},{1,9},{5... | collective-permute-start | bytes 884744 | tf_op jit(solution)/shard_map/ppermute | solution.py:523
  141.1 14.5 %collective-permute-start.48 = (f32[128,768]{1,0:T(8,128)S(1)}, f32[128,768]{1,0:T(8,128)S(1)}, u32[]{:S(2)}, u32[]{:S(2)}) collective-permute-start(f32[128,768]{1,0:T(8,128)S(1)} %get-tuple-element.223.own), channel_id=1, source_target_pairs={{0,1},{1,0},{2,3},{3,2},{4,5},{5,4},{6,7},{7,6},{8,9},{9,8},{10,11... | collective-permute-start | bytes 1179656 | tf_op jit(solution)/shard_map/ppermute | solution.py:523
  141.1 11.8 %collective-permute-start.49 = (bf16[128,768]{1,0:T(8,128)(2,1)S(1)}, bf16[128,768]{1,0:T(8,128)(2,1)S(1)}, u32[]{:S(2)}, u32[]{:S(2)}) collective-permute-start(bf16[128,768]{1,0:T(8,128)(2,1)S(1)} %get-tuple-element.224.own_low), channel_id=1, source_target_pairs={{0,1},{1,0},{2,3},{3,2},{4,5},{5,4},{6,7},{7,6},{8,9},{9,8},{10,11... | collective-permute-start | bytes 589832 | tf_op jit(solution)/shard_map/ppermute | solution.py:523
  150.9 11.4 %collective-permute-start.53 = (bf16[208,768]{1,0:T(8,128)(2,1)S(1)}, bf16[208,768]{1,0:T(8,128)(2,1)S(1)}, u32[]{:S(2)}, u32[]{:S(2)}) collective-permute-start(bf16[208,768]{1,0:T(8,128)(2,1)S(1)} %get-tuple-element.235), channel_id=1, source_target_pairs={{0,8},{4,12},{8,0},{12,4},{16,24},{20,28},{24,16},{28,20},{1,9},{5... | collective-permute-start | bytes 958472 | tf_op jit(solution)/shard_map/ppermute | solution.py:523
  162.3 18.1 %collective-permute-start.54 = (bf16[112,768]{1,0:T(8,128)(2,1)S(1)}, bf16[112,768]{1,0:T(8,128)(2,1)S(1)}, u32[]{:S(2)}, u32[]{:S(2)}) collective-permute-start(bf16[112,768]{1,0:T(8,128)(2,1)S(1)} %get-tuple-element.239), channel_id=1, source_target_pairs={{0,16},{4,20},{8,24},{12,28},{16,0},{20,4},{24,8},{28,12},{1,17},{... | collective-permute-start | bytes 516104 | tf_op jit(solution)/shard_map/ppermute | solution.py:523
  164.6 13.4 %collective-permute-start.55 = (bf16[96,768]{1,0:T(8,128)(2,1)S(1)}, bf16[96,768]{1,0:T(8,128)(2,1)S(1)}, u32[]{:S(2)}, u32[]{:S(2)}) collective-permute-start(bf16[96,768]{1,0:T(8,128)(2,1)S(1)} %get-tuple-element.244), channel_id=1, source_target_pairs={{0,16},{4,20},{8,24},{12,28},{16,0},{20,4},{24,8},{28,12},{1,17},{... | collective-permute-start | bytes 442376 | tf_op jit(solution)/shard_map/ppermute | solution.py:523
  (48 other events, 414.9 us)

commit v3 on v2

--- a/solution.py
+++ b/solution.py
@@ -360,34 +360,46 @@
     scatter_blocks(turned, 3 * width, outs)
 
 
-def image_part_kernel(dkt, dvt, wk, wv, send_away, send_own, keep_away, keep_own):
+def image_part_kernel(dkt, dvt, wk, wv, away_one, away_two, own_one, own_two, keep_away, keep_own):
     width = wk.shape[1]
-    for k, target in enumerate((keep_own, keep_away, send_own, send_away)):
-        core, level = lax.axis_index("mp") & 1, lax.axis_index("mp") >> 1
+    core, level = lax.axis_index("mp") & 1, lax.axis_index("mp") >> 1
+    half = own_one.shape[1]
+    for k, targets in enumerate(
+        ((keep_own,), (keep_away,), (own_one, own_two), (away_one, away_two))
+    ):
         at = (2 * (level ^ (k & 1)) + (core ^ (k >> 1))) * width
         rows = pl.ds(pl.multiple_of(at, 64), width)
-        target[...] = (nn(wk[rows, :], dkt[...]) + nn(wv[rows, :], dvt[...])).astype(BF)
+        part = (nn(wk[rows, :], dkt[...]) + nn(wv[rows, :], dvt[...])).astype(BF)
+        if len(targets) == 1:
+            targets[0][...] = part
+        else:
+            targets[0][...] = part[:, :half]
+            targets[1][...] = part[:, half:]
 
 
 def add_pair_kernel(one, two, out):
     out[...] = (one[...].astype(F32) + two[...].astype(F32)).astype(BF)
 
 
-def image_chip_kernel(keep_own, own, keep_away, away, out_own, out_away):
-    out_own[...] = keep_own[...].astype(F32) + own[...].astype(F32)
-    out_away[...] = (keep_away[...].astype(F32) + away[...].astype(F32)).astype(BF)
-
-
-def image_sum_kernel(own, away, out):
+def add_halves_kernel(keep, one, two, out):
+    half = one.shape[1]
+    out[:, :half] = (keep[:, :half].astype(F32) + one[...].astype(F32)).astype(BF)
+    out[:, half:] = (keep[:, half:].astype(F32) + two[...].astype(F32)).astype(BF)
+
+
+def image_sum_kernel(keep, one, two, away, out):
     patches = out.shape[2]
+    per = one.shape[1] // patches
     for b in range(out.shape[0]):
         ks = slice(b * patches, (b + 1) * patches)
-        out[b] = own[:, ks] + away[:, ks].astype(F32)
+        part = one if b < per else two
+        ps = slice((b % per) * patches, (b % per + 1) * patches)
+        out[b] = keep[:, ks].astype(F32) + part[:, ps].astype(F32) + away[:, ks].astype(F32)
 
 
 def self_back_kernel(
     seqs, parts, lens, own, other, text, gain, bias, w, qkv,
-    out_send, out_keep, one, two, ups, *refs
+    one, two, ups, *refs
 ):
     outs = refs[:parts]
     send, keep, low, dqkv, full, narrow, vec = refs[parts:]
@@ -419,8 +431,6 @@
     full[...] = part
     split_halves(full, send, keep)
     half = own.shape[0]
-    send[half : 2 * half] = out_send[...]
-    keep[half : 2 * half] = out_keep[...]
     vec[...] = jnp.zeros_like(vec)
     vec[0:1] = jnp.sum(part * n, axis=0, keepdims=True)
     vec[1:2], vec[2:3] = one[0:1], two[0:1]
@@ -428,21 +438,23 @@
     vec[4:5], vec[5:6] = one[1:2], two[1:2]
     vec[6:7], vec[7:8], vec[8:9] = one[2:3], two[2:3], two[3:4]
     vec[pl.ds(9 + lax.axis_index("mp"), 1), :] = ups[...]
-    send[2 * half :] = vec[...].astype(BF)
-    keep[2 * half :] = vec[...].astype(BF)
-
-
-def finish_kernel(chip, other, text, resid, gain, hidden, out_bias, grad_out, layer_out, vec):
+    send[half:] = vec[...].astype(BF)
+    keep[half:] = vec[...].astype(BF)
+
+
+def finish_kernel(chip, other, text, resid, gain, grad_out, vec):
     half = resid.shape[0]
     grad = chip[:half].astype(F32) + other[:half].astype(F32)
     base = text[half_rows(half), :].astype(F32)
     n, inv_std = norm_parts(base)
     grad_out[...] = resid[...] + norm_back(grad, n, inv_std, gain[0:1])
-    mid = slice(half, 2 * half)
-    layer_out[...] = (
-        hidden[...] + (chip[mid].astype(F32) + other[mid].astype(F32)) + out_bias[2:3]
+    vec[...] = (chip[half:].astype(F32) + other[half:].astype(F32)).astype(BF)
+
+
+def layer_out_kernel(chip, other, hidden, out_bias, out):
+    out[...] = (
+        hidden[...] + (chip[...].astype(F32) + other[...].astype(F32)) + out_bias[2:3]
     ).astype(BF)
-    vec[...] = (chip[2 * half :].astype(F32) + other[2 * half :].astype(F32)).astype(BF)
 
 
 def join_both_kernel(own, other, own_low, other_low, out, out_low):
@@ -790,17 +802,17 @@
         [full],
         flops=2 * rows * model * width * 2,
     )
-    chip, other = mp_sum(send, keep)
+    turned_half = ((width, image_rows // 2), BF)
+    away_one, away_two, own_one, own_two, keep_away, keep_own = call(
+        image_part_kernel,
+        "image_part",
+        [turned_half] * 4 + [turned] * 2,
+        (),
+        (dkt, dvt, ck, cv),
+    )
+    chip, other = mp_sum(send, gate(keep, keep_own))
     up_sums = fold(up_sums, 4, "fold_up", chip)
     down_sums = fold(down_sums, 2, "fold_down", up_sums[0])
-    send_away, send_own, keep_away, keep_own = call(
-        image_part_kernel,
-        "image_part",
-        [turned] * 4,
-        (),
-        (gate(dkt, chip), dvt, ck, cv),
-    )
-
     cross_blocks = call(
         functools.partial(cross_weight_kernel, parts),
         "cross_weights",
@@ -818,7 +830,14 @@
         (),
         (gate(chip, *cross_blocks), other, hidden_one, grad_two, norm_gain),
     )
-    tall = ((rows + 16, model), BF)
+    (chip_away,) = call(
+        add_halves_kernel,
+        "image_chip",
+        [turned],
+        (),
+        (gate(keep_away, low_half), core_swap(away_one), core_swap(away_two)),
+    )
+    tall = ((half + 16, model), BF)
     self_back = call(
         functools.partial(self_back_kernel, seqs, parts),
         "self_back",
@@ -827,13 +846,11 @@
         (
             low_half,
             core_swap(low_half),
-            text,
+            gate(text, chip_away),
             norm_gain,
             norm_bias,
             w_self,
             saved,
-            out_send,
-            out_keep,
             vec_one,
             vec_two,
             up_sum,
@@ -848,25 +865,20 @@
     )
     self_blocks, (send, keep) = self_back[:parts], self_back[parts:]
     self_sums = send_blocks(self_blocks, 1)
-    chip_own, chip_away = call(
-        image_chip_kernel,
-        "image_chip",
-        [((width, image_rows), F32), turned],
-        (),
-        (gate(keep_own, keep), core_swap(send_own), keep_away, core_swap(send_away)),
-    )
-    chip, other = mp_sum(send, gate(keep, chip_away))
-    up_sums = fold(up_sums, 1, "fold_up", chip)
-    cross_sums = fold(cross_sums, 2, "fold_cross", up_sums[0])
-    down_sums = fold(down_sums, 4, "fold_down", cross_sums[0])
-    text_half, out_half, vec = call(
+    chip, other = mp_sum(send, keep)
+    text_half, vec = call(
         finish_kernel,
         "finish",
-        [half_f32, half_low, ((16, model), BF)],
-        (),
-        (gate(chip, down_sums[0]), other, text, grad_one, norm_gain, hidden_two, out_bias),
+        [half_f32, ((16, model), BF)],
+        (),
+        (chip, other, text, grad_one, norm_gain),
     )
     image_away = level_swap(gate(chip_away, vec))
+    cross_sums = fold(cross_sums, 2, "fold_cross", vec)
+    down_sums = fold(down_sums, 4, "fold_down", cross_sums[0])
+    up_sums = fold(up_sums, 1, "fold_up", down_sums[0])
+    out_chip = add_pair(gate(out_keep, up_sums[0]), core_swap(out_send))
+    out_other = level_swap(out_chip)
     if quick:
         low_rows = lambda count: ((count, 4 * width), BF)
         near, send, vec = call(
@@ -874,30 +886,42 @@
             "fold_self",
             [low_rows(2 * height), low_rows(2 * height + 16), low_rows(16)],
             (),
-            (*self_sums, vec, swap(vec, "dp", 8, 1)),
+            (gate(self_sums[0], out_chip), self_sums[1], vec, swap(vec, "dp", 8, 1)),
         )
         self_sums = near, swap(send, "dp", 8, 2)
-        cross_sums = fold(cross_sums, 4, "fold_cross", near)
+        cross_sums = gate(cross_sums[0], near), cross_sums[1]
+    cross_sums = fold(cross_sums, 4, "fold_cross", *self_sums[:1])
+    if quick:
+        close = lambda sums, first, name: call(
+            close_ffn_kernel, name, [((height, hidden), F32)], (), (gate(sums[0], first), sums[1])
+        )[0]
+        down_turned = close(down_sums, cross_sums[0], "close_down")
+        up_grad = close(up_sums, down_turned, "close_up")
+        down_grad = down_turned.T
+        join_first = gate(text_half, up_grad)
+    else:
+        join_first = text_half
+    (out_half,) = call(
+        layer_out_kernel,
+        "layer_out",
+        [half_low],
+        (),
+        (gate(out_chip, join_first), out_other, hidden_two, out_bias),
+    )
     text_grad, layer_out = call(
         join_both_kernel,
         "join",
         [((rows, model), F32), wide],
         (),
-        (gate(text_half, cross_sums[0]), core_swap(text_half), out_half, core_swap(out_half)),
+        (join_first, core_swap(text_half), out_half, core_swap(out_half)),
     )
     if quick:
-        close = lambda sums, first, name: call(
-            close_ffn_kernel, name, [((height, hidden), F32)], (), (gate(sums[0], first), sums[1])
-        )[0]
-        up_grad = close(up_sums, text_grad, "close_up")
-        down_turned = close(down_sums, up_grad, "close_down")
-        down_grad = down_turned.T
         near, send, vec = call(
             fold_self_two_kernel,
             "fold_self",
             [((height, 4 * width), F32), low_rows(height + 16), low_rows(16)],
             (),
-            (gate(self_sums[0], down_turned), self_sums[1], vec),
+            (gate(self_sums[0], text_grad), self_sums[1], vec),
         )
         self_sums = near, swap(send, "dp", 8, 4)
         query_grad, keyval_grad, cross_out_grad = call(
@@ -912,7 +936,7 @@
         "image_sum",
         [((seqs, width, patches), F32)],
         (),
-        (gate(chip_own, cross_sums[0]), image_away),
+        (gate(keep_own, query_grad) if quick else keep_own, core_swap(own_one), core_swap(own_two), image_away),
     )
     vec_outs = [((3, model), F32)] * 3 + [((hidden,), F32)]
     if quick:

time: 182 us -> 176 us (0.967)
  waiting for transfers between devices: 91.4 us -> 83.4 us
  starting transfers between devices: 51.3 us -> 53.5 us
    ppermute x44 -> x48, waiting for transfers between devices: 60.8 us -> 52.8 us  [swap(): return lax.ppermute(value, axis, [(i, i ^ bits) for i in range(size)])]
    ppermute x44 -> x48, starting transfers between devices: 27.9 us -> 30.1 us  [swap(): return lax.ppermute(value, axis, [(i, i ^ bits) for i in range(size)])]
    pallas_call x42 -> x44, Pallas kernels: 27.2 us -> 27.2 us  [call(): pl.pallas_call(body, out_shape=[jax.ShapeDtypeStruct(s, d) for s, d in ou...]
  transfers between devices with their start and end apart: 56 -> 60, of which waited for: 25 -> 28; matrix products, arithmetic and copies ran while one was open for 0% -> 0% of each run, Pallas kernels for 17% -> 17%
where the time goes in v3:
time: 176 us
  waiting for transfers between devices  83.4 us (47%)
  starting transfers between devices  53.5 us (30%)
  Pallas kernels  33.3 us (19%)
  local copies, waits for them, and re-layouts  4.25 us (2%)
    ppermute x48, waiting for transfers between devices, swap(): return lax.ppermute(value, axis, [(i, i ^ bits) for i in range(size)])  52.8 us
    ppermute x12, waiting for transfers between devices, around(): return lax.ppermute(value, ('dp', 'mp'), turns)  30.6 us
    ppermute x48, starting transfers between devices, swap(): return lax.ppermute(value, axis, [(i, i ^ bits) for i in range(size)])  30.1 us
    pallas_call x44, Pallas kernels, call(): pl.pallas_call(body, out_shape=[jax.ShapeDtypeStruct(s, d) for s, d in ou...  27.2 us
    ppermute x12, starting transfers between devices, around(): return lax.ppermute(value, ('dp', 'mp'), turns)  23.4 us
    unnamed x32, local copies, waits for them, and re-layouts  4.25 us
  transfers between devices with their start and end apart: 60, of which 28 were waited for; matrix products, arithmetic and copies ran while one was open for 0% of the time, Pallas kernels for 17%

profile of v3, /device:TPU:0, one launch (start us, length us, event | category | flops | bytes accessed | tf_op | source)
XLA Modules:
  0.0 175.5 jit_solution(973900053748744769)
XLA Ops:
  5.9 3.0 %collective-permute-start.1 = (bf16[2,96,768]{2,1,0:T(8,128)(2,1)S(1)}, bf16[2,96,768]{2,1,0:T(8,128)(2,1)S(1)}, u32[]{:S(2)}, u32[]{:S(2)}) collective-permute-start(bf16[2,96,768]{2,1,0:T(8,128)(2,1)S(1)} %pairA.1), channel_id=1, source_target_pairs={{0,8},{1,5},{2,10},{3,7},{8,16},{9,1},{10,18},{11,3},{16,24},{17,9... | collective-permute-start | bytes 884744 | tf_op jit(solution)/shard_map/ppermute | solution.py:585
  10.6 2.9 %collective-permute-done.1.refs_1_ = bf16[2,96,768]{2,1,0:T(8,128)(2,1)S(1)} collective-permute-done((bf16[2,96,768]{2,1,0:T(8,128)(2,1)S(1)}, bf16[2,96,768]{2,1,0:T(8,128)(2,1)S(1)}, u32[]{:S(2)}, u32[]{:S(2)}) %collective-permute-start.1) | collective-permute-done | bytes 294944 | tf_op jit(solution)/shard_map/ppermute | solution.py:585
  13.5 3.2 %collective-permute-done.4.refs_1_ = bf16[2,96,768]{2,1,0:T(8,128)(2,1)S(1)} collective-permute-done((bf16[2,96,768]{2,1,0:T(8,128)(2,1)S(1)}, bf16[2,96,768]{2,1,0:T(8,128)(2,1)S(1)}, u32[]{:S(2)}, u32[]{:S(2)}) %collective-permute-start.4) | collective-permute-done | bytes 294944 | tf_op jit(solution)/shard_map/ppermute | solution.py:585
  20.4 3.0 %collective-permute-done.5.refs_2_ = bf16[2,96,768]{2,1,0:T(8,128)(2,1)S(1)} collective-permute-done((bf16[2,96,768]{2,1,0:T(8,128)(2,1)S(1)}, bf16[2,96,768]{2,1,0:T(8,128)(2,1)S(1)}, u32[]{:S(2)}, u32[]{:S(2)}) %collective-permute-start.5) | collective-permute-done | bytes 294944 | tf_op jit(solution)/shard_map/ppermute | solution.py:585
  30.2 6.2 %collective-permute-done.9.pair.refs_3_ = bf16[2,96,768]{2,1,0:T(8,128)(2,1)S(1)} collective-permute-done((bf16[2,96,768]{2,1,0:T(8,128)(2,1)S(1)}, bf16[2,96,768]{2,1,0:T(8,128)(2,1)S(1)}, u32[]{:S(2)}, u32[]{:S(2)}) %collective-permute-start.9) | collective-permute-done | bytes 294944 | tf_op jit(solution)/shard_map/ppermute | solution.py:585
  40.2 7.7 %collective-permute-done.13.refs_7_ = bf16[96,768]{1,0:T(8,128)(2,1)S(1)} collective-permute-done((bf16[96,768]{1,0:T(8,128)(2,1)S(1)}, bf16[96,768]{1,0:T(8,128)(2,1)S(1)}, u32[]{:S(2)}, u32[]{:S(2)}) %collective-permute-start.13) | collective-permute-done | bytes 147488 | tf_op jit(solution)/shard_map/ppermute | solution.py:585
  47.9 3.2 %self_forward.1 = (bf16[768,768]{1,0:T(8,128)(2,1)S(1)}, bf16[256,768]{1,0:T(8,128)(2,1)S(1)}, bf16[128,768]{1,0:T(8,128)(2,1)S(1)}, bf16[128,768]{1,0:T(8,128)(2,1)S(1)}) custom-call(s32[4]{0:T(128)S(1)} %copy-done.13, bf16[256,768]{1,0:T(8,128)(2,1)S(1)} %bitcast.10, f32[3,768]{1,0:T(4,128)S(1)} %copy-done.3, f32[3,768]{1,0:T(4,128)S(1)} %copy-done.4, ...), custom_call_target="tpu_custom_call" | custom-call | flops 1 | bytes 10000000 | tf_op jit(solution)/shard_map/self_forward/pallas_call | solution.py:684
  56.4 3.6 %collective-permute-done.18.refs_7_ = bf16[96,768]{1,0:T(8,128)(2,1)S(1)} collective-permute-done((bf16[96,768]{1,0:T(8,128)(2,1)S(1)}, bf16[96,768]{1,0:T(8,128)(2,1)S(1)}, u32[]{:S(2)}, u32[]{:S(2)}) %collective-permute-start.18) | collective-permute-done | bytes 147488 | tf_op jit(solution)/shard_map/ppermute | solution.py:585
  60.0 2.9 %keyval.3 = (bf16[768,192]{1,0:T(8,128)(2,1)S(1)}, bf16[768,192]{1,0:T(8,128)(2,1)S(1)}, bf16[768,192]{1,0:T(8,128)(2,1)S(1)}, bf16[768,192]{1,0:T(8,128)(2,1)S(...) custom-call(bf16[2304,768]{1,0:T(8,128)(2,1)S(1)} %bitcast.8, ...), custom_call_target="tpu_custom_call" | custom-call | flops 1 | bytes 10000000 | tf_op jit(solution)/shard_map/keyval/pallas_call | solution.py:708
  66.3 3.0 %cross_forward.1 = (bf16[256,768]{1,0:T(8,128)(2,1)S(1)}, bf16[256,192]{1,0:T(8,128)(2,1)S(1)}, f32[4,192,576]{2,1,0:T(8,128)S(1)}, bf16[256,192]{1,0:T(8,128)(2...) custom-call(s32[4]{0:T(128)S(1)} %copy-done.14, bf16[128,768]{1,0:T(8,128)(2,1)S(1)} %get-tuple-element.143.own, ...), custom_call_target="tpu_custom_call" | custom-call | flops 1 | bytes 5505025 | tf_op jit(solution)/shard_map/cross_forward/pallas_call | solution.py:69
  70.1 3.1 %collective-permute-done.25.pair.refs_3_ = bf16[2,96,1536]{2,1,0:T(8,128)(2,1)S(1)} collective-permute-done((bf16[2,96,1536]{2,1,0:T(8,128)(2,1)S(1)}, bf16[2,96,1536]{2,1,0:T(8,128)(2,1)S(1)}, u32[]{:S(2)}, u32[]{:S(2)}) %collective-permute-start.25) | collective-permute-done | bytes 589856 | tf_op jit(solution)/shard_map/ppermute | solution.py:585
  73.3 2.3 %collective-permute-start.29 = (bf16[96,1536]{1,0:T(8,128)(2,1)S(1)}, bf16[96,1536]{1,0:T(8,128)(2,1)S(1)}, u32[]{:S(2)}, u32[]{:S(2)}) collective-permute-start(bf16[96,1536]{1,0:T(8,128)(2,1)S(1)} %takeF.1), channel_id=1, source_target_pairs={{0,8},{1,5},{2,10},{3,7},{8,16},{9,1},{10,18},{11,3},{16,24},{17,9... | collective-permute-start | bytes 884744 | tf_op jit(solution)/shard_map/ppermute | solution.py:585
  75.6 5.0 %collective-permute-done.23.other = bf16[128,768]{1,0:T(8,128)(2,1)S(1)} collective-permute-done((bf16[128,768]{1,0:T(8,128)(2,1)S(1)}, bf16[128,768]{1,0:T(8,128)(2,1)S(1)}, u32[]{:S(2)}, u32[]{:S(2)}) %collective-permute-start.23) | collective-permute-done | bytes 196640 | tf_op jit(solution)/shard_map/ppermute | solution.py:535
  94.3 2.9 %cross_back.1 = (bf16[256,768]{1,0:T(8,128)(2,1)S(1)}, bf16[256,192]{1,0:T(8,128)(2,1)S(1)}, bf16[192,2304]{1,0:T(8,128)(2,1)S(1)}, bf16[192,2304]{1,0:T(8,128)(...) custom-call(bf16[128,768]{1,0:T(8,128)(2,1)S(1)} %get-tuple-element.167.own, ...), custom_call_target="tpu_custom_call" | custom-call | flops 1 | bytes 7274497 | tf_op jit(solution)/shard_map/cross_back/pallas_call | solution.py:69
  109.6 4.3 %self_back.1 = (bf16[4,96,768]{2,1,0:T(8,128)(2,1)S(1)}, bf16[4,96,768]{2,1,0:T(8,128)(2,1)S(1)}, bf16[144,768]{1,0:T(8,128)(2,1)S(1)}, bf16[144,768]{1,0:T(8,128)(2,1)S(1)}) custom-call(s32[4]{0:T(128)S(1)} %copy-done.13, bf16[128,768]{1,0:T(8,128)(2,1)S(1)} %get-tuple-element.191.own, bf16[128,768]{1,0:T(8,128)(2,1)S(1)} %collective-permute-done.37.other, ...), custom_call_target="tpu_custom_call" | custom-call | flops 1 | bytes 4051969 | tf_op jit(solution)/shard_map/self_back/pallas_call | solution.py:69
  117.7 2.6 %collective-permute-start.44 = (bf16[2,96,768]{2,1,0:T(8,128)(2,1)S(1)}, bf16[2,96,768]{2,1,0:T(8,128)(2,1)S(1)}, u32[]{:S(2)}, u32[]{:S(2)}) collective-permute-start(bf16[2,96,768]{2,1,0:T(8,128)(2,1)S(1)} %get-tuple-element.213), channel_id=1, source_target_pairs={{0,16},{4,20},{8,24},{12,28},{16,0},{20,4},{24,8},{28,12},{1,17},{... | collective-permute-start | bytes 884744 | tf_op jit(solution)/shard_map/ppermute | solution.py:535
  120.3 2.7 %collective-permute-done.41.other = bf16[144,768]{1,0:T(8,128)(2,1)S(1)} collective-permute-done((bf16[144,768]{1,0:T(8,128)(2,1)S(1)}, bf16[144,768]{1,0:T(8,128)(2,1)S(1)}, u32[]{:S(2)}, u32[]{:S(2)}) %collective-permute-start.41) | collective-permute-done | bytes 221216 | tf_op jit(solution)/shard_map/ppermute | solution.py:535
  124.7 6.4 %collective-permute-done.43.other = bf16[2,96,768]{2,1,0:T(8,128)(2,1)S(1)} collective-permute-done((bf16[2,96,768]{2,1,0:T(8,128)(2,1)S(1)}, bf16[2,96,768]{2,1,0:T(8,128)(2,1)S(1)}, u32[]{:S(2)}, u32[]{:S(2)}) %collective-permute-start.43) | collective-permute-done | bytes 294944 | tf_op jit(solution)/shard_map/ppermute | solution.py:535
  134.6 2.8 %collective-permute-done.47.vec_other = bf16[16,768]{1,0:T(8,128)(2,1)S(1)} collective-permute-done((bf16[16,768]{1,0:T(8,128)(2,1)S(1)}, bf16[16,768]{1,0:T(8,128)(2,1)S(1)}, u32[]{:S(2)}, u32[]{:S(2)}) %collective-permute-start.47) | collective-permute-done | bytes 24608 | tf_op jit(solution)/shard_map/ppermute | solution.py:535
  137.3 3.4 %collective-permute-start.48 = (bf16[2,96,768]{2,1,0:T(8,128)(2,1)S(1)}, bf16[2,96,768]{2,1,0:T(8,128)(2,1)S(1)}, u32[]{:S(2)}, u32[]{:S(2)}) collective-permute-start(bf16[2,96,768]{2,1,0:T(8,128)(2,1)S(1)} %get-tuple-element.224), channel_id=1, source_target_pairs={{0,8},{4,12},{8,0},{12,4},{16,24},{20,28},{24,16},{28,20},{1,9},{5... | collective-permute-start | bytes 884744 | tf_op jit(solution)/shard_map/ppermute | solution.py:535
  143.6 3.9 %collective-permute-done.50.other = bf16[96,768]{1,0:T(8,128)(2,1)S(1)} collective-permute-done((bf16[96,768]{1,0:T(8,128)(2,1)S(1)}, bf16[96,768]{1,0:T(8,128)(2,1)S(1)}, u32[]{:S(2)}, u32[]{:S(2)}) %collective-permute-start.50) | collective-permute-done | bytes 147488 | tf_op jit(solution)/shard_map/ppermute | solution.py:535
  147.5 2.2 %collective-permute-done.52.other = bf16[128,768]{1,0:T(8,128)(2,1)S(1)} collective-permute-done((bf16[128,768]{1,0:T(8,128)(2,1)S(1)}, bf16[128,768]{1,0:T(8,128)(2,1)S(1)}, u32[]{:S(2)}, u32[]{:S(2)}) %collective-permute-start.52) | collective-permute-done | bytes 196640 | tf_op jit(solution)/shard_map/ppermute | solution.py:535
  154.6 3.4 %collective-permute-start.59 = (bf16[112,768]{1,0:T(8,128)(2,1)S(1)}, bf16[112,768]{1,0:T(8,128)(2,1)S(1)}, u32[]{:S(2)}, u32[]{:S(2)}) collective-permute-start(bf16[112,768]{1,0:T(8,128)(2,1)S(1)} %get-tuple-element.246), channel_id=1, source_target_pairs={{0,16},{4,20},{8,24},{12,28},{16,0},{20,4},{24,8},{28,12},{1,17},{... | collective-permute-start | bytes 516104 | tf_op jit(solution)/shard_map/ppermute | solution.py:535
  158.1 13.9 %collective-permute-done.55.refs_1_ = bf16[96,768]{1,0:T(8,128)(2,1)S(1)} collective-permute-done((bf16[96,768]{1,0:T(8,128)(2,1)S(1)}, bf16[96,768]{1,0:T(8,128)(2,1)S(1)}, u32[]{:S(2)}, u32[]{:S(2)}) %collective-permute-start.55) | collective-permute-done | bytes 147488 | tf_op jit(solution)/shard_map/ppermute | solution.py:535
  (175 shorter events, 77.0 us)
Async XLA Ops:
  23.4 13.0 %collective-permute-start.6 = (bf16[2,96,1536]{2,1,0:T(8,128)(2,1)S(1)}, bf16[2,96,1536]{2,1,0:T(8,128)(2,1)S(1)}, u32[]{:S(2)}, u32[]{:S(2)}) collective-permute-start(bf16[2,96,1536]{2,1,0:T(8,128)(2,1)S(1)} %pairF.1), channel_id=1, source_target_pairs={{0,8},{1,5},{2,10},{3,7},{8,16},{9,1},{10,18},{11,3},{16,24},{17,9... | collective-permute-start | bytes 1769480 | tf_op jit(solution)/shard_map/ppermute | solution.py:585
  28.7 11.5 %collective-permute-start.7 = (bf16[2,96,768]{2,1,0:T(8,128)(2,1)S(1)}, bf16[2,96,768]{2,1,0:T(8,128)(2,1)S(1)}, u32[]{:S(2)}, u32[]{:S(2)}) collective-permute-start(bf16[2,96,768]{2,1,0:T(8,128)(2,1)S(1)} %collective-permute-done.5.refs_2_), channel_id=1, source_target_pairs={{0,8},{1,5},{2,10},{3,7},{8,16},{9,1},{10,18},{11,3},{16,24},{17,9... | collective-permute-start | bytes 884744 | tf_op jit(solution)/shard_map/ppermute | solution.py:585
  30.2 10.0 %collective-permute-start.11 = (bf16[2,96,768]{2,1,0:T(8,128)(2,1)S(1)}, bf16[2,96,768]{2,1,0:T(8,128)(2,1)S(1)}, u32[]{:S(2)}, u32[]{:S(2)}) collective-permute-start(bf16[2,96,768]{2,1,0:T(8,128)(2,1)S(1)} %collective-permute-done.8.refs_2_), channel_id=1, source_target_pairs={{0,1},{1,0},{2,3},{3,2},{4,5},{5,4},{6,7},{7,6},{8,9},{9,8},{10,11... | collective-permute-start | bytes 884744 | tf_op jit(solution)/shard_map/ppermute | solution.py:535
  36.4 11.5 %collective-permute-start.12 = (bf16[2,96,768]{2,1,0:T(8,128)(2,1)S(1)}, bf16[2,96,768]{2,1,0:T(8,128)(2,1)S(1)}, u32[]{:S(2)}, u32[]{:S(2)}) collective-permute-start(bf16[2,96,768]{2,1,0:T(8,128)(2,1)S(1)} %collective-permute-done.9.pair.refs_3_), channel_id=1, source_target_pairs={{0,1},{1,0},{2,3},{3,2},{4,5},{5,4},{6,7},{7,6},{8,9},{9,8},{10,11... | collective-permute-start | bytes 884744 | tf_op jit(solution)/shard_map/ppermute | solution.py:535
  36.4 26.5 %collective-permute-start.19 = (bf16[2,96,1536]{2,1,0:T(8,128)(2,1)S(1)}, bf16[2,96,1536]{2,1,0:T(8,128)(2,1)S(1)}, u32[]{:S(2)}, u32[]{:S(2)}) collective-permute-start(bf16[2,96,1536]{2,1,0:T(8,128)(2,1)S(1)} %collective-permute-done.6.refs_1_), channel_id=1, source_target_pairs={{0,8},{1,5},{2,10},{3,7},{8,16},{9,1},{10,18},{11,3},{16,24},{17,9... | collective-permute-start | bytes 1769480 | tf_op jit(solution)/shard_map/ppermute | solution.py:585
  40.2 14.6 %collective-permute-start.15 = (bf16[2,96,768]{2,1,0:T(8,128)(2,1)S(1)}, bf16[2,96,768]{2,1,0:T(8,128)(2,1)S(1)}, u32[]{:S(2)}, u32[]{:S(2)}) collective-permute-start(bf16[2,96,768]{2,1,0:T(8,128)(2,1)S(1)} %collective-permute-done.4.refs_1_), channel_id=1, source_target_pairs={{0,1},{1,0},{2,3},{3,2},{4,5},{5,4},{6,7},{7,6},{8,9},{9,8},{10,11... | collective-permute-start | bytes 884744 | tf_op jit(solution)/shard_map/ppermute | solution.py:535
  52.7 10.3 %collective-permute-start.20 = (bf16[128,768]{1,0:T(8,128)(2,1)S(1)}, bf16[128,768]{1,0:T(8,128)(2,1)S(1)}, u32[]{:S(2)}, u32[]{:S(2)}) collective-permute-start(bf16[128,768]{1,0:T(8,128)(2,1)S(1)} %add_pair.6.chip), channel_id=1, source_target_pairs={{0,2},{1,3},{2,0},{3,1},{4,6},{5,7},{6,4},{7,5},{8,10},{9,11},{10,... | collective-permute-start | bytes 589832 | tf_op jit(solution)/shard_map/ppermute | solution.py:535
  63.2 9.9 %collective-permute-start.25 = (bf16[2,96,1536]{2,1,0:T(8,128)(2,1)S(1)}, bf16[2,96,1536]{2,1,0:T(8,128)(2,1)S(1)}, u32[]{:S(2)}, u32[]{:S(2)}) collective-permute-start(bf16[2,96,1536]{2,1,0:T(8,128)(2,1)S(1)} %collective-permute-done.19.refs_2_), channel_id=1, source_target_pairs={{0,8},{1,5},{2,10},{3,7},{8,16},{9,1},{10,18},{11,3},{16,24},{17,9... | collective-permute-start | bytes 1769480 | tf_op jit(solution)/shard_map/ppermute | solution.py:585
  69.6 11.4 %collective-permute-start.26 = (bf16[2,96,1536]{2,1,0:T(8,128)(2,1)S(1)}, bf16[2,96,1536]{2,1,0:T(8,128)(2,1)S(1)}, u32[]{:S(2)}, u32[]{:S(2)}) collective-permute-start(bf16[2,96,1536]{2,1,0:T(8,128)(2,1)S(1)} %collective-permute-done.6.refs_1_), channel_id=1, source_target_pairs={{0,1},{1,0},{2,3},{3,2},{4,5},{5,4},{6,7},{7,6},{8,9},{9,8},{10,11... | collective-permute-start | bytes 1769480 | tf_op jit(solution)/shard_map/ppermute | solution.py:535
  69.9 11.0 %collective-permute-start.27 = (bf16[2,96,1536]{2,1,0:T(8,128)(2,1)S(1)}, bf16[2,96,1536]{2,1,0:T(8,128)(2,1)S(1)}, u32[]{:S(2)}, u32[]{:S(2)}) collective-permute-start(bf16[2,96,1536]{2,1,0:T(8,128)(2,1)S(1)} %collective-permute-done.19.refs_2_), channel_id=1, source_target_pairs={{0,1},{1,0},{2,3},{3,2},{4,5},{5,4},{6,7},{7,6},{8,9},{9,8},{10,11... | collective-permute-start | bytes 1769480 | tf_op jit(solution)/shard_map/ppermute | solution.py:535
  87.1 15.2 %collective-permute-start.34 = (bf16[4,96,768]{2,1,0:T(8,128)(2,1)S(1)}, bf16[4,96,768]{2,1,0:T(8,128)(2,1)S(1)}, u32[]{:S(2)}, u32[]{:S(2)}) collective-permute-start(bf16[4,96,768]{2,1,0:T(8,128)(2,1)S(1)} %get-tuple-element.162), channel_id=1, source_target_pairs={{0,8},{4,12},{8,0},{12,4},{16,24},{20,28},{24,16},{28,20},{1,9},{5... | collective-permute-start | bytes 1769480 | tf_op jit(solution)/shard_map/ppermute | solution.py:535
  88.7 14.8 %collective-permute-start.35 = (bf16[4,96,768]{2,1,0:T(8,128)(2,1)S(1)}, bf16[4,96,768]{2,1,0:T(8,128)(2,1)S(1)}, u32[]{:S(2)}, u32[]{:S(2)}) collective-permute-start(bf16[4,96,768]{2,1,0:T(8,128)(2,1)S(1)} %get-tuple-element.164), channel_id=1, source_target_pairs={{0,4},{4,0},{8,12},{12,8},{16,20},{20,16},{24,28},{28,24},{1,5},{5... | collective-permute-start | bytes 1769480 | tf_op jit(solution)/shard_map/ppermute | solution.py:535
  107.8 16.2 %collective-permute-start.42 = (bf16[4,96,768]{2,1,0:T(8,128)(2,1)S(1)}, bf16[4,96,768]{2,1,0:T(8,128)(2,1)S(1)}, u32[]{:S(2)}, u32[]{:S(2)}) collective-permute-start(bf16[4,96,768]{2,1,0:T(8,128)(2,1)S(1)} %get-tuple-element.188), channel_id=1, source_target_pairs={{0,4},{4,0},{8,12},{12,8},{16,20},{20,16},{24,28},{28,24},{1,5},{5... | collective-permute-start | bytes 1769480 | tf_op jit(solution)/shard_map/ppermute | solution.py:535
  114.1 26.7 %collective-permute-start.46 = (bf16[4,96,768]{2,1,0:T(8,128)(2,1)S(1)}, bf16[4,96,768]{2,1,0:T(8,128)(2,1)S(1)}, u32[]{:S(2)}, u32[]{:S(2)}) collective-permute-start(bf16[4,96,768]{2,1,0:T(8,128)(2,1)S(1)} %get-tuple-element.220), channel_id=1, source_target_pairs={{0,4},{4,0},{8,12},{12,8},{16,20},{20,16},{24,28},{28,24},{1,5},{5... | collective-permute-start | bytes 1769480 | tf_op jit(solution)/shard_map/ppermute | solution.py:535
  116.2 15.0 %collective-permute-start.43 = (bf16[2,96,768]{2,1,0:T(8,128)(2,1)S(1)}, bf16[2,96,768]{2,1,0:T(8,128)(2,1)S(1)}, u32[]{:S(2)}, u32[]{:S(2)}) collective-permute-start(bf16[2,96,768]{2,1,0:T(8,128)(2,1)S(1)} %get-tuple-element.210), channel_id=1, source_target_pairs={{0,8},{4,12},{8,0},{12,4},{16,24},{20,28},{24,16},{28,20},{1,9},{5... | collective-permute-start | bytes 884744 | tf_op jit(solution)/shard_map/ppermute | solution.py:535
  117.7 15.8 %collective-permute-start.44 = (bf16[2,96,768]{2,1,0:T(8,128)(2,1)S(1)}, bf16[2,96,768]{2,1,0:T(8,128)(2,1)S(1)}, u32[]{:S(2)}, u32[]{:S(2)}) collective-permute-start(bf16[2,96,768]{2,1,0:T(8,128)(2,1)S(1)} %get-tuple-element.213), channel_id=1, source_target_pairs={{0,16},{4,20},{8,24},{12,28},{16,0},{20,4},{24,8},{28,12},{1,17},{... | collective-permute-start | bytes 884744 | tf_op jit(solution)/shard_map/ppermute | solution.py:535
  124.0 48.9 %collective-permute-start.58 = (bf16[192,2304]{1,0:T(8,128)(2,1)S(1)}, bf16[192,2304]{1,0:T(8,128)(2,1)S(1)}, u32[]{:S(2)}, u32[]{:S(2)}) collective-permute-start(bf16[192,2304]{1,0:T(8,128)(2,1)S(1)} %image_chip.1), channel_id=1, source_target_pairs={{0,2},{1,3},{2,0},{3,1},{4,6},{5,7},{6,4},{7,5},{8,10},{9,11},{10,... | collective-permute-start | bytes 2654216 | tf_op jit(solution)/shard_map/ppermute | solution.py:535
  131.2 11.1 %collective-permute-start.49 = (bf16[96,768]{1,0:T(8,128)(2,1)S(1)}, bf16[96,768]{1,0:T(8,128)(2,1)S(1)}, u32[]{:S(2)}, u32[]{:S(2)}) collective-permute-start(bf16[96,768]{1,0:T(8,128)(2,1)S(1)} %get-tuple-element.227), channel_id=1, source_target_pairs={{0,16},{4,20},{8,24},{12,28},{16,0},{20,4},{24,8},{28,12},{1,17},{... | collective-permute-start | bytes 442376 | tf_op jit(solution)/shard_map/ppermute | solution.py:535
  131.9 20.1 %collective-permute-start.51 = (f32[128,768]{1,0:T(8,128)S(1)}, f32[128,768]{1,0:T(8,128)S(1)}, u32[]{:S(2)}, u32[]{:S(2)}) collective-permute-start(f32[128,768]{1,0:T(8,128)S(1)} %get-tuple-element.230.own), channel_id=1, source_target_pairs={{0,1},{1,0},{2,3},{3,2},{4,5},{5,4},{6,7},{7,6},{8,9},{9,8},{10,11... | collective-permute-start | bytes 1179656 | tf_op jit(solution)/shard_map/ppermute | solution.py:535
  137.3 12.4 %collective-permute-start.48 = (bf16[2,96,768]{2,1,0:T(8,128)(2,1)S(1)}, bf16[2,96,768]{2,1,0:T(8,128)(2,1)S(1)}, u32[]{:S(2)}, u32[]{:S(2)}) collective-permute-start(bf16[2,96,768]{2,1,0:T(8,128)(2,1)S(1)} %get-tuple-element.224), channel_id=1, source_target_pairs={{0,8},{4,12},{8,0},{12,4},{16,24},{20,28},{24,16},{28,20},{1,9},{5... | collective-permute-start | bytes 884744 | tf_op jit(solution)/shard_map/ppermute | solution.py:535
  149.7 23.1 %collective-permute-start.56 = (bf16[192,1152]{1,0:T(8,128)(2,1)S(1)}, bf16[192,1152]{1,0:T(8,128)(2,1)S(1)}, u32[]{:S(2)}, u32[]{:S(2)}) collective-permute-start(bf16[192,1152]{1,0:T(8,128)(2,1)S(1)} %get-tuple-element.242), channel_id=1, source_target_pairs={{0,1},{1,0},{2,3},{3,2},{4,5},{5,4},{6,7},{7,6},{8,9},{9,8},{10,11... | collective-permute-start | bytes 1327112 | tf_op jit(solution)/shard_map/ppermute | solution.py:535
  149.8 23.1 %collective-permute-start.57 = (bf16[192,1152]{1,0:T(8,128)(2,1)S(1)}, bf16[192,1152]{1,0:T(8,128)(2,1)S(1)}, u32[]{:S(2)}, u32[]{:S(2)}) collective-permute-start(bf16[192,1152]{1,0:T(8,128)(2,1)S(1)} %get-tuple-element.243), channel_id=1, source_target_pairs={{0,1},{1,0},{2,3},{3,2},{4,5},{5,4},{6,7},{7,6},{8,9},{9,8},{10,11... | collective-permute-start | bytes 1327112 | tf_op jit(solution)/shard_map/ppermute | solution.py:535
  154.6 20.0 %collective-permute-start.59 = (bf16[112,768]{1,0:T(8,128)(2,1)S(1)}, bf16[112,768]{1,0:T(8,128)(2,1)S(1)}, u32[]{:S(2)}, u32[]{:S(2)}) collective-permute-start(bf16[112,768]{1,0:T(8,128)(2,1)S(1)} %get-tuple-element.246), channel_id=1, source_target_pairs={{0,16},{4,20},{8,24},{12,28},{16,0},{20,4},{24,8},{28,12},{1,17},{... | collective-permute-start | bytes 516104 | tf_op jit(solution)/shard_map/ppermute | solution.py:535
  158.0 14.0 %collective-permute-start.55 = (bf16[96,768]{1,0:T(8,128)(2,1)S(1)}, bf16[96,768]{1,0:T(8,128)(2,1)S(1)}, u32[]{:S(2)}, u32[]{:S(2)}) collective-permute-start(bf16[96,768]{1,0:T(8,128)(2,1)S(1)} %get-tuple-element.239), channel_id=1, source_target_pairs={{0,16},{4,20},{8,24},{12,28},{16,0},{20,4},{24,8},{28,12},{1,17},{... | collective-permute-start | bytes 442376 | tf_op jit(solution)/shard_map/ppermute | solution.py:535
  (52 other events, 438.2 us)

commit v4 on v3

--- a/solution.py
+++ b/solution.py
@@ -87,6 +87,7 @@
 
 X_FIRST = (1, 2, 4)
 Z_FIRST = (2, 4, 1)
+X_THEN_FAR = (1, 4, 2)
 
 
 def block_rows(turn, height):
@@ -351,13 +352,13 @@
     outs, turned = refs[:parts], refs[parts]
     width = dq.shape[1]
     turned[...] = tn(normed[...], dq[...])
-    scatter_blocks(turned, 0, outs)
+    scatter_blocks(turned, 0, outs, X_THEN_FAR)
     turned[...] = nn(dkt[...], image[...]).T
-    scatter_blocks(turned, width, outs)
+    scatter_blocks(turned, width, outs, X_THEN_FAR)
     turned[...] = nn(dvt[...], image[...]).T
-    scatter_blocks(turned, 2 * width, outs)
+    scatter_blocks(turned, 2 * width, outs, X_THEN_FAR)
     turned[...] = tn(grad_two[...], ctx[...])
-    scatter_blocks(turned, 3 * width, outs)
+    scatter_blocks(turned, 3 * width, outs, X_THEN_FAR)
 
 
 def image_part_kernel(dkt, dvt, wk, wv, away_one, away_two, own_one, own_two, keep_away, keep_own):
@@ -874,7 +875,7 @@
         (chip, other, text, grad_one, norm_gain),
     )
     image_away = level_swap(gate(chip_away, vec))
-    cross_sums = fold(cross_sums, 2, "fold_cross", vec)
+    cross_sums = fold(cross_sums, 4, "fold_cross", vec)
     down_sums = fold(down_sums, 4, "fold_down", cross_sums[0])
     up_sums = fold(up_sums, 1, "fold_up", down_sums[0])
     out_chip = add_pair(gate(out_keep, up_sums[0]), core_swap(out_send))
@@ -890,7 +891,7 @@
         )
         self_sums = near, swap(send, "dp", 8, 2)
         cross_sums = gate(cross_sums[0], near), cross_sums[1]
-    cross_sums = fold(cross_sums, 4, "fold_cross", *self_sums[:1])
+    cross_sums = fold(cross_sums, 2, "fold_cross", *self_sums[:1])
     if quick:
         close = lambda sums, first, name: call(
             close_ffn_kernel, name, [((height, hidden), F32)], (), (gate(sums[0], first), sums[1])
@@ -924,20 +925,21 @@
             (gate(self_sums[0], text_grad), self_sums[1], vec),
         )
         self_sums = near, swap(send, "dp", 8, 4)
+    (image_grad,) = call(
+        image_sum_kernel,
+        "image_sum",
+        [((seqs, width, patches), F32)],
+        (),
+        (gate(keep_own, near if quick else text_grad), core_swap(own_one), core_swap(own_two), image_away),
+    )
+    if quick:
         query_grad, keyval_grad, cross_out_grad = call(
             close_cross_kernel,
             "close_cross",
             [((height, width), F32), ((2, height, width), F32), ((width, height), F32)],
             (),
-            (gate(cross_sums[0], near), cross_sums[1]),
+            (gate(cross_sums[0], image_grad), cross_sums[1]),
         )
-    (image_grad,) = call(
-        image_sum_kernel,
-        "image_sum",
-        [((seqs, width, patches), F32)],
-        (),
-        (gate(keep_own, query_grad) if quick else keep_own, core_swap(own_one), core_swap(own_two), image_away),
-    )
     vec_outs = [((3, model), F32)] * 3 + [((hidden,), F32)]
     if quick:
         qkv_grad, self_out_grad, gains, shifts, biases, ups = call(
@@ -945,7 +947,7 @@
             "close_self",
             [((3, height, width), F32), ((width, height), F32)] + vec_outs,
             (),
-            (gate(self_sums[0], image_grad), self_sums[1], vec),
+            (gate(self_sums[0], query_grad), self_sums[1], vec),
         )
     else:
         gains, shifts, biases, ups = call(

time: 176 us -> 171 us (0.972)
  waiting for transfers between devices: 83.4 us -> 77.8 us
    ppermute x48, waiting for transfers between devices: 52.8 us -> 47.2 us  [swap(): return lax.ppermute(value, axis, [(i, i ^ bits) for i in range(size)])]
  transfers between devices with their start and end apart: 60 -> 60, of which waited for: 28 -> 31; matrix products, arithmetic and copies ran while one was open for 0% -> 0% of each run, Pallas kernels for 17% -> 18%
where the time goes in v4:
time: 171 us; the launch traced here: 170 us
  waiting for transfers between devices  77.8 us (45%)
  starting transfers between devices  53.8 us (31%)
  Pallas kernels  33.3 us (19%)
  local copies, waits for them, and re-layouts  4.25 us (2%)
    ppermute x48, waiting for transfers between devices, swap(): return lax.ppermute(value, axis, [(i, i ^ bits) for i in range(size)])  47.2 us
    ppermute x12, waiting for transfers between devices, around(): return lax.ppermute(value, ('dp', 'mp'), turns)  30.6 us
    ppermute x48, starting transfers between devices, swap(): return lax.ppermute(value, axis, [(i, i ^ bits) for i in range(size)])  30.4 us
    pallas_call x44, Pallas kernels, call(): pl.pallas_call(body, out_shape=[jax.ShapeDtypeStruct(s, d) for s, d in ou...  27.2 us
    ppermute x12, starting transfers between devices, around(): return lax.ppermute(value, ('dp', 'mp'), turns)  23.4 us
    unnamed x32, local copies, waits for them, and re-layouts  4.25 us
  transfers between devices with their start and end apart: 60, of which 31 were waited for; matrix products, arithmetic and copies ran while one was open for 0% of the time, Pallas kernels for 18%

profile of v4, /device:TPU:0, one launch (start us, length us, event | category | flops | bytes accessed | tf_op | source)
XLA Modules:
  0.0 170.3 jit_solution(4410263554685361283)
XLA Ops:
  5.9 3.0 %collective-permute-start.1 = (bf16[2,96,768]{2,1,0:T(8,128)(2,1)S(1)}, bf16[2,96,768]{2,1,0:T(8,128)(2,1)S(1)}, u32[]{:S(2)}, u32[]{:S(2)}) collective-permute-start(bf16[2,96,768]{2,1,0:T(8,128)(2,1)S(1)} %pairA.1), channel_id=1, source_target_pairs={{0,8},{1,5},{2,10},{3,7},{8,16},{9,1},{10,18},{11,3},{16,24},{17,9... | collective-permute-start | bytes 884744 | tf_op jit(solution)/shard_map/ppermute | solution.py:586
  10.6 2.9 %collective-permute-done.1.refs_1_ = bf16[2,96,768]{2,1,0:T(8,128)(2,1)S(1)} collective-permute-done((bf16[2,96,768]{2,1,0:T(8,128)(2,1)S(1)}, bf16[2,96,768]{2,1,0:T(8,128)(2,1)S(1)}, u32[]{:S(2)}, u32[]{:S(2)}) %collective-permute-start.1) | collective-permute-done | bytes 294944 | tf_op jit(solution)/shard_map/ppermute | solution.py:586
  13.5 3.2 %collective-permute-done.4.refs_1_ = bf16[2,96,768]{2,1,0:T(8,128)(2,1)S(1)} collective-permute-done((bf16[2,96,768]{2,1,0:T(8,128)(2,1)S(1)}, bf16[2,96,768]{2,1,0:T(8,128)(2,1)S(1)}, u32[]{:S(2)}, u32[]{:S(2)}) %collective-permute-start.4) | collective-permute-done | bytes 294944 | tf_op jit(solution)/shard_map/ppermute | solution.py:586
  20.4 3.0 %collective-permute-done.5.refs_2_ = bf16[2,96,768]{2,1,0:T(8,128)(2,1)S(1)} collective-permute-done((bf16[2,96,768]{2,1,0:T(8,128)(2,1)S(1)}, bf16[2,96,768]{2,1,0:T(8,128)(2,1)S(1)}, u32[]{:S(2)}, u32[]{:S(2)}) %collective-permute-start.5) | collective-permute-done | bytes 294944 | tf_op jit(solution)/shard_map/ppermute | solution.py:586
  30.2 6.2 %collective-permute-done.9.pair.refs_3_ = bf16[2,96,768]{2,1,0:T(8,128)(2,1)S(1)} collective-permute-done((bf16[2,96,768]{2,1,0:T(8,128)(2,1)S(1)}, bf16[2,96,768]{2,1,0:T(8,128)(2,1)S(1)}, u32[]{:S(2)}, u32[]{:S(2)}) %collective-permute-start.9) | collective-permute-done | bytes 294944 | tf_op jit(solution)/shard_map/ppermute | solution.py:586
  40.2 7.7 %collective-permute-done.13.refs_7_ = bf16[96,768]{1,0:T(8,128)(2,1)S(1)} collective-permute-done((bf16[96,768]{1,0:T(8,128)(2,1)S(1)}, bf16[96,768]{1,0:T(8,128)(2,1)S(1)}, u32[]{:S(2)}, u32[]{:S(2)}) %collective-permute-start.13) | collective-permute-done | bytes 147488 | tf_op jit(solution)/shard_map/ppermute | solution.py:586
  47.9 3.2 %self_forward.1 = (bf16[768,768]{1,0:T(8,128)(2,1)S(1)}, bf16[256,768]{1,0:T(8,128)(2,1)S(1)}, bf16[128,768]{1,0:T(8,128)(2,1)S(1)}, bf16[128,768]{1,0:T(8,128)(2,1)S(1)}) custom-call(s32[4]{0:T(128)S(1)} %copy-done.13, bf16[256,768]{1,0:T(8,128)(2,1)S(1)} %bitcast.10, f32[3,768]{1,0:T(4,128)S(1)} %copy-done.3, f32[3,768]{1,0:T(4,128)S(1)} %copy-done.4, ...), custom_call_target="tpu_custom_call" | custom-call | flops 1 | bytes 10000000 | tf_op jit(solution)/shard_map/self_forward/pallas_call | solution.py:685
  56.4 3.6 %collective-permute-done.18.refs_7_ = bf16[96,768]{1,0:T(8,128)(2,1)S(1)} collective-permute-done((bf16[96,768]{1,0:T(8,128)(2,1)S(1)}, bf16[96,768]{1,0:T(8,128)(2,1)S(1)}, u32[]{:S(2)}, u32[]{:S(2)}) %collective-permute-start.18) | collective-permute-done | bytes 147488 | tf_op jit(solution)/shard_map/ppermute | solution.py:586
  60.0 2.9 %keyval.3 = (bf16[768,192]{1,0:T(8,128)(2,1)S(1)}, bf16[768,192]{1,0:T(8,128)(2,1)S(1)}, bf16[768,192]{1,0:T(8,128)(2,1)S(1)}, bf16[768,192]{1,0:T(8,128)(2,1)S(...) custom-call(bf16[2304,768]{1,0:T(8,128)(2,1)S(1)} %bitcast.8, ...), custom_call_target="tpu_custom_call" | custom-call | flops 1 | bytes 10000000 | tf_op jit(solution)/shard_map/keyval/pallas_call | solution.py:709
  66.3 3.0 %cross_forward.1 = (bf16[256,768]{1,0:T(8,128)(2,1)S(1)}, bf16[256,192]{1,0:T(8,128)(2,1)S(1)}, f32[4,192,576]{2,1,0:T(8,128)S(1)}, bf16[256,192]{1,0:T(8,128)(2...) custom-call(s32[4]{0:T(128)S(1)} %copy-done.14, bf16[128,768]{1,0:T(8,128)(2,1)S(1)} %get-tuple-element.143.own, ...), custom_call_target="tpu_custom_call" | custom-call | flops 1 | bytes 5505025 | tf_op jit(solution)/shard_map/cross_forward/pallas_call | solution.py:69
  70.1 3.1 %collective-permute-done.25.pair.refs_3_ = bf16[2,96,1536]{2,1,0:T(8,128)(2,1)S(1)} collective-permute-done((bf16[2,96,1536]{2,1,0:T(8,128)(2,1)S(1)}, bf16[2,96,1536]{2,1,0:T(8,128)(2,1)S(1)}, u32[]{:S(2)}, u32[]{:S(2)}) %collective-permute-start.25) | collective-permute-done | bytes 589856 | tf_op jit(solution)/shard_map/ppermute | solution.py:586
  73.3 2.3 %collective-permute-start.29 = (bf16[96,1536]{1,0:T(8,128)(2,1)S(1)}, bf16[96,1536]{1,0:T(8,128)(2,1)S(1)}, u32[]{:S(2)}, u32[]{:S(2)}) collective-permute-start(bf16[96,1536]{1,0:T(8,128)(2,1)S(1)} %takeF.1), channel_id=1, source_target_pairs={{0,8},{1,5},{2,10},{3,7},{8,16},{9,1},{10,18},{11,3},{16,24},{17,9... | collective-permute-start | bytes 884744 | tf_op jit(solution)/shard_map/ppermute | solution.py:586
  75.6 5.0 %collective-permute-done.23.other = bf16[128,768]{1,0:T(8,128)(2,1)S(1)} collective-permute-done((bf16[128,768]{1,0:T(8,128)(2,1)S(1)}, bf16[128,768]{1,0:T(8,128)(2,1)S(1)}, u32[]{:S(2)}, u32[]{:S(2)}) %collective-permute-start.23) | collective-permute-done | bytes 196640 | tf_op jit(solution)/shard_map/ppermute | solution.py:536
  94.3 2.9 %cross_back.1 = (bf16[256,768]{1,0:T(8,128)(2,1)S(1)}, bf16[256,192]{1,0:T(8,128)(2,1)S(1)}, bf16[192,2304]{1,0:T(8,128)(2,1)S(1)}, bf16[192,2304]{1,0:T(8,128)(...) custom-call(bf16[128,768]{1,0:T(8,128)(2,1)S(1)} %get-tuple-element.167.own, ...), custom_call_target="tpu_custom_call" | custom-call | flops 1 | bytes 7274497 | tf_op jit(solution)/shard_map/cross_back/pallas_call | solution.py:69
  109.6 4.3 %self_back.1 = (bf16[4,96,768]{2,1,0:T(8,128)(2,1)S(1)}, bf16[4,96,768]{2,1,0:T(8,128)(2,1)S(1)}, bf16[144,768]{1,0:T(8,128)(2,1)S(1)}, bf16[144,768]{1,0:T(8,128)(2,1)S(1)}) custom-call(s32[4]{0:T(128)S(1)} %copy-done.13, bf16[128,768]{1,0:T(8,128)(2,1)S(1)} %get-tuple-element.191.own, bf16[128,768]{1,0:T(8,128)(2,1)S(1)} %collective-permute-done.37.other, ...), custom_call_target="tpu_custom_call" | custom-call | flops 1 | bytes 4051969 | tf_op jit(solution)/shard_map/self_back/pallas_call | solution.py:69
  117.7 2.6 %collective-permute-start.44 = (bf16[2,96,768]{2,1,0:T(8,128)(2,1)S(1)}, bf16[2,96,768]{2,1,0:T(8,128)(2,1)S(1)}, u32[]{:S(2)}, u32[]{:S(2)}) collective-permute-start(bf16[2,96,768]{2,1,0:T(8,128)(2,1)S(1)} %get-tuple-element.213), channel_id=1, source_target_pairs={{0,16},{4,20},{8,24},{12,28},{16,0},{20,4},{24,8},{28,12},{1,17},{... | collective-permute-start | bytes 884744 | tf_op jit(solution)/shard_map/ppermute | solution.py:536
  120.3 2.7 %collective-permute-done.41.other = bf16[144,768]{1,0:T(8,128)(2,1)S(1)} collective-permute-done((bf16[144,768]{1,0:T(8,128)(2,1)S(1)}, bf16[144,768]{1,0:T(8,128)(2,1)S(1)}, u32[]{:S(2)}, u32[]{:S(2)}) %collective-permute-start.41) | collective-permute-done | bytes 221216 | tf_op jit(solution)/shard_map/ppermute | solution.py:536
  124.7 6.4 %collective-permute-done.43.other = bf16[2,96,768]{2,1,0:T(8,128)(2,1)S(1)} collective-permute-done((bf16[2,96,768]{2,1,0:T(8,128)(2,1)S(1)}, bf16[2,96,768]{2,1,0:T(8,128)(2,1)S(1)}, u32[]{:S(2)}, u32[]{:S(2)}) %collective-permute-start.43) | collective-permute-done | bytes 294944 | tf_op jit(solution)/shard_map/ppermute | solution.py:536
  133.5 3.2 %collective-permute-done.47.vec_other = bf16[16,768]{1,0:T(8,128)(2,1)S(1)} collective-permute-done((bf16[16,768]{1,0:T(8,128)(2,1)S(1)}, bf16[16,768]{1,0:T(8,128)(2,1)S(1)}, u32[]{:S(2)}, u32[]{:S(2)}) %collective-permute-start.47) | collective-permute-done | bytes 24608 | tf_op jit(solution)/shard_map/ppermute | solution.py:536
  136.7 2.6 %collective-permute-start.48 = (bf16[2,96,768]{2,1,0:T(8,128)(2,1)S(1)}, bf16[2,96,768]{2,1,0:T(8,128)(2,1)S(1)}, u32[]{:S(2)}, u32[]{:S(2)}) collective-permute-start(bf16[2,96,768]{2,1,0:T(8,128)(2,1)S(1)} %get-tuple-element.224), channel_id=1, source_target_pairs={{0,16},{4,20},{8,24},{12,28},{16,0},{20,4},{24,8},{28,12},{1,17},{... | collective-permute-start | bytes 884744 | tf_op jit(solution)/shard_map/ppermute | solution.py:536
  141.7 4.0 %collective-permute-done.50.other = bf16[96,768]{1,0:T(8,128)(2,1)S(1)} collective-permute-done((bf16[96,768]{1,0:T(8,128)(2,1)S(1)}, bf16[96,768]{1,0:T(8,128)(2,1)S(1)}, u32[]{:S(2)}, u32[]{:S(2)}) %collective-permute-start.50) | collective-permute-done | bytes 147488 | tf_op jit(solution)/shard_map/ppermute | solution.py:536
  149.8 3.0 %collective-permute-done.48.other = bf16[2,96,768]{2,1,0:T(8,128)(2,1)S(1)} collective-permute-done((bf16[2,96,768]{2,1,0:T(8,128)(2,1)S(1)}, bf16[2,96,768]{2,1,0:T(8,128)(2,1)S(1)}, u32[]{:S(2)}, u32[]{:S(2)}) %collective-permute-start.48) | collective-permute-done | bytes 294944 | tf_op jit(solution)/shard_map/ppermute | solution.py:536
  160.2 2.5 %collective-permute-start.58 = (bf16[96,768]{1,0:T(8,128)(2,1)S(1)}, bf16[96,768]{1,0:T(8,128)(2,1)S(1)}, u32[]{:S(2)}, u32[]{:S(2)}) collective-permute-start(bf16[96,768]{1,0:T(8,128)(2,1)S(1)} %get-tuple-element.243), channel_id=1, source_target_pairs={{0,8},{4,12},{8,0},{12,4},{16,24},{20,28},{24,16},{28,20},{1,9},{5... | collective-permute-start | bytes 442376 | tf_op jit(solution)/shard_map/ppermute | solution.py:536
  164.5 2.7 %collective-permute-done.58.refs_1_ = bf16[96,768]{1,0:T(8,128)(2,1)S(1)} collective-permute-done((bf16[96,768]{1,0:T(8,128)(2,1)S(1)}, bf16[96,768]{1,0:T(8,128)(2,1)S(1)}, u32[]{:S(2)}, u32[]{:S(2)}) %collective-permute-start.58) | collective-permute-done | bytes 147488 | tf_op jit(solution)/shard_map/ppermute | solution.py:536
  (175 shorter events, 83.3 us)
Async XLA Ops:
  23.4 13.0 %collective-permute-start.6 = (bf16[2,96,1536]{2,1,0:T(8,128)(2,1)S(1)}, bf16[2,96,1536]{2,1,0:T(8,128)(2,1)S(1)}, u32[]{:S(2)}, u32[]{:S(2)}) collective-permute-start(bf16[2,96,1536]{2,1,0:T(8,128)(2,1)S(1)} %pairF.1), channel_id=1, source_target_pairs={{0,8},{1,5},{2,10},{3,7},{8,16},{9,1},{10,18},{11,3},{16,24},{17,9... | collective-permute-start | bytes 1769480 | tf_op jit(solution)/shard_map/ppermute | solution.py:586
  28.7 11.5 %collective-permute-start.7 = (bf16[2,96,768]{2,1,0:T(8,128)(2,1)S(1)}, bf16[2,96,768]{2,1,0:T(8,128)(2,1)S(1)}, u32[]{:S(2)}, u32[]{:S(2)}) collective-permute-start(bf16[2,96,768]{2,1,0:T(8,128)(2,1)S(1)} %collective-permute-done.5.refs_2_), channel_id=1, source_target_pairs={{0,8},{1,5},{2,10},{3,7},{8,16},{9,1},{10,18},{11,3},{16,24},{17,9... | collective-permute-start | bytes 884744 | tf_op jit(solution)/shard_map/ppermute | solution.py:586
  30.2 10.0 %collective-permute-start.11 = (bf16[2,96,768]{2,1,0:T(8,128)(2,1)S(1)}, bf16[2,96,768]{2,1,0:T(8,128)(2,1)S(1)}, u32[]{:S(2)}, u32[]{:S(2)}) collective-permute-start(bf16[2,96,768]{2,1,0:T(8,128)(2,1)S(1)} %collective-permute-done.8.refs_2_), channel_id=1, source_target_pairs={{0,1},{1,0},{2,3},{3,2},{4,5},{5,4},{6,7},{7,6},{8,9},{9,8},{10,11... | collective-permute-start | bytes 884744 | tf_op jit(solution)/shard_map/ppermute | solution.py:536
  36.4 11.5 %collective-permute-start.12 = (bf16[2,96,768]{2,1,0:T(8,128)(2,1)S(1)}, bf16[2,96,768]{2,1,0:T(8,128)(2,1)S(1)}, u32[]{:S(2)}, u32[]{:S(2)}) collective-permute-start(bf16[2,96,768]{2,1,0:T(8,128)(2,1)S(1)} %collective-permute-done.9.pair.refs_3_), channel_id=1, source_target_pairs={{0,1},{1,0},{2,3},{3,2},{4,5},{5,4},{6,7},{7,6},{8,9},{9,8},{10,11... | collective-permute-start | bytes 884744 | tf_op jit(solution)/shard_map/ppermute | solution.py:536
  36.4 26.5 %collective-permute-start.19 = (bf16[2,96,1536]{2,1,0:T(8,128)(2,1)S(1)}, bf16[2,96,1536]{2,1,0:T(8,128)(2,1)S(1)}, u32[]{:S(2)}, u32[]{:S(2)}) collective-permute-start(bf16[2,96,1536]{2,1,0:T(8,128)(2,1)S(1)} %collective-permute-done.6.refs_1_), channel_id=1, source_target_pairs={{0,8},{1,5},{2,10},{3,7},{8,16},{9,1},{10,18},{11,3},{16,24},{17,9... | collective-permute-start | bytes 1769480 | tf_op jit(solution)/shard_map/ppermute | solution.py:586
  40.2 14.6 %collective-permute-start.15 = (bf16[2,96,768]{2,1,0:T(8,128)(2,1)S(1)}, bf16[2,96,768]{2,1,0:T(8,128)(2,1)S(1)}, u32[]{:S(2)}, u32[]{:S(2)}) collective-permute-start(bf16[2,96,768]{2,1,0:T(8,128)(2,1)S(1)} %collective-permute-done.4.refs_1_), channel_id=1, source_target_pairs={{0,1},{1,0},{2,3},{3,2},{4,5},{5,4},{6,7},{7,6},{8,9},{9,8},{10,11... | collective-permute-start | bytes 884744 | tf_op jit(solution)/shard_map/ppermute | solution.py:536
  52.7 10.3 %collective-permute-start.20 = (bf16[128,768]{1,0:T(8,128)(2,1)S(1)}, bf16[128,768]{1,0:T(8,128)(2,1)S(1)}, u32[]{:S(2)}, u32[]{:S(2)}) collective-permute-start(bf16[128,768]{1,0:T(8,128)(2,1)S(1)} %add_pair.6.chip), channel_id=1, source_target_pairs={{0,2},{1,3},{2,0},{3,1},{4,6},{5,7},{6,4},{7,5},{8,10},{9,11},{10,... | collective-permute-start | bytes 589832 | tf_op jit(solution)/shard_map/ppermute | solution.py:536
  63.2 9.9 %collective-permute-start.25 = (bf16[2,96,1536]{2,1,0:T(8,128)(2,1)S(1)}, bf16[2,96,1536]{2,1,0:T(8,128)(2,1)S(1)}, u32[]{:S(2)}, u32[]{:S(2)}) collective-permute-start(bf16[2,96,1536]{2,1,0:T(8,128)(2,1)S(1)} %collective-permute-done.19.refs_2_), channel_id=1, source_target_pairs={{0,8},{1,5},{2,10},{3,7},{8,16},{9,1},{10,18},{11,3},{16,24},{17,9... | collective-permute-start | bytes 1769480 | tf_op jit(solution)/shard_map/ppermute | solution.py:586
  69.6 11.4 %collective-permute-start.26 = (bf16[2,96,1536]{2,1,0:T(8,128)(2,1)S(1)}, bf16[2,96,1536]{2,1,0:T(8,128)(2,1)S(1)}, u32[]{:S(2)}, u32[]{:S(2)}) collective-permute-start(bf16[2,96,1536]{2,1,0:T(8,128)(2,1)S(1)} %collective-permute-done.6.refs_1_), channel_id=1, source_target_pairs={{0,1},{1,0},{2,3},{3,2},{4,5},{5,4},{6,7},{7,6},{8,9},{9,8},{10,11... | collective-permute-start | bytes 1769480 | tf_op jit(solution)/shard_map/ppermute | solution.py:536
  69.9 11.0 %collective-permute-start.27 = (bf16[2,96,1536]{2,1,0:T(8,128)(2,1)S(1)}, bf16[2,96,1536]{2,1,0:T(8,128)(2,1)S(1)}, u32[]{:S(2)}, u32[]{:S(2)}) collective-permute-start(bf16[2,96,1536]{2,1,0:T(8,128)(2,1)S(1)} %collective-permute-done.19.refs_2_), channel_id=1, source_target_pairs={{0,1},{1,0},{2,3},{3,2},{4,5},{5,4},{6,7},{7,6},{8,9},{9,8},{10,11... | collective-permute-start | bytes 1769480 | tf_op jit(solution)/shard_map/ppermute | solution.py:536
  87.1 15.2 %collective-permute-start.34 = (bf16[4,96,768]{2,1,0:T(8,128)(2,1)S(1)}, bf16[4,96,768]{2,1,0:T(8,128)(2,1)S(1)}, u32[]{:S(2)}, u32[]{:S(2)}) collective-permute-start(bf16[4,96,768]{2,1,0:T(8,128)(2,1)S(1)} %get-tuple-element.162), channel_id=1, source_target_pairs={{0,8},{4,12},{8,0},{12,4},{16,24},{20,28},{24,16},{28,20},{1,9},{5... | collective-permute-start | bytes 1769480 | tf_op jit(solution)/shard_map/ppermute | solution.py:536
  88.7 14.8 %collective-permute-start.35 = (bf16[4,96,768]{2,1,0:T(8,128)(2,1)S(1)}, bf16[4,96,768]{2,1,0:T(8,128)(2,1)S(1)}, u32[]{:S(2)}, u32[]{:S(2)}) collective-permute-start(bf16[4,96,768]{2,1,0:T(8,128)(2,1)S(1)} %get-tuple-element.164), channel_id=1, source_target_pairs={{0,4},{4,0},{8,12},{12,8},{16,20},{20,16},{24,28},{28,24},{1,5},{5... | collective-permute-start | bytes 1769480 | tf_op jit(solution)/shard_map/ppermute | solution.py:536
  99.4 9.9 %collective-permute-start.38 = (bf16[192,1152]{1,0:T(8,128)(2,1)S(1)}, bf16[192,1152]{1,0:T(8,128)(2,1)S(1)}, u32[]{:S(2)}, u32[]{:S(2)}) collective-permute-start(bf16[192,1152]{1,0:T(8,128)(2,1)S(1)} %get-tuple-element.194), channel_id=1, source_target_pairs={{0,1},{1,0},{2,3},{3,2},{4,5},{5,4},{6,7},{7,6},{8,9},{9,8},{10,11... | collective-permute-start | bytes 1327112 | tf_op jit(solution)/shard_map/ppermute | solution.py:536
  107.8 16.2 %collective-permute-start.42 = (bf16[4,96,768]{2,1,0:T(8,128)(2,1)S(1)}, bf16[4,96,768]{2,1,0:T(8,128)(2,1)S(1)}, u32[]{:S(2)}, u32[]{:S(2)}) collective-permute-start(bf16[4,96,768]{2,1,0:T(8,128)(2,1)S(1)} %get-tuple-element.188), channel_id=1, source_target_pairs={{0,4},{4,0},{8,12},{12,8},{16,20},{20,16},{24,28},{28,24},{1,5},{5... | collective-permute-start | bytes 1769480 | tf_op jit(solution)/shard_map/ppermute | solution.py:536
  114.1 25.3 %collective-permute-start.46 = (bf16[4,96,768]{2,1,0:T(8,128)(2,1)S(1)}, bf16[4,96,768]{2,1,0:T(8,128)(2,1)S(1)}, u32[]{:S(2)}, u32[]{:S(2)}) collective-permute-start(bf16[4,96,768]{2,1,0:T(8,128)(2,1)S(1)} %get-tuple-element.220), channel_id=1, source_target_pairs={{0,4},{4,0},{8,12},{12,8},{16,20},{20,16},{24,28},{28,24},{1,5},{5... | collective-permute-start | bytes 1769480 | tf_op jit(solution)/shard_map/ppermute | solution.py:536
  116.2 15.0 %collective-permute-start.43 = (bf16[2,96,768]{2,1,0:T(8,128)(2,1)S(1)}, bf16[2,96,768]{2,1,0:T(8,128)(2,1)S(1)}, u32[]{:S(2)}, u32[]{:S(2)}) collective-permute-start(bf16[2,96,768]{2,1,0:T(8,128)(2,1)S(1)} %get-tuple-element.210), channel_id=1, source_target_pairs={{0,8},{4,12},{8,0},{12,4},{16,24},{20,28},{24,16},{28,20},{1,9},{5... | collective-permute-start | bytes 884744 | tf_op jit(solution)/shard_map/ppermute | solution.py:536
  117.7 15.8 %collective-permute-start.44 = (bf16[2,96,768]{2,1,0:T(8,128)(2,1)S(1)}, bf16[2,96,768]{2,1,0:T(8,128)(2,1)S(1)}, u32[]{:S(2)}, u32[]{:S(2)}) collective-permute-start(bf16[2,96,768]{2,1,0:T(8,128)(2,1)S(1)} %get-tuple-element.213), channel_id=1, source_target_pairs={{0,16},{4,20},{8,24},{12,28},{16,0},{20,4},{24,8},{28,12},{1,17},{... | collective-permute-start | bytes 884744 | tf_op jit(solution)/shard_map/ppermute | solution.py:536
  124.0 38.7 %collective-permute-start.57 = (bf16[192,2304]{1,0:T(8,128)(2,1)S(1)}, bf16[192,2304]{1,0:T(8,128)(2,1)S(1)}, u32[]{:S(2)}, u32[]{:S(2)}) collective-permute-start(bf16[192,2304]{1,0:T(8,128)(2,1)S(1)} %image_chip.1), channel_id=1, source_target_pairs={{0,2},{1,3},{2,0},{3,1},{4,6},{5,7},{6,4},{7,5},{8,10},{9,11},{10,... | collective-permute-start | bytes 2654216 | tf_op jit(solution)/shard_map/ppermute | solution.py:536
  133.5 20.9 %collective-permute-start.51 = (f32[128,768]{1,0:T(8,128)S(1)}, f32[128,768]{1,0:T(8,128)S(1)}, u32[]{:S(2)}, u32[]{:S(2)}) collective-permute-start(f32[128,768]{1,0:T(8,128)S(1)} %get-tuple-element.230.own), channel_id=1, source_target_pairs={{0,1},{1,0},{2,3},{3,2},{4,5},{5,4},{6,7},{7,6},{8,9},{9,8},{10,11... | collective-permute-start | bytes 1179656 | tf_op jit(solution)/shard_map/ppermute | solution.py:536
  136.7 16.0 %collective-permute-start.48 = (bf16[2,96,768]{2,1,0:T(8,128)(2,1)S(1)}, bf16[2,96,768]{2,1,0:T(8,128)(2,1)S(1)}, u32[]{:S(2)}, u32[]{:S(2)}) collective-permute-start(bf16[2,96,768]{2,1,0:T(8,128)(2,1)S(1)} %get-tuple-element.224), channel_id=1, source_target_pairs={{0,16},{4,20},{8,24},{12,28},{16,0},{20,4},{24,8},{28,12},{1,17},{... | collective-permute-start | bytes 884744 | tf_op jit(solution)/shard_map/ppermute | solution.py:536
  139.4 10.3 %collective-permute-start.52 = (bf16[128,768]{1,0:T(8,128)(2,1)S(1)}, bf16[128,768]{1,0:T(8,128)(2,1)S(1)}, u32[]{:S(2)}, u32[]{:S(2)}) collective-permute-start(bf16[128,768]{1,0:T(8,128)(2,1)S(1)} %add_pair.11.chip), channel_id=1, source_target_pairs={{0,2},{1,3},{2,0},{3,1},{4,6},{5,7},{6,4},{7,5},{8,10},{9,11},{10,... | collective-permute-start | bytes 589832 | tf_op jit(solution)/shard_map/ppermute | solution.py:536
  145.8 13.6 %collective-permute-start.54 = (bf16[208,768]{1,0:T(8,128)(2,1)S(1)}, bf16[208,768]{1,0:T(8,128)(2,1)S(1)}, u32[]{:S(2)}, u32[]{:S(2)}) collective-permute-start(bf16[208,768]{1,0:T(8,128)(2,1)S(1)} %get-tuple-element.235), channel_id=1, source_target_pairs={{0,8},{4,12},{8,0},{12,4},{16,24},{20,28},{24,16},{28,20},{1,9},{5... | collective-permute-start | bytes 958472 | tf_op jit(solution)/shard_map/ppermute | solution.py:536
  149.7 12.9 %collective-permute-start.55 = (bf16[192,1152]{1,0:T(8,128)(2,1)S(1)}, bf16[192,1152]{1,0:T(8,128)(2,1)S(1)}, u32[]{:S(2)}, u32[]{:S(2)}) collective-permute-start(bf16[192,1152]{1,0:T(8,128)(2,1)S(1)} %get-tuple-element.239), channel_id=1, source_target_pairs={{0,1},{1,0},{2,3},{3,2},{4,5},{5,4},{6,7},{7,6},{8,9},{9,8},{10,11... | collective-permute-start | bytes 1327112 | tf_op jit(solution)/shard_map/ppermute | solution.py:536
  152.7 9.9 %collective-permute-start.56 = (bf16[192,1152]{1,0:T(8,128)(2,1)S(1)}, bf16[192,1152]{1,0:T(8,128)(2,1)S(1)}, u32[]{:S(2)}, u32[]{:S(2)}) collective-permute-start(bf16[192,1152]{1,0:T(8,128)(2,1)S(1)} %get-tuple-element.240), channel_id=1, source_target_pairs={{0,1},{1,0},{2,3},{3,2},{4,5},{5,4},{6,7},{7,6},{8,9},{9,8},{10,11... | collective-permute-start | bytes 1327112 | tf_op jit(solution)/shard_map/ppermute | solution.py:536
  (52 other events, 439.7 us)

commit v5 on v4

--- a/solution.py
+++ b/solution.py
@@ -656,9 +656,9 @@
         self_pieces = collect(self_shard, self_hops, self_swaps)
         cross_pieces = collect(cross_shard, cross_hops)
         ffn_pair = pair_up(gate(ffn_shard, self_hops[0]), "pairF")
-        ffn_hops = [around(gate(ffn_pair, cross_hops[1]))]
+        ffn_hops = [around(gate(ffn_pair, self_hops[1]))]
         ffn_hops.append(around(ffn_hops[0]))
-        text_in = gate(text, ffn_hops[0], cross_hops[2])
+        text_in = gate(text, ffn_hops[0], cross_hops[3])
     else:
         gather = lambda shard: [lax.all_gather(shard, "dp", axis=0, tiled=True)]
         self_pieces = gather(

time: 171 us -> 168 us (0.982)
  waiting for transfers between devices: 77.8 us -> 73.5 us
    ppermute x12, waiting for transfers between devices: 30.6 us -> 26.4 us  [around(): return lax.ppermute(value, ('dp', 'mp'), turns)]
    ppermute x48, starting transfers between devices: 30.4 us -> 34.5 us  [swap(): return lax.ppermute(value, axis, [(i, i ^ bits) for i in range(size)])]
    ppermute x12, starting transfers between devices: 23.4 us -> 20.8 us  [around(): return lax.ppermute(value, ('dp', 'mp'), turns)]
  transfers between devices with their start and end apart: 60 -> 60, of which waited for: 31 -> 35; matrix products, arithmetic and copies ran while one was open for 0% -> 0% of each run, Pallas kernels for 18% -> 18%
where the time goes in v5:
time: 168 us; the launch traced here: 167 us
  waiting for transfers between devices  73.5 us (44%)
  starting transfers between devices  55.3 us (33%)
  Pallas kernels  33.3 us (20%)
  local copies, waits for them, and re-layouts  4.25 us (3%)
    ppermute x48, waiting for transfers between devices, swap(): return lax.ppermute(value, axis, [(i, i ^ bits) for i in range(size)])  47.1 us
    ppermute x48, starting transfers between devices, swap(): return lax.ppermute(value, axis, [(i, i ^ bits) for i in range(size)])  34.5 us
    pallas_call x44, Pallas kernels, call(): pl.pallas_call(body, out_shape=[jax.ShapeDtypeStruct(s, d) for s, d in ou...  27.2 us
    ppermute x12, waiting for transfers between devices, around(): return lax.ppermute(value, ('dp', 'mp'), turns)  26.4 us
    ppermute x12, starting transfers between devices, around(): return lax.ppermute(value, ('dp', 'mp'), turns)  20.8 us
    unnamed x32, local copies, waits for them, and re-layouts  4.25 us
  transfers between devices with their start and end apart: 60, of which 35 were waited for; matrix products, arithmetic and copies ran while one was open for 0% of the time, Pallas kernels for 18%

profile of v5, /device:TPU:0, one launch (start us, length us, event | category | flops | bytes accessed | tf_op | source)
XLA Modules:
  0.0 167.4 jit_solution(17403338105521859987)
XLA Ops:
  4.1 3.0 %collective-permute-start.1 = (bf16[2,96,768]{2,1,0:T(8,128)(2,1)S(1)}, bf16[2,96,768]{2,1,0:T(8,128)(2,1)S(1)}, u32[]{:S(2)}, u32[]{:S(2)}) collective-permute-start(bf16[2,96,768]{2,1,0:T(8,128)(2,1)S(1)} %pairA.1), channel_id=1, source_target_pairs={{0,8},{1,5},{2,10},{3,7},{8,16},{9,1},{10,18},{11,3},{16,24},{17,9... | collective-permute-start | bytes 884744 | tf_op jit(solution)/shard_map/ppermute | solution.py:586
  14.6 3.3 %collective-permute-done.6.refs_1_ = bf16[2,96,768]{2,1,0:T(8,128)(2,1)S(1)} collective-permute-done((bf16[2,96,768]{2,1,0:T(8,128)(2,1)S(1)}, bf16[2,96,768]{2,1,0:T(8,128)(2,1)S(1)}, u32[]{:S(2)}, u32[]{:S(2)}) %collective-permute-start.6) | collective-permute-done | bytes 294944 | tf_op jit(solution)/shard_map/ppermute | solution.py:586
  22.7 2.0 %collective-permute-done.7.refs_2_ = bf16[2,96,768]{2,1,0:T(8,128)(2,1)S(1)} collective-permute-done((bf16[2,96,768]{2,1,0:T(8,128)(2,1)S(1)}, bf16[2,96,768]{2,1,0:T(8,128)(2,1)S(1)}, u32[]{:S(2)}, u32[]{:S(2)}) %collective-permute-start.7) | collective-permute-done | bytes 294944 | tf_op jit(solution)/shard_map/ppermute | solution.py:586
  28.3 5.8 %collective-permute-done.8.pair.refs_3_ = bf16[2,96,768]{2,1,0:T(8,128)(2,1)S(1)} collective-permute-done((bf16[2,96,768]{2,1,0:T(8,128)(2,1)S(1)}, bf16[2,96,768]{2,1,0:T(8,128)(2,1)S(1)}, u32[]{:S(2)}, u32[]{:S(2)}) %collective-permute-start.8) | collective-permute-done | bytes 294944 | tf_op jit(solution)/shard_map/ppermute | solution.py:586
  41.0 7.8 %collective-permute-done.14.refs_7_ = bf16[96,768]{1,0:T(8,128)(2,1)S(1)} collective-permute-done((bf16[96,768]{1,0:T(8,128)(2,1)S(1)}, bf16[96,768]{1,0:T(8,128)(2,1)S(1)}, u32[]{:S(2)}, u32[]{:S(2)}) %collective-permute-start.14) | collective-permute-done | bytes 147488 | tf_op jit(solution)/shard_map/ppermute | solution.py:586
  48.8 3.2 %self_forward.1 = (bf16[768,768]{1,0:T(8,128)(2,1)S(1)}, bf16[256,768]{1,0:T(8,128)(2,1)S(1)}, bf16[128,768]{1,0:T(8,128)(2,1)S(1)}, bf16[128,768]{1,0:T(8,128)(2,1)S(1)}) custom-call(s32[4]{0:T(128)S(1)} %copy-done.13, bf16[256,768]{1,0:T(8,128)(2,1)S(1)} %bitcast.10, f32[3,768]{1,0:T(4,128)S(1)} %copy-done.3, f32[3,768]{1,0:T(4,128)S(1)} %copy-done.4, ...), custom_call_target="tpu_custom_call" | custom-call | flops 1 | bytes 10000000 | tf_op jit(solution)/shard_map/self_forward/pallas_call | solution.py:685
  55.2 2.9 %keyval.3 = (bf16[768,192]{1,0:T(8,128)(2,1)S(1)}, bf16[768,192]{1,0:T(8,128)(2,1)S(1)}, bf16[768,192]{1,0:T(8,128)(2,1)S(1)}, bf16[768,192]{1,0:T(8,128)(2,1)S(...) custom-call(bf16[2304,768]{1,0:T(8,128)(2,1)S(1)} %bitcast.8, ...), custom_call_target="tpu_custom_call" | custom-call | flops 1 | bytes 10000000 | tf_op jit(solution)/shard_map/keyval/pallas_call | solution.py:709
  58.1 2.5 %collective-permute-done.20.other = bf16[128,768]{1,0:T(8,128)(2,1)S(1)} collective-permute-done((bf16[128,768]{1,0:T(8,128)(2,1)S(1)}, bf16[128,768]{1,0:T(8,128)(2,1)S(1)}, u32[]{:S(2)}, u32[]{:S(2)}) %collective-permute-start.20) | collective-permute-done | bytes 196640 | tf_op jit(solution)/shard_map/ppermute | solution.py:536
  63.9 3.0 %cross_forward.1 = (bf16[256,768]{1,0:T(8,128)(2,1)S(1)}, bf16[256,192]{1,0:T(8,128)(2,1)S(1)}, f32[4,192,576]{2,1,0:T(8,128)S(1)}, bf16[256,192]{1,0:T(8,128)(2...) custom-call(s32[4]{0:T(128)S(1)} %copy-done.14, bf16[128,768]{1,0:T(8,128)(2,1)S(1)} %get-tuple-element.143.own, ...), custom_call_target="tpu_custom_call" | custom-call | flops 1 | bytes 5505025 | tf_op jit(solution)/shard_map/cross_forward/pallas_call | solution.py:69
  67.7 3.1 %collective-permute-done.25.pair.refs_3_ = bf16[2,96,1536]{2,1,0:T(8,128)(2,1)S(1)} collective-permute-done((bf16[2,96,1536]{2,1,0:T(8,128)(2,1)S(1)}, bf16[2,96,1536]{2,1,0:T(8,128)(2,1)S(1)}, u32[]{:S(2)}, u32[]{:S(2)}) %collective-permute-start.25) | collective-permute-done | bytes 589856 | tf_op jit(solution)/shard_map/ppermute | solution.py:586
  74.2 4.0 %collective-permute-done.23.other = bf16[128,768]{1,0:T(8,128)(2,1)S(1)} collective-permute-done((bf16[128,768]{1,0:T(8,128)(2,1)S(1)}, bf16[128,768]{1,0:T(8,128)(2,1)S(1)}, u32[]{:S(2)}, u32[]{:S(2)}) %collective-permute-start.23) | collective-permute-done | bytes 196640 | tf_op jit(solution)/shard_map/ppermute | solution.py:536
  92.1 2.9 %cross_back.1 = (bf16[256,768]{1,0:T(8,128)(2,1)S(1)}, bf16[256,192]{1,0:T(8,128)(2,1)S(1)}, bf16[192,2304]{1,0:T(8,128)(2,1)S(1)}, bf16[192,2304]{1,0:T(8,128)(...) custom-call(bf16[128,768]{1,0:T(8,128)(2,1)S(1)} %get-tuple-element.167.own, ...), custom_call_target="tpu_custom_call" | custom-call | flops 1 | bytes 7274497 | tf_op jit(solution)/shard_map/cross_back/pallas_call | solution.py:69
  95.2 2.0 %image_part.1 = (bf16[192,1152]{1,0:T(8,128)(2,1)S(1)}, bf16[192,1152]{1,0:T(8,128)(2,1)S(1)}, bf16[192,1152]{1,0:T(8,128)(2,1)S(1)}, bf16[192,1152]{1,0:T(8,128...) custom-call(bf16[192,2304]{1,0:T(8,128)(2,1)S(1)} %get-tuple-element.182.dkt, ...), custom_call_target="tpu_custom_call" | custom-call | flops 1 | bytes 5898241 | tf_op jit(solution)/shard_map/image_part/pallas_call | solution.py:69
  102.2 2.2 %cross_weights.1 = (bf16[4,96,768]{2,1,0:T(8,128)(2,1)S(1)}, bf16[4,96,768]{2,1,0:T(8,128)(2,1)S(1)}) custom-call(bf16[2304,768]{1,0:T(8,128)(2,1)S(1)} %bitcast.9, bf16[192,2304]{1,0:T(8,128)(2,1)S(1)} %get-tuple-element.182.dkt, bf16[192,2304]{1,0:T(8,128)(2,1)S(1)} %get-tuple-element.172.dvt, bf16[256,768]{1,0:T(8,128)(2,1)S(1)} %get-tuple-element.183.normed, ...), custom_call_target="tpu_custom_call" | custom-call | flops 1 | bytes 7471105 | tf_op jit(solution)/shard_map/cross_weights/pallas_call | solution.py:69
  107.0 4.3 %self_back.1 = (bf16[4,96,768]{2,1,0:T(8,128)(2,1)S(1)}, bf16[4,96,768]{2,1,0:T(8,128)(2,1)S(1)}, bf16[144,768]{1,0:T(8,128)(2,1)S(1)}, bf16[144,768]{1,0:T(8,128)(2,1)S(1)}) custom-call(s32[4]{0:T(128)S(1)} %copy-done.13, bf16[128,768]{1,0:T(8,128)(2,1)S(1)} %get-tuple-element.191.own, bf16[128,768]{1,0:T(8,128)(2,1)S(1)} %collective-permute-done.37.other, ...), custom_call_target="tpu_custom_call" | custom-call | flops 1 | bytes 4051969 | tf_op jit(solution)/shard_map/self_back/pallas_call | solution.py:69
  115.9 2.5 %collective-permute-start.44 = (bf16[2,96,768]{2,1,0:T(8,128)(2,1)S(1)}, bf16[2,96,768]{2,1,0:T(8,128)(2,1)S(1)}, u32[]{:S(2)}, u32[]{:S(2)}) collective-permute-start(bf16[2,96,768]{2,1,0:T(8,128)(2,1)S(1)} %get-tuple-element.213), channel_id=1, source_target_pairs={{0,16},{4,20},{8,24},{12,28},{16,0},{20,4},{24,8},{28,12},{1,17},{... | collective-permute-start | bytes 884744 | tf_op jit(solution)/shard_map/ppermute | solution.py:536
  118.4 2.0 %collective-permute-done.41.other = bf16[144,768]{1,0:T(8,128)(2,1)S(1)} collective-permute-done((bf16[144,768]{1,0:T(8,128)(2,1)S(1)}, bf16[144,768]{1,0:T(8,128)(2,1)S(1)}, u32[]{:S(2)}, u32[]{:S(2)}) %collective-permute-start.41) | collective-permute-done | bytes 221216 | tf_op jit(solution)/shard_map/ppermute | solution.py:536
  123.3 6.0 %collective-permute-done.43.other = bf16[2,96,768]{2,1,0:T(8,128)(2,1)S(1)} collective-permute-done((bf16[2,96,768]{2,1,0:T(8,128)(2,1)S(1)}, bf16[2,96,768]{2,1,0:T(8,128)(2,1)S(1)}, u32[]{:S(2)}, u32[]{:S(2)}) %collective-permute-start.43) | collective-permute-done | bytes 294944 | tf_op jit(solution)/shard_map/ppermute | solution.py:536
  131.6 2.8 %collective-permute-done.47.vec_other = bf16[16,768]{1,0:T(8,128)(2,1)S(1)} collective-permute-done((bf16[16,768]{1,0:T(8,128)(2,1)S(1)}, bf16[16,768]{1,0:T(8,128)(2,1)S(1)}, u32[]{:S(2)}, u32[]{:S(2)}) %collective-permute-start.47) | collective-permute-done | bytes 24608 | tf_op jit(solution)/shard_map/ppermute | solution.py:536
  134.4 2.6 %collective-permute-start.48 = (bf16[2,96,768]{2,1,0:T(8,128)(2,1)S(1)}, bf16[2,96,768]{2,1,0:T(8,128)(2,1)S(1)}, u32[]{:S(2)}, u32[]{:S(2)}) collective-permute-start(bf16[2,96,768]{2,1,0:T(8,128)(2,1)S(1)} %get-tuple-element.224), channel_id=1, source_target_pairs={{0,16},{4,20},{8,24},{12,28},{16,0},{20,4},{24,8},{28,12},{1,17},{... | collective-permute-start | bytes 884744 | tf_op jit(solution)/shard_map/ppermute | solution.py:536
  139.8 4.0 %collective-permute-done.50.other = bf16[96,768]{1,0:T(8,128)(2,1)S(1)} collective-permute-done((bf16[96,768]{1,0:T(8,128)(2,1)S(1)}, bf16[96,768]{1,0:T(8,128)(2,1)S(1)}, u32[]{:S(2)}, u32[]{:S(2)}) %collective-permute-start.50) | collective-permute-done | bytes 147488 | tf_op jit(solution)/shard_map/ppermute | solution.py:536
  147.1 3.6 %collective-permute-done.48.other = bf16[2,96,768]{2,1,0:T(8,128)(2,1)S(1)} collective-permute-done((bf16[2,96,768]{2,1,0:T(8,128)(2,1)S(1)}, bf16[2,96,768]{2,1,0:T(8,128)(2,1)S(1)}, u32[]{:S(2)}, u32[]{:S(2)}) %collective-permute-start.48) | collective-permute-done | bytes 294944 | tf_op jit(solution)/shard_map/ppermute | solution.py:536
  157.9 2.5 %collective-permute-start.58 = (bf16[96,768]{1,0:T(8,128)(2,1)S(1)}, bf16[96,768]{1,0:T(8,128)(2,1)S(1)}, u32[]{:S(2)}, u32[]{:S(2)}) collective-permute-start(bf16[96,768]{1,0:T(8,128)(2,1)S(1)} %get-tuple-element.243), channel_id=1, source_target_pairs={{0,8},{4,12},{8,0},{12,4},{16,24},{20,28},{24,16},{28,20},{1,9},{5... | collective-permute-start | bytes 442376 | tf_op jit(solution)/shard_map/ppermute | solution.py:536
  162.2 2.8 %collective-permute-done.58.refs_1_ = bf16[96,768]{1,0:T(8,128)(2,1)S(1)} collective-permute-done((bf16[96,768]{1,0:T(8,128)(2,1)S(1)}, bf16[96,768]{1,0:T(8,128)(2,1)S(1)}, u32[]{:S(2)}, u32[]{:S(2)}) %collective-permute-start.58) | collective-permute-done | bytes 147488 | tf_op jit(solution)/shard_map/ppermute | solution.py:536
  (175 shorter events, 85.6 us)
Async XLA Ops:
  21.1 16.2 %collective-permute-start.4 = (bf16[2,96,1536]{2,1,0:T(8,128)(2,1)S(1)}, bf16[2,96,1536]{2,1,0:T(8,128)(2,1)S(1)}, u32[]{:S(2)}, u32[]{:S(2)}) collective-permute-start(bf16[2,96,1536]{2,1,0:T(8,128)(2,1)S(1)} %pairF.1), channel_id=1, source_target_pairs={{0,8},{1,5},{2,10},{3,7},{8,16},{9,1},{10,18},{11,3},{16,24},{17,9... | collective-permute-start | bytes 1769480 | tf_op jit(solution)/shard_map/ppermute | solution.py:586
  26.3 11.1 %collective-permute-start.10 = (bf16[2,96,768]{2,1,0:T(8,128)(2,1)S(1)}, bf16[2,96,768]{2,1,0:T(8,128)(2,1)S(1)}, u32[]{:S(2)}, u32[]{:S(2)}) collective-permute-start(bf16[2,96,768]{2,1,0:T(8,128)(2,1)S(1)} %collective-permute-done.3.refs_2_), channel_id=1, source_target_pairs={{0,8},{1,5},{2,10},{3,7},{8,16},{9,1},{10,18},{11,3},{16,24},{17,9... | collective-permute-start | bytes 884744 | tf_op jit(solution)/shard_map/ppermute | solution.py:586
  27.8 13.1 %collective-permute-start.11 = (bf16[2,96,768]{2,1,0:T(8,128)(2,1)S(1)}, bf16[2,96,768]{2,1,0:T(8,128)(2,1)S(1)}, u32[]{:S(2)}, u32[]{:S(2)}) collective-permute-start(bf16[2,96,768]{2,1,0:T(8,128)(2,1)S(1)} %collective-permute-done.1.refs_1_), channel_id=1, source_target_pairs={{0,1},{1,0},{2,3},{3,2},{4,5},{5,4},{6,7},{7,6},{8,9},{9,8},{10,11... | collective-permute-start | bytes 884744 | tf_op jit(solution)/shard_map/ppermute | solution.py:536
  27.8 13.1 %collective-permute-start.12 = (bf16[2,96,768]{2,1,0:T(8,128)(2,1)S(1)}, bf16[2,96,768]{2,1,0:T(8,128)(2,1)S(1)}, u32[]{:S(2)}, u32[]{:S(2)}) collective-permute-start(bf16[2,96,768]{2,1,0:T(8,128)(2,1)S(1)} %collective-permute-done.3.refs_2_), channel_id=1, source_target_pairs={{0,1},{1,0},{2,3},{3,2},{4,5},{5,4},{6,7},{7,6},{8,9},{9,8},{10,11... | collective-permute-start | bytes 884744 | tf_op jit(solution)/shard_map/ppermute | solution.py:536
  37.3 11.5 %collective-permute-start.13 = (bf16[2,96,768]{2,1,0:T(8,128)(2,1)S(1)}, bf16[2,96,768]{2,1,0:T(8,128)(2,1)S(1)}, u32[]{:S(2)}, u32[]{:S(2)}) collective-permute-start(bf16[2,96,768]{2,1,0:T(8,128)(2,1)S(1)} %collective-permute-done.10.pair.refs_3_), channel_id=1, source_target_pairs={{0,1},{1,0},{2,3},{3,2},{4,5},{5,4},{6,7},{7,6},{8,9},{9,8},{10,11... | collective-permute-start | bytes 884744 | tf_op jit(solution)/shard_map/ppermute | solution.py:536
  37.3 20.7 %collective-permute-start.19 = (bf16[2,96,1536]{2,1,0:T(8,128)(2,1)S(1)}, bf16[2,96,1536]{2,1,0:T(8,128)(2,1)S(1)}, u32[]{:S(2)}, u32[]{:S(2)}) collective-permute-start(bf16[2,96,1536]{2,1,0:T(8,128)(2,1)S(1)} %collective-permute-done.4.refs_1_), channel_id=1, source_target_pairs={{0,8},{1,5},{2,10},{3,7},{8,16},{9,1},{10,18},{11,3},{16,24},{17,9... | collective-permute-start | bytes 1769480 | tf_op jit(solution)/shard_map/ppermute | solution.py:586
  60.8 9.9 %collective-permute-start.25 = (bf16[2,96,1536]{2,1,0:T(8,128)(2,1)S(1)}, bf16[2,96,1536]{2,1,0:T(8,128)(2,1)S(1)}, u32[]{:S(2)}, u32[]{:S(2)}) collective-permute-start(bf16[2,96,1536]{2,1,0:T(8,128)(2,1)S(1)} %collective-permute-done.19.refs_2_), channel_id=1, source_target_pairs={{0,8},{1,5},{2,10},{3,7},{8,16},{9,1},{10,18},{11,3},{16,24},{17,9... | collective-permute-start | bytes 1769480 | tf_op jit(solution)/shard_map/ppermute | solution.py:586
  67.2 11.4 %collective-permute-start.26 = (bf16[2,96,1536]{2,1,0:T(8,128)(2,1)S(1)}, bf16[2,96,1536]{2,1,0:T(8,128)(2,1)S(1)}, u32[]{:S(2)}, u32[]{:S(2)}) collective-permute-start(bf16[2,96,1536]{2,1,0:T(8,128)(2,1)S(1)} %collective-permute-done.4.refs_1_), channel_id=1, source_target_pairs={{0,1},{1,0},{2,3},{3,2},{4,5},{5,4},{6,7},{7,6},{8,9},{9,8},{10,11... | collective-permute-start | bytes 1769480 | tf_op jit(solution)/shard_map/ppermute | solution.py:536
  67.6 11.0 %collective-permute-start.27 = (bf16[2,96,1536]{2,1,0:T(8,128)(2,1)S(1)}, bf16[2,96,1536]{2,1,0:T(8,128)(2,1)S(1)}, u32[]{:S(2)}, u32[]{:S(2)}) collective-permute-start(bf16[2,96,1536]{2,1,0:T(8,128)(2,1)S(1)} %collective-permute-done.19.refs_2_), channel_id=1, source_target_pairs={{0,1},{1,0},{2,3},{3,2},{4,5},{5,4},{6,7},{7,6},{8,9},{9,8},{10,11... | collective-permute-start | bytes 1769480 | tf_op jit(solution)/shard_map/ppermute | solution.py:536
  85.6 15.2 %collective-permute-start.34 = (bf16[4,96,768]{2,1,0:T(8,128)(2,1)S(1)}, bf16[4,96,768]{2,1,0:T(8,128)(2,1)S(1)}, u32[]{:S(2)}, u32[]{:S(2)}) collective-permute-start(bf16[4,96,768]{2,1,0:T(8,128)(2,1)S(1)} %get-tuple-element.162), channel_id=1, source_target_pairs={{0,8},{4,12},{8,0},{12,4},{16,24},{20,28},{24,16},{28,20},{1,9},{5... | collective-permute-start | bytes 1769480 | tf_op jit(solution)/shard_map/ppermute | solution.py:536
  87.3 14.8 %collective-permute-start.35 = (bf16[4,96,768]{2,1,0:T(8,128)(2,1)S(1)}, bf16[4,96,768]{2,1,0:T(8,128)(2,1)S(1)}, u32[]{:S(2)}, u32[]{:S(2)}) collective-permute-start(bf16[4,96,768]{2,1,0:T(8,128)(2,1)S(1)} %get-tuple-element.164), channel_id=1, source_target_pairs={{0,4},{4,0},{8,12},{12,8},{16,20},{20,16},{24,28},{28,24},{1,5},{5... | collective-permute-start | bytes 1769480 | tf_op jit(solution)/shard_map/ppermute | solution.py:536
  105.5 16.2 %collective-permute-start.42 = (bf16[4,96,768]{2,1,0:T(8,128)(2,1)S(1)}, bf16[4,96,768]{2,1,0:T(8,128)(2,1)S(1)}, u32[]{:S(2)}, u32[]{:S(2)}) collective-permute-start(bf16[4,96,768]{2,1,0:T(8,128)(2,1)S(1)} %get-tuple-element.188), channel_id=1, source_target_pairs={{0,4},{4,0},{8,12},{12,8},{16,20},{20,16},{24,28},{28,24},{1,5},{5... | collective-permute-start | bytes 1769480 | tf_op jit(solution)/shard_map/ppermute | solution.py:536
  111.4 25.7 %collective-permute-start.46 = (bf16[4,96,768]{2,1,0:T(8,128)(2,1)S(1)}, bf16[4,96,768]{2,1,0:T(8,128)(2,1)S(1)}, u32[]{:S(2)}, u32[]{:S(2)}) collective-permute-start(bf16[4,96,768]{2,1,0:T(8,128)(2,1)S(1)} %get-tuple-element.220), channel_id=1, source_target_pairs={{0,4},{4,0},{8,12},{12,8},{16,20},{20,16},{24,28},{28,24},{1,5},{5... | collective-permute-start | bytes 1769480 | tf_op jit(solution)/shard_map/ppermute | solution.py:536
  114.3 15.0 %collective-permute-start.43 = (bf16[2,96,768]{2,1,0:T(8,128)(2,1)S(1)}, bf16[2,96,768]{2,1,0:T(8,128)(2,1)S(1)}, u32[]{:S(2)}, u32[]{:S(2)}) collective-permute-start(bf16[2,96,768]{2,1,0:T(8,128)(2,1)S(1)} %get-tuple-element.210), channel_id=1, source_target_pairs={{0,8},{4,12},{8,0},{12,4},{16,24},{20,28},{24,16},{28,20},{1,9},{5... | collective-permute-start | bytes 884744 | tf_op jit(solution)/shard_map/ppermute | solution.py:536
  115.9 15.8 %collective-permute-start.44 = (bf16[2,96,768]{2,1,0:T(8,128)(2,1)S(1)}, bf16[2,96,768]{2,1,0:T(8,128)(2,1)S(1)}, u32[]{:S(2)}, u32[]{:S(2)}) collective-permute-start(bf16[2,96,768]{2,1,0:T(8,128)(2,1)S(1)} %get-tuple-element.213), channel_id=1, source_target_pairs={{0,16},{4,20},{8,24},{12,28},{16,0},{20,4},{24,8},{28,12},{1,17},{... | collective-permute-start | bytes 884744 | tf_op jit(solution)/shard_map/ppermute | solution.py:536
  120.4 9.5 %collective-permute-start.45 = (bf16[128,768]{1,0:T(8,128)(2,1)S(1)}, bf16[128,768]{1,0:T(8,128)(2,1)S(1)}, u32[]{:S(2)}, u32[]{:S(2)}) collective-permute-start(bf16[128,768]{1,0:T(8,128)(2,1)S(1)} %get-tuple-element.218), channel_id=1, source_target_pairs={{0,1},{1,0},{2,3},{3,2},{4,5},{5,4},{6,7},{7,6},{8,9},{9,8},{10,11... | collective-permute-start | bytes 589832 | tf_op jit(solution)/shard_map/ppermute | solution.py:536
  121.7 38.7 %collective-permute-start.57 = (bf16[192,2304]{1,0:T(8,128)(2,1)S(1)}, bf16[192,2304]{1,0:T(8,128)(2,1)S(1)}, u32[]{:S(2)}, u32[]{:S(2)}) collective-permute-start(bf16[192,2304]{1,0:T(8,128)(2,1)S(1)} %image_chip.1), channel_id=1, source_target_pairs={{0,2},{1,3},{2,0},{3,1},{4,6},{5,7},{6,4},{7,5},{8,10},{9,11},{10,... | collective-permute-start | bytes 2654216 | tf_op jit(solution)/shard_map/ppermute | solution.py:536
  131.6 20.7 %collective-permute-start.51 = (f32[128,768]{1,0:T(8,128)S(1)}, f32[128,768]{1,0:T(8,128)S(1)}, u32[]{:S(2)}, u32[]{:S(2)}) collective-permute-start(f32[128,768]{1,0:T(8,128)S(1)} %get-tuple-element.230.own), channel_id=1, source_target_pairs={{0,1},{1,0},{2,3},{3,2},{4,5},{5,4},{6,7},{7,6},{8,9},{9,8},{10,11... | collective-permute-start | bytes 1179656 | tf_op jit(solution)/shard_map/ppermute | solution.py:536
  134.4 16.3 %collective-permute-start.48 = (bf16[2,96,768]{2,1,0:T(8,128)(2,1)S(1)}, bf16[2,96,768]{2,1,0:T(8,128)(2,1)S(1)}, u32[]{:S(2)}, u32[]{:S(2)}) collective-permute-start(bf16[2,96,768]{2,1,0:T(8,128)(2,1)S(1)} %get-tuple-element.224), channel_id=1, source_target_pairs={{0,16},{4,20},{8,24},{12,28},{16,0},{20,4},{24,8},{28,12},{1,17},{... | collective-permute-start | bytes 884744 | tf_op jit(solution)/shard_map/ppermute | solution.py:536
  137.2 9.9 %collective-permute-start.52 = (bf16[128,768]{1,0:T(8,128)(2,1)S(1)}, bf16[128,768]{1,0:T(8,128)(2,1)S(1)}, u32[]{:S(2)}, u32[]{:S(2)}) collective-permute-start(bf16[128,768]{1,0:T(8,128)(2,1)S(1)} %add_pair.11.chip), channel_id=1, source_target_pairs={{0,2},{1,3},{2,0},{3,1},{4,6},{5,7},{6,4},{7,5},{8,10},{9,11},{10,... | collective-permute-start | bytes 589832 | tf_op jit(solution)/shard_map/ppermute | solution.py:536
  143.8 12.7 %collective-permute-start.54 = (bf16[208,768]{1,0:T(8,128)(2,1)S(1)}, bf16[208,768]{1,0:T(8,128)(2,1)S(1)}, u32[]{:S(2)}, u32[]{:S(2)}) collective-permute-start(bf16[208,768]{1,0:T(8,128)(2,1)S(1)} %get-tuple-element.235), channel_id=1, source_target_pairs={{0,8},{4,12},{8,0},{12,4},{16,24},{20,28},{24,16},{28,20},{1,9},{5... | collective-permute-start | bytes 958472 | tf_op jit(solution)/shard_map/ppermute | solution.py:536
  147.1 13.4 %collective-permute-start.55 = (bf16[192,1152]{1,0:T(8,128)(2,1)S(1)}, bf16[192,1152]{1,0:T(8,128)(2,1)S(1)}, u32[]{:S(2)}, u32[]{:S(2)}) collective-permute-start(bf16[192,1152]{1,0:T(8,128)(2,1)S(1)} %get-tuple-element.239), channel_id=1, source_target_pairs={{0,1},{1,0},{2,3},{3,2},{4,5},{5,4},{6,7},{7,6},{8,9},{9,8},{10,11... | collective-permute-start | bytes 1327112 | tf_op jit(solution)/shard_map/ppermute | solution.py:536
  150.7 9.7 %collective-permute-start.56 = (bf16[192,1152]{1,0:T(8,128)(2,1)S(1)}, bf16[192,1152]{1,0:T(8,128)(2,1)S(1)}, u32[]{:S(2)}, u32[]{:S(2)}) collective-permute-start(bf16[192,1152]{1,0:T(8,128)(2,1)S(1)} %get-tuple-element.240), channel_id=1, source_target_pairs={{0,1},{1,0},{2,3},{3,2},{4,5},{5,4},{6,7},{7,6},{8,9},{9,8},{10,11... | collective-permute-start | bytes 1327112 | tf_op jit(solution)/shard_map/ppermute | solution.py:536
  156.6 9.9 %collective-permute-start.59 = (bf16[112,768]{1,0:T(8,128)(2,1)S(1)}, bf16[112,768]{1,0:T(8,128)(2,1)S(1)}, u32[]{:S(2)}, u32[]{:S(2)}) collective-permute-start(bf16[112,768]{1,0:T(8,128)(2,1)S(1)} %get-tuple-element.246), channel_id=1, source_target_pairs={{0,16},{4,20},{8,24},{12,28},{16,0},{20,4},{24,8},{28,12},{1,17},{... | collective-permute-start | bytes 516104 | tf_op jit(solution)/shard_map/ppermute | solution.py:536
  (52 other events, 415.4 us)

commit v6 on v5

--- a/solution.py
+++ b/solution.py
@@ -634,17 +634,17 @@
         (self_shard,) = call(
             pack_self_kernel, "pack_self", [((height, 4 * width), BF)], (), (self_qkv, self_out)
         )
+        (ffn_shard,) = call(
+            pack_ffn_kernel, "pack_ffn", [((height, 2 * hidden), BF)], (), (mlp_up, mlp_down.T)
+        )
+        self_pair = pair_up(self_shard, "pairA")
         (cross_shard,) = call(
             pack_cross_kernel,
             "pack_cross",
             [((height, 4 * width), BF)],
             (),
-            (cross_query, cross_keyval, cross_out),
+            (gate(cross_query, self_pair), cross_keyval, cross_out),
         )
-        (ffn_shard,) = call(
-            pack_ffn_kernel, "pack_ffn", [((height, 2 * hidden), BF)], (), (mlp_up, mlp_down.T)
-        )
-        self_pair = pair_up(self_shard, "pairA")
         self_hops = [around(self_pair)]
         cross_hops = [around(pair_up(gate(cross_shard, self_pair), "pairB"))]
         for k in range(2):

time: 168 us -> 168 us (level)
  no operation moved by 1% of the time
where the time goes in v6:
time: 168 us; the launch traced here: 167 us
  waiting for transfers between devices  73.5 us (44%)
  starting transfers between devices  55.3 us (33%)
  Pallas kernels  33.3 us (20%)
  local copies, waits for them, and re-layouts  4.25 us (3%)
    ppermute x48, waiting for transfers between devices, swap(): return lax.ppermute(value, axis, [(i, i ^ bits) for i in range(size)])  47.1 us
    ppermute x48, starting transfers between devices, swap(): return lax.ppermute(value, axis, [(i, i ^ bits) for i in range(size)])  34.5 us
    pallas_call x44, Pallas kernels, call(): pl.pallas_call(body, out_shape=[jax.ShapeDtypeStruct(s, d) for s, d in ou...  27.2 us
    ppermute x12, waiting for transfers between devices, around(): return lax.ppermute(value, ('dp', 'mp'), turns)  26.4 us
    ppermute x12, starting transfers between devices, around(): return lax.ppermute(value, ('dp', 'mp'), turns)  20.8 us
    unnamed x32, local copies, waits for them, and re-layouts  4.25 us
  transfers between devices with their start and end apart: 60, of which 35 were waited for; matrix products, arithmetic and copies ran while one was open for 0% of the time, Pallas kernels for 18%

profile of v6, /device:TPU:0, one launch (start us, length us, event | category | flops | bytes accessed | tf_op | source)
XLA Modules:
  0.0 167.4 jit_solution(17403338105521859987)
XLA Ops:
  4.1 3.0 %collective-permute-start.1 = (bf16[2,96,768]{2,1,0:T(8,128)(2,1)S(1)}, bf16[2,96,768]{2,1,0:T(8,128)(2,1)S(1)}, u32[]{:S(2)}, u32[]{:S(2)}) collective-permute-start(bf16[2,96,768]{2,1,0:T(8,128)(2,1)S(1)} %pairA.1), channel_id=1, source_target_pairs={{0,8},{1,5},{2,10},{3,7},{8,16},{9,1},{10,18},{11,3},{16,24},{17,9... | collective-permute-start | bytes 884744 | tf_op jit(solution)/shard_map/ppermute | solution.py:586
  14.6 3.3 %collective-permute-done.6.refs_1_ = bf16[2,96,768]{2,1,0:T(8,128)(2,1)S(1)} collective-permute-done((bf16[2,96,768]{2,1,0:T(8,128)(2,1)S(1)}, bf16[2,96,768]{2,1,0:T(8,128)(2,1)S(1)}, u32[]{:S(2)}, u32[]{:S(2)}) %collective-permute-start.6) | collective-permute-done | bytes 294944 | tf_op jit(solution)/shard_map/ppermute | solution.py:586
  22.7 2.0 %collective-permute-done.7.refs_2_ = bf16[2,96,768]{2,1,0:T(8,128)(2,1)S(1)} collective-permute-done((bf16[2,96,768]{2,1,0:T(8,128)(2,1)S(1)}, bf16[2,96,768]{2,1,0:T(8,128)(2,1)S(1)}, u32[]{:S(2)}, u32[]{:S(2)}) %collective-permute-start.7) | collective-permute-done | bytes 294944 | tf_op jit(solution)/shard_map/ppermute | solution.py:586
  28.3 5.8 %collective-permute-done.8.pair.refs_3_ = bf16[2,96,768]{2,1,0:T(8,128)(2,1)S(1)} collective-permute-done((bf16[2,96,768]{2,1,0:T(8,128)(2,1)S(1)}, bf16[2,96,768]{2,1,0:T(8,128)(2,1)S(1)}, u32[]{:S(2)}, u32[]{:S(2)}) %collective-permute-start.8) | collective-permute-done | bytes 294944 | tf_op jit(solution)/shard_map/ppermute | solution.py:586
  41.0 7.8 %collective-permute-done.14.refs_7_ = bf16[96,768]{1,0:T(8,128)(2,1)S(1)} collective-permute-done((bf16[96,768]{1,0:T(8,128)(2,1)S(1)}, bf16[96,768]{1,0:T(8,128)(2,1)S(1)}, u32[]{:S(2)}, u32[]{:S(2)}) %collective-permute-start.14) | collective-permute-done | bytes 147488 | tf_op jit(solution)/shard_map/ppermute | solution.py:586
  48.8 3.2 %self_forward.1 = (bf16[768,768]{1,0:T(8,128)(2,1)S(1)}, bf16[256,768]{1,0:T(8,128)(2,1)S(1)}, bf16[128,768]{1,0:T(8,128)(2,1)S(1)}, bf16[128,768]{1,0:T(8,128)(2,1)S(1)}) custom-call(s32[4]{0:T(128)S(1)} %copy-done.13, bf16[256,768]{1,0:T(8,128)(2,1)S(1)} %bitcast.10, f32[3,768]{1,0:T(4,128)S(1)} %copy-done.3, f32[3,768]{1,0:T(4,128)S(1)} %copy-done.4, ...), custom_call_target="tpu_custom_call" | custom-call | flops 1 | bytes 10000000 | tf_op jit(solution)/shard_map/self_forward/pallas_call | solution.py:685
  55.2 2.9 %keyval.3 = (bf16[768,192]{1,0:T(8,128)(2,1)S(1)}, bf16[768,192]{1,0:T(8,128)(2,1)S(1)}, bf16[768,192]{1,0:T(8,128)(2,1)S(1)}, bf16[768,192]{1,0:T(8,128)(2,1)S(...) custom-call(bf16[2304,768]{1,0:T(8,128)(2,1)S(1)} %bitcast.8, ...), custom_call_target="tpu_custom_call" | custom-call | flops 1 | bytes 10000000 | tf_op jit(solution)/shard_map/keyval/pallas_call | solution.py:709
  58.1 2.5 %collective-permute-done.20.other = bf16[128,768]{1,0:T(8,128)(2,1)S(1)} collective-permute-done((bf16[128,768]{1,0:T(8,128)(2,1)S(1)}, bf16[128,768]{1,0:T(8,128)(2,1)S(1)}, u32[]{:S(2)}, u32[]{:S(2)}) %collective-permute-start.20) | collective-permute-done | bytes 196640 | tf_op jit(solution)/shard_map/ppermute | solution.py:536
  63.9 3.0 %cross_forward.1 = (bf16[256,768]{1,0:T(8,128)(2,1)S(1)}, bf16[256,192]{1,0:T(8,128)(2,1)S(1)}, f32[4,192,576]{2,1,0:T(8,128)S(1)}, bf16[256,192]{1,0:T(8,128)(2...) custom-call(s32[4]{0:T(128)S(1)} %copy-done.14, bf16[128,768]{1,0:T(8,128)(2,1)S(1)} %get-tuple-element.145.own, ...), custom_call_target="tpu_custom_call" | custom-call | flops 1 | bytes 5505025 | tf_op jit(solution)/shard_map/cross_forward/pallas_call | solution.py:69
  67.7 3.1 %collective-permute-done.25.pair.refs_3_ = bf16[2,96,1536]{2,1,0:T(8,128)(2,1)S(1)} collective-permute-done((bf16[2,96,1536]{2,1,0:T(8,128)(2,1)S(1)}, bf16[2,96,1536]{2,1,0:T(8,128)(2,1)S(1)}, u32[]{:S(2)}, u32[]{:S(2)}) %collective-permute-start.25) | collective-permute-done | bytes 589856 | tf_op jit(solution)/shard_map/ppermute | solution.py:586
  74.2 4.0 %collective-permute-done.23.other = bf16[128,768]{1,0:T(8,128)(2,1)S(1)} collective-permute-done((bf16[128,768]{1,0:T(8,128)(2,1)S(1)}, bf16[128,768]{1,0:T(8,128)(2,1)S(1)}, u32[]{:S(2)}, u32[]{:S(2)}) %collective-permute-start.23) | collective-permute-done | bytes 196640 | tf_op jit(solution)/shard_map/ppermute | solution.py:536
  92.1 2.9 %cross_back.1 = (bf16[256,768]{1,0:T(8,128)(2,1)S(1)}, bf16[256,192]{1,0:T(8,128)(2,1)S(1)}, bf16[192,2304]{1,0:T(8,128)(2,1)S(1)}, bf16[192,2304]{1,0:T(8,128)(...) custom-call(bf16[128,768]{1,0:T(8,128)(2,1)S(1)} %get-tuple-element.169.own, ...), custom_call_target="tpu_custom_call" | custom-call | flops 1 | bytes 7274497 | tf_op jit(solution)/shard_map/cross_back/pallas_call | solution.py:69
  95.2 2.0 %image_part.1 = (bf16[192,1152]{1,0:T(8,128)(2,1)S(1)}, bf16[192,1152]{1,0:T(8,128)(2,1)S(1)}, bf16[192,1152]{1,0:T(8,128)(2,1)S(1)}, bf16[192,1152]{1,0:T(8,128...) custom-call(bf16[192,2304]{1,0:T(8,128)(2,1)S(1)} %get-tuple-element.184.dkt, ...), custom_call_target="tpu_custom_call" | custom-call | flops 1 | bytes 5898241 | tf_op jit(solution)/shard_map/image_part/pallas_call | solution.py:69
  102.2 2.2 %cross_weights.1 = (bf16[4,96,768]{2,1,0:T(8,128)(2,1)S(1)}, bf16[4,96,768]{2,1,0:T(8,128)(2,1)S(1)}) custom-call(bf16[2304,768]{1,0:T(8,128)(2,1)S(1)} %bitcast.9, bf16[192,2304]{1,0:T(8,128)(2,1)S(1)} %get-tuple-element.184.dkt, bf16[192,2304]{1,0:T(8,128)(2,1)S(1)} %get-tuple-element.174.dvt, bf16[256,768]{1,0:T(8,128)(2,1)S(1)} %get-tuple-element.185.normed, ...), custom_call_target="tpu_custom_call" | custom-call | flops 1 | bytes 7471105 | tf_op jit(solution)/shard_map/cross_weights/pallas_call | solution.py:69
  107.0 4.3 %self_back.1 = (bf16[4,96,768]{2,1,0:T(8,128)(2,1)S(1)}, bf16[4,96,768]{2,1,0:T(8,128)(2,1)S(1)}, bf16[144,768]{1,0:T(8,128)(2,1)S(1)}, bf16[144,768]{1,0:T(8,128)(2,1)S(1)}) custom-call(s32[4]{0:T(128)S(1)} %copy-done.13, bf16[128,768]{1,0:T(8,128)(2,1)S(1)} %get-tuple-element.193.own, bf16[128,768]{1,0:T(8,128)(2,1)S(1)} %collective-permute-done.37.other, ...), custom_call_target="tpu_custom_call" | custom-call | flops 1 | bytes 4051969 | tf_op jit(solution)/shard_map/self_back/pallas_call | solution.py:69
  115.9 2.5 %collective-permute-start.44 = (bf16[2,96,768]{2,1,0:T(8,128)(2,1)S(1)}, bf16[2,96,768]{2,1,0:T(8,128)(2,1)S(1)}, u32[]{:S(2)}, u32[]{:S(2)}) collective-permute-start(bf16[2,96,768]{2,1,0:T(8,128)(2,1)S(1)} %get-tuple-element.215), channel_id=1, source_target_pairs={{0,16},{4,20},{8,24},{12,28},{16,0},{20,4},{24,8},{28,12},{1,17},{... | collective-permute-start | bytes 884744 | tf_op jit(solution)/shard_map/ppermute | solution.py:536
  118.4 2.0 %collective-permute-done.41.other = bf16[144,768]{1,0:T(8,128)(2,1)S(1)} collective-permute-done((bf16[144,768]{1,0:T(8,128)(2,1)S(1)}, bf16[144,768]{1,0:T(8,128)(2,1)S(1)}, u32[]{:S(2)}, u32[]{:S(2)}) %collective-permute-start.41) | collective-permute-done | bytes 221216 | tf_op jit(solution)/shard_map/ppermute | solution.py:536
  123.3 6.0 %collective-permute-done.43.other = bf16[2,96,768]{2,1,0:T(8,128)(2,1)S(1)} collective-permute-done((bf16[2,96,768]{2,1,0:T(8,128)(2,1)S(1)}, bf16[2,96,768]{2,1,0:T(8,128)(2,1)S(1)}, u32[]{:S(2)}, u32[]{:S(2)}) %collective-permute-start.43) | collective-permute-done | bytes 294944 | tf_op jit(solution)/shard_map/ppermute | solution.py:536
  131.6 2.8 %collective-permute-done.47.vec_other = bf16[16,768]{1,0:T(8,128)(2,1)S(1)} collective-permute-done((bf16[16,768]{1,0:T(8,128)(2,1)S(1)}, bf16[16,768]{1,0:T(8,128)(2,1)S(1)}, u32[]{:S(2)}, u32[]{:S(2)}) %collective-permute-start.47) | collective-permute-done | bytes 24608 | tf_op jit(solution)/shard_map/ppermute | solution.py:536
  134.4 2.6 %collective-permute-start.48 = (bf16[2,96,768]{2,1,0:T(8,128)(2,1)S(1)}, bf16[2,96,768]{2,1,0:T(8,128)(2,1)S(1)}, u32[]{:S(2)}, u32[]{:S(2)}) collective-permute-start(bf16[2,96,768]{2,1,0:T(8,128)(2,1)S(1)} %get-tuple-element.226), channel_id=1, source_target_pairs={{0,16},{4,20},{8,24},{12,28},{16,0},{20,4},{24,8},{28,12},{1,17},{... | collective-permute-start | bytes 884744 | tf_op jit(solution)/shard_map/ppermute | solution.py:536
  139.8 4.0 %collective-permute-done.50.other = bf16[96,768]{1,0:T(8,128)(2,1)S(1)} collective-permute-done((bf16[96,768]{1,0:T(8,128)(2,1)S(1)}, bf16[96,768]{1,0:T(8,128)(2,1)S(1)}, u32[]{:S(2)}, u32[]{:S(2)}) %collective-permute-start.50) | collective-permute-done | bytes 147488 | tf_op jit(solution)/shard_map/ppermute | solution.py:536
  147.1 3.6 %collective-permute-done.48.other = bf16[2,96,768]{2,1,0:T(8,128)(2,1)S(1)} collective-permute-done((bf16[2,96,768]{2,1,0:T(8,128)(2,1)S(1)}, bf16[2,96,768]{2,1,0:T(8,128)(2,1)S(1)}, u32[]{:S(2)}, u32[]{:S(2)}) %collective-permute-start.48) | collective-permute-done | bytes 294944 | tf_op jit(solution)/shard_map/ppermute | solution.py:536
  157.9 2.5 %collective-permute-start.58 = (bf16[96,768]{1,0:T(8,128)(2,1)S(1)}, bf16[96,768]{1,0:T(8,128)(2,1)S(1)}, u32[]{:S(2)}, u32[]{:S(2)}) collective-permute-start(bf16[96,768]{1,0:T(8,128)(2,1)S(1)} %get-tuple-element.245), channel_id=1, source_target_pairs={{0,8},{4,12},{8,0},{12,4},{16,24},{20,28},{24,16},{28,20},{1,9},{5... | collective-permute-start | bytes 442376 | tf_op jit(solution)/shard_map/ppermute | solution.py:536
  162.2 2.8 %collective-permute-done.58.refs_1_ = bf16[96,768]{1,0:T(8,128)(2,1)S(1)} collective-permute-done((bf16[96,768]{1,0:T(8,128)(2,1)S(1)}, bf16[96,768]{1,0:T(8,128)(2,1)S(1)}, u32[]{:S(2)}, u32[]{:S(2)}) %collective-permute-start.58) | collective-permute-done | bytes 147488 | tf_op jit(solution)/shard_map/ppermute | solution.py:536
  (175 shorter events, 85.6 us)
Async XLA Ops:
  21.1 16.2 %collective-permute-start.4 = (bf16[2,96,1536]{2,1,0:T(8,128)(2,1)S(1)}, bf16[2,96,1536]{2,1,0:T(8,128)(2,1)S(1)}, u32[]{:S(2)}, u32[]{:S(2)}) collective-permute-start(bf16[2,96,1536]{2,1,0:T(8,128)(2,1)S(1)} %pairF.1), channel_id=1, source_target_pairs={{0,8},{1,5},{2,10},{3,7},{8,16},{9,1},{10,18},{11,3},{16,24},{17,9... | collective-permute-start | bytes 1769480 | tf_op jit(solution)/shard_map/ppermute | solution.py:586
  26.3 11.1 %collective-permute-start.10 = (bf16[2,96,768]{2,1,0:T(8,128)(2,1)S(1)}, bf16[2,96,768]{2,1,0:T(8,128)(2,1)S(1)}, u32[]{:S(2)}, u32[]{:S(2)}) collective-permute-start(bf16[2,96,768]{2,1,0:T(8,128)(2,1)S(1)} %collective-permute-done.3.refs_2_), channel_id=1, source_target_pairs={{0,8},{1,5},{2,10},{3,7},{8,16},{9,1},{10,18},{11,3},{16,24},{17,9... | collective-permute-start | bytes 884744 | tf_op jit(solution)/shard_map/ppermute | solution.py:586
  27.8 13.1 %collective-permute-start.11 = (bf16[2,96,768]{2,1,0:T(8,128)(2,1)S(1)}, bf16[2,96,768]{2,1,0:T(8,128)(2,1)S(1)}, u32[]{:S(2)}, u32[]{:S(2)}) collective-permute-start(bf16[2,96,768]{2,1,0:T(8,128)(2,1)S(1)} %collective-permute-done.1.refs_1_), channel_id=1, source_target_pairs={{0,1},{1,0},{2,3},{3,2},{4,5},{5,4},{6,7},{7,6},{8,9},{9,8},{10,11... | collective-permute-start | bytes 884744 | tf_op jit(solution)/shard_map/ppermute | solution.py:536
  27.8 13.1 %collective-permute-start.12 = (bf16[2,96,768]{2,1,0:T(8,128)(2,1)S(1)}, bf16[2,96,768]{2,1,0:T(8,128)(2,1)S(1)}, u32[]{:S(2)}, u32[]{:S(2)}) collective-permute-start(bf16[2,96,768]{2,1,0:T(8,128)(2,1)S(1)} %collective-permute-done.3.refs_2_), channel_id=1, source_target_pairs={{0,1},{1,0},{2,3},{3,2},{4,5},{5,4},{6,7},{7,6},{8,9},{9,8},{10,11... | collective-permute-start | bytes 884744 | tf_op jit(solution)/shard_map/ppermute | solution.py:536
  37.3 11.5 %collective-permute-start.13 = (bf16[2,96,768]{2,1,0:T(8,128)(2,1)S(1)}, bf16[2,96,768]{2,1,0:T(8,128)(2,1)S(1)}, u32[]{:S(2)}, u32[]{:S(2)}) collective-permute-start(bf16[2,96,768]{2,1,0:T(8,128)(2,1)S(1)} %collective-permute-done.10.pair.refs_3_), channel_id=1, source_target_pairs={{0,1},{1,0},{2,3},{3,2},{4,5},{5,4},{6,7},{7,6},{8,9},{9,8},{10,11... | collective-permute-start | bytes 884744 | tf_op jit(solution)/shard_map/ppermute | solution.py:536
  37.3 20.7 %collective-permute-start.19 = (bf16[2,96,1536]{2,1,0:T(8,128)(2,1)S(1)}, bf16[2,96,1536]{2,1,0:T(8,128)(2,1)S(1)}, u32[]{:S(2)}, u32[]{:S(2)}) collective-permute-start(bf16[2,96,1536]{2,1,0:T(8,128)(2,1)S(1)} %collective-permute-done.4.refs_1_), channel_id=1, source_target_pairs={{0,8},{1,5},{2,10},{3,7},{8,16},{9,1},{10,18},{11,3},{16,24},{17,9... | collective-permute-start | bytes 1769480 | tf_op jit(solution)/shard_map/ppermute | solution.py:586
  60.8 9.9 %collective-permute-start.25 = (bf16[2,96,1536]{2,1,0:T(8,128)(2,1)S(1)}, bf16[2,96,1536]{2,1,0:T(8,128)(2,1)S(1)}, u32[]{:S(2)}, u32[]{:S(2)}) collective-permute-start(bf16[2,96,1536]{2,1,0:T(8,128)(2,1)S(1)} %collective-permute-done.19.refs_2_), channel_id=1, source_target_pairs={{0,8},{1,5},{2,10},{3,7},{8,16},{9,1},{10,18},{11,3},{16,24},{17,9... | collective-permute-start | bytes 1769480 | tf_op jit(solution)/shard_map/ppermute | solution.py:586
  67.2 11.4 %collective-permute-start.26 = (bf16[2,96,1536]{2,1,0:T(8,128)(2,1)S(1)}, bf16[2,96,1536]{2,1,0:T(8,128)(2,1)S(1)}, u32[]{:S(2)}, u32[]{:S(2)}) collective-permute-start(bf16[2,96,1536]{2,1,0:T(8,128)(2,1)S(1)} %collective-permute-done.4.refs_1_), channel_id=1, source_target_pairs={{0,1},{1,0},{2,3},{3,2},{4,5},{5,4},{6,7},{7,6},{8,9},{9,8},{10,11... | collective-permute-start | bytes 1769480 | tf_op jit(solution)/shard_map/ppermute | solution.py:536
  67.6 11.0 %collective-permute-start.27 = (bf16[2,96,1536]{2,1,0:T(8,128)(2,1)S(1)}, bf16[2,96,1536]{2,1,0:T(8,128)(2,1)S(1)}, u32[]{:S(2)}, u32[]{:S(2)}) collective-permute-start(bf16[2,96,1536]{2,1,0:T(8,128)(2,1)S(1)} %collective-permute-done.19.refs_2_), channel_id=1, source_target_pairs={{0,1},{1,0},{2,3},{3,2},{4,5},{5,4},{6,7},{7,6},{8,9},{9,8},{10,11... | collective-permute-start | bytes 1769480 | tf_op jit(solution)/shard_map/ppermute | solution.py:536
  85.6 15.2 %collective-permute-start.34 = (bf16[4,96,768]{2,1,0:T(8,128)(2,1)S(1)}, bf16[4,96,768]{2,1,0:T(8,128)(2,1)S(1)}, u32[]{:S(2)}, u32[]{:S(2)}) collective-permute-start(bf16[4,96,768]{2,1,0:T(8,128)(2,1)S(1)} %get-tuple-element.164), channel_id=1, source_target_pairs={{0,8},{4,12},{8,0},{12,4},{16,24},{20,28},{24,16},{28,20},{1,9},{5... | collective-permute-start | bytes 1769480 | tf_op jit(solution)/shard_map/ppermute | solution.py:536
  87.3 14.8 %collective-permute-start.35 = (bf16[4,96,768]{2,1,0:T(8,128)(2,1)S(1)}, bf16[4,96,768]{2,1,0:T(8,128)(2,1)S(1)}, u32[]{:S(2)}, u32[]{:S(2)}) collective-permute-start(bf16[4,96,768]{2,1,0:T(8,128)(2,1)S(1)} %get-tuple-element.166), channel_id=1, source_target_pairs={{0,4},{4,0},{8,12},{12,8},{16,20},{20,16},{24,28},{28,24},{1,5},{5... | collective-permute-start | bytes 1769480 | tf_op jit(solution)/shard_map/ppermute | solution.py:536
  105.5 16.2 %collective-permute-start.42 = (bf16[4,96,768]{2,1,0:T(8,128)(2,1)S(1)}, bf16[4,96,768]{2,1,0:T(8,128)(2,1)S(1)}, u32[]{:S(2)}, u32[]{:S(2)}) collective-permute-start(bf16[4,96,768]{2,1,0:T(8,128)(2,1)S(1)} %get-tuple-element.190), channel_id=1, source_target_pairs={{0,4},{4,0},{8,12},{12,8},{16,20},{20,16},{24,28},{28,24},{1,5},{5... | collective-permute-start | bytes 1769480 | tf_op jit(solution)/shard_map/ppermute | solution.py:536
  111.4 25.7 %collective-permute-start.46 = (bf16[4,96,768]{2,1,0:T(8,128)(2,1)S(1)}, bf16[4,96,768]{2,1,0:T(8,128)(2,1)S(1)}, u32[]{:S(2)}, u32[]{:S(2)}) collective-permute-start(bf16[4,96,768]{2,1,0:T(8,128)(2,1)S(1)} %get-tuple-element.222), channel_id=1, source_target_pairs={{0,4},{4,0},{8,12},{12,8},{16,20},{20,16},{24,28},{28,24},{1,5},{5... | collective-permute-start | bytes 1769480 | tf_op jit(solution)/shard_map/ppermute | solution.py:536
  114.3 15.0 %collective-permute-start.43 = (bf16[2,96,768]{2,1,0:T(8,128)(2,1)S(1)}, bf16[2,96,768]{2,1,0:T(8,128)(2,1)S(1)}, u32[]{:S(2)}, u32[]{:S(2)}) collective-permute-start(bf16[2,96,768]{2,1,0:T(8,128)(2,1)S(1)} %get-tuple-element.212), channel_id=1, source_target_pairs={{0,8},{4,12},{8,0},{12,4},{16,24},{20,28},{24,16},{28,20},{1,9},{5... | collective-permute-start | bytes 884744 | tf_op jit(solution)/shard_map/ppermute | solution.py:536
  115.9 15.8 %collective-permute-start.44 = (bf16[2,96,768]{2,1,0:T(8,128)(2,1)S(1)}, bf16[2,96,768]{2,1,0:T(8,128)(2,1)S(1)}, u32[]{:S(2)}, u32[]{:S(2)}) collective-permute-start(bf16[2,96,768]{2,1,0:T(8,128)(2,1)S(1)} %get-tuple-element.215), channel_id=1, source_target_pairs={{0,16},{4,20},{8,24},{12,28},{16,0},{20,4},{24,8},{28,12},{1,17},{... | collective-permute-start | bytes 884744 | tf_op jit(solution)/shard_map/ppermute | solution.py:536
  120.4 9.5 %collective-permute-start.45 = (bf16[128,768]{1,0:T(8,128)(2,1)S(1)}, bf16[128,768]{1,0:T(8,128)(2,1)S(1)}, u32[]{:S(2)}, u32[]{:S(2)}) collective-permute-start(bf16[128,768]{1,0:T(8,128)(2,1)S(1)} %get-tuple-element.220), channel_id=1, source_target_pairs={{0,1},{1,0},{2,3},{3,2},{4,5},{5,4},{6,7},{7,6},{8,9},{9,8},{10,11... | collective-permute-start | bytes 589832 | tf_op jit(solution)/shard_map/ppermute | solution.py:536
  121.7 38.7 %collective-permute-start.57 = (bf16[192,2304]{1,0:T(8,128)(2,1)S(1)}, bf16[192,2304]{1,0:T(8,128)(2,1)S(1)}, u32[]{:S(2)}, u32[]{:S(2)}) collective-permute-start(bf16[192,2304]{1,0:T(8,128)(2,1)S(1)} %image_chip.1), channel_id=1, source_target_pairs={{0,2},{1,3},{2,0},{3,1},{4,6},{5,7},{6,4},{7,5},{8,10},{9,11},{10,... | collective-permute-start | bytes 2654216 | tf_op jit(solution)/shard_map/ppermute | solution.py:536
  131.6 20.7 %collective-permute-start.51 = (f32[128,768]{1,0:T(8,128)S(1)}, f32[128,768]{1,0:T(8,128)S(1)}, u32[]{:S(2)}, u32[]{:S(2)}) collective-permute-start(f32[128,768]{1,0:T(8,128)S(1)} %get-tuple-element.232.own), channel_id=1, source_target_pairs={{0,1},{1,0},{2,3},{3,2},{4,5},{5,4},{6,7},{7,6},{8,9},{9,8},{10,11... | collective-permute-start | bytes 1179656 | tf_op jit(solution)/shard_map/ppermute | solution.py:536
  134.4 16.3 %collective-permute-start.48 = (bf16[2,96,768]{2,1,0:T(8,128)(2,1)S(1)}, bf16[2,96,768]{2,1,0:T(8,128)(2,1)S(1)}, u32[]{:S(2)}, u32[]{:S(2)}) collective-permute-start(bf16[2,96,768]{2,1,0:T(8,128)(2,1)S(1)} %get-tuple-element.226), channel_id=1, source_target_pairs={{0,16},{4,20},{8,24},{12,28},{16,0},{20,4},{24,8},{28,12},{1,17},{... | collective-permute-start | bytes 884744 | tf_op jit(solution)/shard_map/ppermute | solution.py:536
  137.2 9.9 %collective-permute-start.52 = (bf16[128,768]{1,0:T(8,128)(2,1)S(1)}, bf16[128,768]{1,0:T(8,128)(2,1)S(1)}, u32[]{:S(2)}, u32[]{:S(2)}) collective-permute-start(bf16[128,768]{1,0:T(8,128)(2,1)S(1)} %add_pair.11.chip), channel_id=1, source_target_pairs={{0,2},{1,3},{2,0},{3,1},{4,6},{5,7},{6,4},{7,5},{8,10},{9,11},{10,... | collective-permute-start | bytes 589832 | tf_op jit(solution)/shard_map/ppermute | solution.py:536
  143.8 12.7 %collective-permute-start.54 = (bf16[208,768]{1,0:T(8,128)(2,1)S(1)}, bf16[208,768]{1,0:T(8,128)(2,1)S(1)}, u32[]{:S(2)}, u32[]{:S(2)}) collective-permute-start(bf16[208,768]{1,0:T(8,128)(2,1)S(1)} %get-tuple-element.237), channel_id=1, source_target_pairs={{0,8},{4,12},{8,0},{12,4},{16,24},{20,28},{24,16},{28,20},{1,9},{5... | collective-permute-start | bytes 958472 | tf_op jit(solution)/shard_map/ppermute | solution.py:536
  147.1 13.4 %collective-permute-start.55 = (bf16[192,1152]{1,0:T(8,128)(2,1)S(1)}, bf16[192,1152]{1,0:T(8,128)(2,1)S(1)}, u32[]{:S(2)}, u32[]{:S(2)}) collective-permute-start(bf16[192,1152]{1,0:T(8,128)(2,1)S(1)} %get-tuple-element.241), channel_id=1, source_target_pairs={{0,1},{1,0},{2,3},{3,2},{4,5},{5,4},{6,7},{7,6},{8,9},{9,8},{10,11... | collective-permute-start | bytes 1327112 | tf_op jit(solution)/shard_map/ppermute | solution.py:536
  150.7 9.7 %collective-permute-start.56 = (bf16[192,1152]{1,0:T(8,128)(2,1)S(1)}, bf16[192,1152]{1,0:T(8,128)(2,1)S(1)}, u32[]{:S(2)}, u32[]{:S(2)}) collective-permute-start(bf16[192,1152]{1,0:T(8,128)(2,1)S(1)} %get-tuple-element.242), channel_id=1, source_target_pairs={{0,1},{1,0},{2,3},{3,2},{4,5},{5,4},{6,7},{7,6},{8,9},{9,8},{10,11... | collective-permute-start | bytes 1327112 | tf_op jit(solution)/shard_map/ppermute | solution.py:536
  156.6 9.9 %collective-permute-start.59 = (bf16[112,768]{1,0:T(8,128)(2,1)S(1)}, bf16[112,768]{1,0:T(8,128)(2,1)S(1)}, u32[]{:S(2)}, u32[]{:S(2)}) collective-permute-start(bf16[112,768]{1,0:T(8,128)(2,1)S(1)} %get-tuple-element.248), channel_id=1, source_target_pairs={{0,16},{4,20},{8,24},{12,28},{16,0},{20,4},{24,8},{28,12},{1,17},{... | collective-permute-start | bytes 516104 | tf_op jit(solution)/shard_map/ppermute | solution.py:536
  (52 other events, 415.4 us)
